TPU v7x, 32 devices: a whole 2x2x4 slice. The times are simulated.
32 devices in a mesh: seq: 8 (over z, y), wt: 4 (over x, core).
Axes of the slice: x: 2, y: 2, z: 4, core: 2. Of those that a mesh axis runs over, the one named last changes fastest.
Arguments:
- inputs: bfloat16 [8, 512, 2560], P('wt', 'seq'), may hold values from -6 to 6
- positions: int32 [8, 512], P('wt', 'seq'), may hold values from 0 to 479, as said below
- cotangent: bfloat16 [8, 512, 2560], P('wt', 'seq'), may hold values from -6 to 6
- gain: float32 [2560], replicated, may hold values from 0.1 to 1.9
- w_x: bfloat16 [2560, 2560], P('wt'), may hold values from -0.125 to 0.125
- w_y: bfloat16 [2560, 2560], P('wt'), may hold values from -0.125 to 0.125
- conv_w: float32 [4, 2560], replicated, may hold values from -3 to 3
- conv_b: float32 [2560], replicated, may hold values from -3 to 3
- gate_a: bfloat16 [2560, 256], P('wt'), may hold values from -0.375 to 0.375
- bias_a: float32 [2560], replicated, may hold values from -4 to 4
- gate_i: bfloat16 [2560, 256], P('wt'), may hold values from -0.375 to 0.375
- bias_i: float32 [2560], replicated, may hold values from -3 to 3
- decay_log: float32 [2560], replicated
- w_out: bfloat16 [2560, 2560], P('wt'), may hold values from -0.125 to 0.125
- gain2: float32 [2560], replicated, may hold values from 0.1 to 1.9
- w_gate: bfloat16 [2560, 7680], P(None, 'wt'), may hold values from -0.125 to 0.125
- w_up: bfloat16 [2560, 7680], P(None, 'wt'), may hold values from -0.125 to 0.125
- w_down: bfloat16 [7680, 2560], P('wt'), may hold values from -0.0625 to 0.0625
Outputs:
- result: bfloat16 [8, 512, 2560], P('wt', 'seq')
- input_grad: float32 [8, 512, 2560], P('wt', 'seq')
- grad_gain: float32 [2560], P(('seq', 'wt'))
- grad_w_x: float32 [2560, 2560], P(('seq', 'wt'))
- grad_w_y: float32 [2560, 2560], P(('seq', 'wt'))
- grad_conv_w: float32 [4, 2560], P(None, ('seq', 'wt'))
- grad_conv_b: float32 [2560], P(('seq', 'wt'))
- grad_gate_a: float32 [2560, 256], P(('seq', 'wt'))
- grad_bias_a: float32 [2560], P(('seq', 'wt'))
- grad_gate_i: float32 [2560, 256], P(('seq', 'wt'))
- grad_bias_i: float32 [2560], P(('seq', 'wt'))
- grad_decay: float32 [2560], P(('seq', 'wt'))
- grad_w_out: float32 [2560, 2560], P(('seq', 'wt'))
- grad_gain2: float32 [2560], P(('seq', 'wt'))
- grad_w_gate: float32 [2560, 7680], P('seq', 'wt')
- grad_w_up: float32 [2560, 7680], P('seq', 'wt')
- grad_w_down: float32 [7680, 2560], P('wt', 'seq')
Inputs may be any that keep to these rules, and one draw needn't show every extreme that they name: `positions`: 0 at a document's first token and one more than the token before otherwise; every sequence starts a document at its first token; in every sequence one document of exactly 480 tokens starts within its first 64 tokens and runs into its last 64 tokens.
All inputs are finite; a program needn't handle non-finite values.
Results may differ from a plain program's by a relative error of at most 0.018.
Values may be sent and summed in bfloat16 or wider, within the bound.
No kernel may reach another device: no remote copies, remote signals or barrier semaphores. Data moves between devices by JAX's collectives and lax.ppermute only.
A program may use at most 640 MiB of HBM per device.

v0:
```python
from functools import partial

import jax
import jax.numpy as jnp
from jax import lax
from jax.sharding import PartitionSpec as P


def from_behind(value, axis, steps):
    count = lax.axis_size(axis)
    initial, last = (max(0, -steps), min(count, count - steps))
    return lax.ppermute(value, axis, [(source, source + steps) for source in range(initial, last)])


def combine(earlier, latter):
    return (latter[0] * earlier[0], latter[1] + latter[0] * earlier[1])


def head_product(values, weight, head_count, head_width):
    shaped = values.reshape(values.shape[0], values.shape[1], head_count, head_width)
    blocks = weight.reshape(head_count, head_width, head_width)
    product = jnp.einsum("bthi,hij->bthj", shaped, blocks, preferred_element_type=jnp.float32)
    return product.reshape(values.shape)


def head_back(grads, weight, head_count, head_width):
    shaped = grads.reshape(grads.shape[0], grads.shape[1], head_count, head_width)
    blocks = weight.reshape(head_count, head_width, head_width)
    product = jnp.einsum("bthj,hij->bthi", shaped, blocks, preferred_element_type=jnp.float32)
    return product.reshape(grads.shape)


def head_weight_grad(values, grads, head_count, head_width):
    left = values.reshape(values.shape[0], values.shape[1], head_count, head_width)
    right = grads.reshape(grads.shape[0], grads.shape[1], head_count, head_width)
    product = jnp.einsum("bthi,bthj->hij", left, right, preferred_element_type=jnp.float32)
    return product.reshape(head_count * head_width, head_width)


def carry_forward(summary):

    def advance(counter, incoming):
        outgoing = summary[1] + summary[0] * incoming
        return from_behind(outgoing, "seq", 1)

    return lax.fori_loop(0, lax.axis_size("seq") - 1, advance, jnp.zeros_like(summary[1]))


def carry_backward(summary):

    def advance(counter, incoming):
        outgoing = summary[1] + summary[0] * incoming
        return from_behind(outgoing, "seq", -1)

    return lax.fori_loop(0, lax.axis_size("seq") - 1, advance, jnp.zeros_like(summary[1]))


def local(
    inputs,
    positions,
    cotangent,
    gain,
    w_x,
    w_y,
    conv_w,
    conv_b,
    gate_a,
    bias_a,
    gate_i,
    bias_i,
    decay_log,
    w_out,
    gain2,
    w_gate,
    w_up,
    w_down,
):
    batches, length, features = inputs.shape
    head_width = gate_a.shape[1]
    head_count = features // head_width
    kernel_taps = conv_w.shape[0]
    unit_share = w_gate.shape[1]
    full_x, full_y, full_out, full_a, full_i = (
        lax.all_gather(w_x, "wt", axis=0, tiled=True),
        lax.all_gather(w_y, "wt", axis=0, tiled=True),
        lax.all_gather(w_out, "wt", axis=0, tiled=True),
        lax.all_gather(gate_a, "wt", axis=0, tiled=True),
        lax.all_gather(gate_i, "wt", axis=0, tiled=True),
    )
    source = inputs.astype(jnp.float32)
    norm_scale = lax.rsqrt(jnp.mean(source * source, axis=-1, keepdims=True) + 1e-06)
    normed = (source * norm_scale * gain).astype(jnp.bfloat16)
    branch_x = jnp.einsum("btd,de->bte", normed, full_x, preferred_element_type=jnp.float32).astype(
        jnp.bfloat16
    )
    branch_pre = jnp.einsum("btd,de->bte", normed, full_y, preferred_element_type=jnp.float32)
    branch_y, gelu_pull = jax.vjp(partial(jax.nn.gelu, approximate=True), branch_pre)
    earlier_rows = from_behind(branch_x[:, length - (kernel_taps - 1) :], "seq", 1)
    extended = jnp.concatenate([earlier_rows, branch_x], axis=1).astype(jnp.float32)
    tap_masks = [
        (positions >= offset).astype(jnp.float32)[..., None] for offset in range(kernel_taps)
    ]
    total = conv_b + jnp.zeros((batches, length, features), jnp.float32)
    for offset in range(kernel_taps):
        shifted = extended[:, kernel_taps - 1 - offset : kernel_taps - 1 - offset + length]
        total = total + conv_w[offset] * shifted * tap_masks[offset]
    conv_out = total.astype(jnp.bfloat16)
    conv_full = conv_out.astype(jnp.float32)
    logit_a = head_product(conv_out, full_a, head_count, head_width)
    logit_i = head_product(conv_out, full_i, head_count, head_width)
    gate_rec = jax.nn.sigmoid(logit_a + bias_a)
    gate_in = jax.nn.sigmoid(logit_i + bias_i)
    decay_rate = jnp.exp(decay_log)
    log_a = -8.0 * gate_rec * decay_rate
    alive_mask = (positions > 0).astype(jnp.float32)[..., None]
    root_term = jnp.sqrt(-jnp.expm1(2.0 * log_a))
    multiplier = alive_mask * root_term + (1.0 - alive_mask)
    decay_raw = jnp.exp(log_a)
    decay = decay_raw * alive_mask
    driven = conv_full * gate_in * multiplier
    running, local_state = lax.associative_scan(combine, (decay, driven), axis=1)
    carry_in = carry_forward((running[:, -1], local_state[:, -1]))
    state_all = local_state + running * carry_in[:, None]
    mixed_rows = (state_all * branch_y).astype(jnp.bfloat16)
    stream = source + jnp.einsum(
        "btd,de->bte", mixed_rows, full_out, preferred_element_type=jnp.float32
    )
    second_scale = lax.rsqrt(jnp.mean(stream * stream, axis=-1, keepdims=True) + 1e-06)
    normed_two = (stream * second_scale * gain2).astype(jnp.bfloat16)
    every_normed, every_cot = (
        lax.all_gather(normed_two, "wt", axis=0, tiled=True),
        lax.all_gather(cotangent, "wt", axis=0, tiled=True),
    )
    gate_pre = jnp.einsum("btd,df->btf", every_normed, w_gate, preferred_element_type=jnp.float32)
    up_pre = jnp.einsum("btd,df->btf", every_normed, w_up, preferred_element_type=jnp.float32)
    gate_act, gate_pull = jax.vjp(partial(jax.nn.gelu, approximate=True), gate_pre)
    hidden = (gate_act * up_pre).astype(jnp.bfloat16)
    part = lax.slice_in_dim(hidden, 0, batches * lax.axis_size("wt"), axis=0)
    ffn_out = lax.psum_scatter(
        jnp.einsum("btf,fd->btd", part, w_down, preferred_element_type=jnp.float32).astype(
            jnp.bfloat16
        ),
        "wt",
        scatter_dimension=0,
        tiled=True,
    ).astype(jnp.float32)
    output = (stream + ffn_out).astype(jnp.bfloat16)
    grad_hidden = jnp.einsum("btd,fd->btf", every_cot, w_down, preferred_element_type=jnp.float32)
    grad_gate_pre = gate_pull(grad_hidden * up_pre)[0].astype(jnp.bfloat16)
    grad_up_pre = (grad_hidden * gate_act).astype(jnp.bfloat16)
    row_count = batches * lax.axis_size("wt")
    part_gate = lax.slice_in_dim(grad_gate_pre, 0, row_count, axis=0)
    part_up = lax.slice_in_dim(grad_up_pre, 0, row_count, axis=0)
    first = jnp.einsum("btf,df->btd", part_gate, w_gate, preferred_element_type=jnp.float32)
    grad_normed_two = lax.psum_scatter(
        first + jnp.einsum("btf,df->btd", part_up, w_up, preferred_element_type=jnp.float32),
        "wt",
        scatter_dimension=0,
        tiled=True,
    )
    weighted_two = grad_normed_two * gain2
    grad_stream = (
        cotangent.astype(jnp.float32)
        + weighted_two * second_scale
        - stream * second_scale**3 * jnp.mean(weighted_two * stream, axis=-1, keepdims=True)
    )
    grad_proj = grad_stream.astype(jnp.bfloat16)
    flat_every = every_normed.reshape(-1, features)
    flat_every_cot = every_cot.reshape(-1, features)
    flat_gate_grad = grad_gate_pre.reshape(-1, unit_share)
    flat_up_grad = grad_up_pre.reshape(-1, unit_share)
    flat_hidden = hidden.reshape(-1, unit_share)
    ffn_whole = jnp.concatenate(
        [
            jnp.einsum("rd,rf->df", flat_every, flat_gate_grad, preferred_element_type=jnp.float32),
            jnp.einsum("rd,rf->df", flat_every, flat_up_grad, preferred_element_type=jnp.float32),
            jnp.einsum(
                "rd,rf->df", flat_every_cot, flat_hidden, preferred_element_type=jnp.float32
            ),
        ],
        axis=1,
    )
    ffn_reduced = lax.psum_scatter(
        ffn_whole.astype(jnp.bfloat16), "seq", scatter_dimension=0, tiled=True
    ).astype(jnp.float32)
    grad_mixed = jnp.einsum("bte,de->btd", grad_proj, full_out, preferred_element_type=jnp.float32)
    grad_direct = grad_mixed * branch_y
    grad_pre = gelu_pull(grad_mixed * state_all)[0].astype(jnp.bfloat16)
    following = jnp.concatenate([decay[:, 1:], jnp.ones_like(decay[:, :1])], axis=1)
    behind, local_grad = lax.associative_scan(
        combine, (following, grad_direct), axis=1, reverse=True
    )
    carry_back = carry_backward((running[:, -1], decay[:, 0] * local_grad[:, 0]))
    grad_state = local_grad + behind * carry_back[:, None]
    state_before = jnp.concatenate([carry_in[:, None], state_all[:, :-1]], axis=1)
    grad_mult = grad_state * conv_full * gate_in * alive_mask
    grad_log = (
        grad_state * state_before * alive_mask * decay_raw
        - grad_mult * decay_raw * decay_raw / root_term
    )
    grad_logit_a = grad_log * (-8.0 * decay_rate) * gate_rec * (1.0 - gate_rec)
    grad_logit_i = grad_state * conv_full * multiplier * gate_in * (1.0 - gate_in)
    low_logit_a = grad_logit_a.astype(jnp.bfloat16)
    low_logit_i = grad_logit_i.astype(jnp.bfloat16)
    grad_conv = grad_state * gate_in * multiplier
    grad_conv = grad_conv + head_back(low_logit_a, full_a, head_count, head_width)
    grad_conv = grad_conv + head_back(low_logit_i, full_i, head_count, head_width)
    grad_conv_full = grad_conv.astype(jnp.bfloat16).astype(jnp.float32)
    spread = jnp.zeros((batches, length + kernel_taps - 1, features), jnp.float32)
    conv_w_grads = []
    for offset in range(kernel_taps):
        masked = grad_conv_full * tap_masks[offset]
        spread = spread + jnp.pad(
            conv_w[offset] * masked, ((0, 0), (kernel_taps - 1 - offset, offset), (0, 0))
        )
        shifted = extended[:, kernel_taps - 1 - offset : kernel_taps - 1 - offset + length]
        conv_w_grads.append(jnp.sum(masked * shifted, axis=(0, 1)))
    later_rows = from_behind(spread[:, : kernel_taps - 1].astype(jnp.bfloat16), "seq", -1).astype(
        jnp.float32
    )
    grad_branch_x = spread[:, kernel_taps - 1 :] + jnp.pad(
        later_rows, ((0, 0), (length - (kernel_taps - 1), 0), (0, 0))
    )
    grad_branch_x = grad_branch_x.astype(jnp.bfloat16)
    grad_normed = jnp.einsum(
        "bte,de->btd", grad_branch_x, full_x, preferred_element_type=jnp.float32
    )
    grad_normed = grad_normed + jnp.einsum(
        "bte,de->btd", grad_pre, full_y, preferred_element_type=jnp.float32
    )
    weighted = grad_normed * gain
    input_grad = (
        grad_stream
        + weighted * norm_scale
        - source * norm_scale**3 * jnp.mean(weighted * source, axis=-1, keepdims=True)
    )
    small_rows = jnp.stack(
        [jnp.sum(grad_normed * source * norm_scale, axis=(0, 1))]
        + conv_w_grads
        + [
            jnp.sum(grad_conv_full, axis=(0, 1)),
            jnp.sum(grad_logit_a, axis=(0, 1)),
            jnp.sum(grad_logit_i, axis=(0, 1)),
            jnp.sum(grad_log * log_a, axis=(0, 1)),
            jnp.sum(grad_normed_two * stream * second_scale, axis=(0, 1)),
        ],
        axis=0,
    )
    small_cols = jnp.pad(small_rows.T, ((0, 0), (0, 128 - small_rows.shape[0])))
    flat_normed = normed.reshape(-1, features)
    flat_mixed = mixed_rows.reshape(-1, features)
    flat_gradx = grad_branch_x.reshape(-1, features)
    flat_pre = grad_pre.reshape(-1, features)
    flat_proj = grad_proj.reshape(-1, features)
    grad_whole = jnp.concatenate(
        [
            jnp.einsum("rd,re->de", flat_normed, flat_gradx, preferred_element_type=jnp.float32),
            jnp.einsum("rd,re->de", flat_normed, flat_pre, preferred_element_type=jnp.float32),
            jnp.einsum("rd,re->de", flat_mixed, flat_proj, preferred_element_type=jnp.float32),
            head_weight_grad(conv_out, low_logit_a, head_count, head_width),
            head_weight_grad(conv_out, low_logit_i, head_count, head_width),
            small_cols,
        ],
        axis=1,
    )
    reduced = lax.psum_scatter(grad_whole, ("seq", "wt"), scatter_dimension=0, tiled=True)
    grad_x_out = reduced[:, :features]
    grad_y_out = reduced[:, features : 2 * features]
    grad_out_out = reduced[:, 2 * features : 3 * features]
    base = 3 * features
    grad_a_out = reduced[:, base : base + head_width]
    grad_i_out = reduced[:, base + head_width : base + 2 * head_width]
    small_out = reduced[:, base + 2 * head_width :]
    grad_gate_out = ffn_reduced[:, :unit_share]
    grad_up_out = ffn_reduced[:, unit_share : 2 * unit_share]
    grad_down_out = ffn_reduced[:, 2 * unit_share :].T
    return (
        output,
        input_grad,
        small_out[:, 0],
        grad_x_out,
        grad_y_out,
        small_out[:, 1 : 1 + kernel_taps].T,
        small_out[:, 1 + kernel_taps],
        grad_a_out,
        small_out[:, 2 + kernel_taps],
        grad_i_out,
        small_out[:, 3 + kernel_taps],
        small_out[:, 4 + kernel_taps],
        grad_out_out,
        small_out[:, 5 + kernel_taps],
        grad_gate_out,
        grad_up_out,
        grad_down_out,
    )


def solution(mesh):
    placed = (
        P("wt", "seq", None),
        P("wt", "seq"),
        P("wt", "seq", None),
        P(),
        P("wt", None),
        P("wt", None),
        P(),
        P(),
        P("wt", None),
        P(),
        P("wt", None),
        P(),
        P(),
        P("wt", None),
        P(),
        P(None, "wt"),
        P(None, "wt"),
        P("wt", None),
    )
    return jax.shard_map(
        local,
        mesh=mesh,
        in_specs=placed,
        out_specs=(
            P("wt", "seq", None),
            P("wt", "seq", None),
            P(("seq", "wt")),
            P(("seq", "wt"), None),
            P(("seq", "wt"), None),
            P(None, ("seq", "wt")),
            P(("seq", "wt")),
            P(("seq", "wt"), None),
            P(("seq", "wt")),
            P(("seq", "wt"), None),
            P(("seq", "wt")),
            P(("seq", "wt")),
            P(("seq", "wt"), None),
            P(("seq", "wt")),
            P("seq", "wt"),
            P("seq", "wt"),
            P("wt", "seq"),
        ),
        check_vma=False,
    )
```

profile of v0, /device:TPU:0, one launch (start us, length us, event | category | flops | bytes accessed | tf_op | source)
XLA Modules:
  0.0 2528.2 jit_solution(11130849427628568541)
XLA Ops:
  13.2 84.2 %all-gather.8.cloned.1.call-done = bf16[2560,2560]{1,0:T(8,128)(2,1)} async-done(((bf16[640,2560]{1,0:T(8,128)(2,1)}), bf16[2560,2560]{1,0:T(8,128)(2,1)}) %all-gather.8.cloned.1.call-update) | async-done | bytes 13107216 | tf_op jit(solution)/shard_map/all_gather | solution.py:84
  97.4 6.6 fusion.44
  110.4 6.7 all-gather.12.cloned.1.call-done
  119.0 18.0 all-gather.10.cloned.1.call-done
  144.7 3.4 slice.485
  151.5 3.6 slice.481
  218.6 3.4 slice.482
  302.0 42.8 %while.20 = (s32[]{:T(128)}, f32[2,2560]{1,0:T(2,128)S(1)}, f32[2,2560]{1,0:T(2,128)S(1)}, f32[2,2560]{1,0:T(2,128)S(1)}, s32[]{:T(128)}) while((s32[]{:T(128)}, f32[2,2560]{1,0:T(2,128)S(1)}, f32[2,2560]{1,0:T(2,128)S(1)}, f32[2,2560]{1,0:T(2,128)S(1)}, s32[]{:T(128)}) %tuple.145), condition=%wide.region_2.0_spmd, body=%wide.region_1.0_spmd.sunk | while | flops 10242 | bytes 163941 | solution.py:46
  307.0 4.2 collective-permute-start
  312.7 4.3 collective-permute-start
  318.5 5.1 collective-permute-start
  325.0 5.1 collective-permute-start
  331.6 5.1 collective-permute-start
  338.2 5.1 collective-permute-start
  344.8 10.3 multiply_convert_fusion.3
  355.1 6.9 multiply_reduce_fusion.3
  364.3 11.7 fusion.12
  376.0 16.5 all-gather.18.cloned.1.call-done
  392.4 11.4 fusion.18
  403.8 14.9 fusion.37
  418.7 9.2 fusion.16
  428.0 9.1 fusion.25
  437.2 9.9 fusion.28
  450.4 3.5 slice.550
  456.1 3.4 slice.540
  459.5 9.9 slice.551
  469.4 9.9 slice.541
  479.3 6.2 slice.545
  491.3 34.7 %reduce-scatter.7.cloned.1.call-done = bf16[2,64,2560]{2,1,0:T(8,128)(2,1)} async-done(((bf16[8,64,2560]{2,1,0:T(8,128)(2,1)}), bf16[2,64,2560]{2,1,0:T(8,128)(2,1)}) %reduce-scatter.7.cloned.1.call-update) | async-done | bytes 655376 | tf_op jit(solution)/shard_map/reduce_scatter | solution.py:139
  529.4 10.8 fusion.92
  550.8 9.9 slice.547
  560.7 6.3 slice.543
  609.5 6.3 slice.538
  660.8 10.7 rev.8
  679.9 10.8 rev.9
  690.7 44.8 %while.21 = (s32[]{:T(128)}, f32[2,2560]{1,0:T(2,128)S(1)}, f32[2,2560]{1,0:T(2,128)S(1)}, f32[2,2560]{1,0:T(2,128)S(1)}, s32[]{:T(128)}) while((s32[]{:T(128)}, f32[2,2560]{1,0:T(2,128)S(1)}, f32[2,2560]{1,0:T(2,128)S(1)}, f32[2,2560]{1,0:T(2,128)S(1)}, s32[]{:T(128)}) %tuple.144), condition=%wide.region_8.0_spmd, body=%wide.region_7.0_spmd.sunk | while | flops 10242 | bytes 163941 | solution.py:55
  692.1 4.4 collective-permute-done.1
  697.8 4.8 collective-permute-done.1
  703.9 5.3 collective-permute-done.1
  710.5 5.3 collective-permute-done.1
  717.1 5.5 collective-permute-done.1
  723.8 5.1 collective-permute-done.1
  730.3 5.3 collective-permute-done.1
  735.7 4.8 fusion.127
  740.5 4.0 multiply_reduce_fusion.1
  750.6 3.5 fusion.55
  757.3 6.5 fusion.4
  766.1 3.6 copy.91
  773.1 10.5 fusion.76
  783.7 10.6 bitcast_dynamic-update-slice_fusion.2
  794.2 10.6 bitcast_dynamic-update-slice_fusion.1
  804.8 10.6 bitcast_dynamic-update-slice_fusion
  821.2 10.2 bitcast_convert_fusion.2
  831.4 7.9 bitcast_convert_fusion.1
  839.3 7.9 fusion.24
  847.2 21.3 pad_maximum_fusion
  868.6 40.2 %copy.107 = bf16[2560,5760]{1,0:T(8,128)(2,1)} copy(bf16[2560,5760]{0,1:T(8,128)(2,1)} %pad_maximum_fusion) | data formatting | bytes 58982400
  912.3 1108.4 %all-reduce.59.cloned.1.call-done = f32[2560,8320]{0,1:T(8,128)} async-done(((f32[2560,8320]{0,1:T(8,128)}), f32[2560,8320]{0,1:T(8,128)}) %all-reduce.59.cloned.1.call-update) | async-done | bytes 85196816
  2020.7 5.5 fusion.129
  2036.8 455.7 %reduce-scatter.11.cloned.1.call-done = bf16[320,5760]{1,0:T(8,128)(2,1)} async-done(((bf16[2560,5760]{1,0:T(8,128)(2,1)}), bf16[320,5760]{1,0:T(8,128)(2,1)}) %reduce-scatter.11.cloned.1.call-update) | async-done | bytes 3686416
  2492.5 6.2 copy.108
  2498.8 4.8 fusion.131
  2503.6 4.1 convert_element_type.126
  2514.4 3.7 slice_bitcast_fusion
  (572 shorter events, 358.7 us)
Async XLA Ops:
  7.2 90.2 %all-gather.8.cloned.1.call-start = ((), (), s32[]{:S(2)}) async-start(), calls=%async_computation.3 | async-start | bytes 16384000 | tf_op jit(solution)/shard_map/all_gather | solution.py:84
  7.9 109.3 %all-gather.12.cloned.1.call-start = ((), (), s32[]{:S(2)}) async-start(), calls=%async_computation.5 | async-start | bytes 1638400 | tf_op jit(solution)/shard_map/all_gather | solution.py:87
  8.7 128.3 %all-gather.10.cloned.1.call-start = ((), (), s32[]{:S(2)}) async-start(), calls=%async_computation.4 | async-start | bytes 1638400 | tf_op jit(solution)/shard_map/all_gather | solution.py:88
  9.4 292.6 %all-gather.14.cloned.1.call-start = ((), (), s32[]{:S(2)}) async-start(), calls=%async_computation.6 | async-start | bytes 16384000 | tf_op jit(solution)/shard_map/all_gather | solution.py:85
  10.0 345.1 %all-gather.16.cloned.1.call-start = ((), (), s32[]{:S(2)}) async-start(), calls=%async_computation.7 | async-start | bytes 16384000 | tf_op jit(solution)/shard_map/all_gather | solution.py:86
  10.6 86.8 %copy-start.52 = (f32[2560]{0:T(1024)S(1)}, f32[2560]{0:T(1024)}, u32[]{:S(2)}) copy-start(f32[2560]{0:T(1024)} %param.25) | copy-start | bytes 30724
  10.6 353.6 %all-gather.20.cloned.1.call-start = ((), (), s32[]{:S(2)}) async-start(), calls=%async_computation.10 | async-start | bytes 3276800 | tf_op jit(solution)/shard_map/all_gather | solution.py:132
  11.2 381.2 %all-gather.18.cloned.1.call-start = ((), (), s32[]{:S(2)}) async-start(), calls=%async_computation.8 | async-start | bytes 3276800 | tf_op jit(solution)/shard_map/all_gather | solution.py:131
  12.4 97.0 %copy-start.98 = (f32[2,64]{1,0:T(2,128)}, f32[2,64]{1,0:T(2,128)S(1)}, u32[]{:S(2)}) copy-start(f32[2,64]{1,0:T(2,128)S(1)} %get-tuple-element.238) | copy-start | bytes 1540
  12.4 126.7 %copy-start.94 = (f32[2,64]{1,0:T(2,128)}, f32[2,64]{1,0:T(2,128)S(1)}, u32[]{:S(2)}) copy-start(f32[2,64]{1,0:T(2,128)S(1)} %get-tuple-element.235) | copy-start | bytes 1540
  12.4 126.7 %copy-start.96 = (f32[2,64]{1,0:T(2,128)}, f32[2,64]{1,0:T(2,128)S(1)}, u32[]{:S(2)}) copy-start(f32[2,64]{1,0:T(2,128)S(1)} %get-tuple-element.236) | copy-start | bytes 1540
  97.4 10.1 copy-start.111
  104.1 5.0 collective-permute-start.2
  107.6 31.5 %copy-start.55 = (f32[2560]{0:T(1024)}, f32[2560]{0:T(1024)S(1)}, u32[]{:S(2)}) copy-start(f32[2560]{0:T(1024)S(1)} %get-tuple-element.125) | copy-start | bytes 30724
  107.6 31.5 %copy-start.57 = (f32[2560]{0:T(1024)}, f32[2560]{0:T(1024)S(1)}, u32[]{:S(2)}) copy-start(f32[2560]{0:T(1024)S(1)} %get-tuple-element.126) | copy-start | bytes 30724
  107.6 31.5 %copy-start.60 = (f32[2560]{0:T(1024)}, f32[2560]{0:T(1024)S(1)}, u32[]{:S(2)}) copy-start(f32[2560]{0:T(1024)S(1)} %get-tuple-element.127) | copy-start | bytes 30724
  107.6 31.5 %copy-start.63 = (f32[2560]{0:T(1024)}, f32[2560]{0:T(1024)S(1)}, u32[]{:S(2)}) copy-start(f32[2560]{0:T(1024)S(1)} %get-tuple-element.128) | copy-start | bytes 30724
  119.0 625.5 %copy-start.3 = (f32[10,2,8,8,256]{4,3,0,2,1:T(8,128)}, f32[10,2,8,8,256]{4,3,0,2,1:T(8,128)S(1)}, u32[]{:S(2)}) copy-start(f32[10,2,8,8,256]{4,3,0,2,1:T(8,128)S(1)} %copy.116) | copy-start | bytes 3932164
  302.1 4.9 collective-permute-start
  307.0 5.7 collective-permute-start
  312.7 5.8 collective-permute-start
  318.5 6.6 collective-permute-start
  325.0 6.6 collective-permute-start
  331.6 6.6 collective-permute-start
  338.2 6.6 collective-permute-start
  364.2 124.5 %reduce-scatter.9.cloned.1.call-start = ((), (), s32[]{:S(2)}) async-start(), calls=%async_computation.11 | async-start | bytes 6553600 | tf_op jit(solution)/shard_map/reduce_scatter | solution.py:155
  392.4 11.4 copy-start.122
  392.4 26.3 %slice-start.4 = ((s8[9830400]{0:T(1024)(128)(4,1)}), s8[4194304]{0:T(1024)(128)(4,1)S(1)}, s32[]{:S(2)}) async-start(s8[9830400]{0:T(1024)(128)(4,1)} %bitcast.236), calls=%async_computation.18 | async-start | bytes 8388608
  392.4 26.3 %slice-start.5 = ((s8[9830400]{0:T(1024)(128)(4,1)}), s8[4194304]{0:T(1024)(128)(4,1)S(1)}, s32[]{:S(2)}) async-start(s8[9830400]{0:T(1024)(128)(4,1)} %bitcast.236), calls=%async_computation.19 | async-start | bytes 8388608
  403.8 14.9 slice-start.6
  403.8 24.2 slice-start.7
  403.8 24.2 slice-start.8
  437.1 88.9 %reduce-scatter.7.cloned.1.call-start = ((), (), s32[]{:S(2)}) async-start(), calls=%async_computation.9 | async-start | bytes 3276800 | tf_op jit(solution)/shard_map/reduce_scatter | solution.py:139
  447.1 1573.6 %all-reduce.59.cloned.1.call-start = ((), (), s32[]{:S(2)}) async-start(), calls=%async_computation.13 | async-start | bytes 170393600
  485.5 40.6 %copy-start.45 = (bf16[2,64,2560]{2,1,0:T(8,128)(2,1)S(1)}, bf16[2,64,2560]{2,1,0:T(8,128)(2,1)}, u32[]{:S(2)}) copy-start(bf16[2,64,2560]{2,1,0:T(8,128)(2,1)} %param.24) | copy-start | bytes 1966084
  529.4 10.9 copy-start.13
  587.1 22.4 copy-start.44
  679.8 55.7 %copy-start.56 = (f32[2560]{0:T(1024)S(1)}, f32[2560]{0:T(1024)}, u32[]{:S(2)}) copy-start(f32[2560]{0:T(1024)} %copy-done.55) | copy-start | bytes 30724
  679.8 55.7 %copy-start.58 = (f32[2560]{0:T(1024)S(1)}, f32[2560]{0:T(1024)}, u32[]{:S(2)}) copy-start(f32[2560]{0:T(1024)} %copy-done.57) | copy-start | bytes 30724
  679.8 55.7 %copy-start.61 = (f32[2560]{0:T(1024)S(1)}, f32[2560]{0:T(1024)}, u32[]{:S(2)}) copy-start(f32[2560]{0:T(1024)} %copy-done.60) | copy-start | bytes 30724
  679.8 55.7 %copy-start.64 = (f32[2560]{0:T(1024)S(1)}, f32[2560]{0:T(1024)}, u32[]{:S(2)}) copy-start(f32[2560]{0:T(1024)} %copy-done.63) | copy-start | bytes 30724
  679.8 55.7 %copy-start.67 = (f32[2560]{0:T(1024)S(1)}, f32[2560]{0:T(1024)}, u32[]{:S(2)}) copy-start(f32[2560]{0:T(1024)} %param.31) | copy-start | bytes 30724
  679.9 55.7 %copy-start.70 = (f32[2560]{0:T(1024)S(1)}, f32[2560]{0:T(1024)}, u32[]{:S(2)}) copy-start(f32[2560]{0:T(1024)} %param.33) | copy-start | bytes 30724
  679.9 55.7 %copy-start.74 = (f32[2560]{0:T(1024)S(1)}, f32[2560]{0:T(1024)}, u32[]{:S(2)}) copy-start(f32[2560]{0:T(1024)} %param.29) | copy-start | bytes 30724
  679.9 55.7 %copy-start.95 = (f32[2,64]{1,0:T(2,128)S(1)}, f32[2,64]{1,0:T(2,128)}, u32[]{:S(2)}) copy-start(f32[2,64]{1,0:T(2,128)} %copy-done.94) | copy-start | bytes 1540
  679.9 55.7 %copy-start.97 = (f32[2,64]{1,0:T(2,128)S(1)}, f32[2,64]{1,0:T(2,128)}, u32[]{:S(2)}) copy-start(f32[2,64]{1,0:T(2,128)} %copy-done.96) | copy-start | bytes 1540
  679.9 55.7 %copy-start.100 = (f32[2,64]{1,0:T(2,128)S(1)}, f32[2,64]{1,0:T(2,128)}, u32[]{:S(2)}) copy-start(f32[2,64]{1,0:T(2,128)} %copy-done.98) | copy-start | bytes 1540
  679.9 55.7 %copy-start.113 = (f32[2,64]{1,0:T(2,128)S(1)}, f32[2,64]{1,0:T(2,128)}, u32[]{:S(2)}) copy-start(f32[2,64]{1,0:T(2,128)} %get-tuple-element.237) | copy-start | bytes 1540
  679.9 55.7 %copy-start.116 = (f32[2,64]{1,0:T(2,128)S(1)}, f32[2,64]{1,0:T(2,128)}, u32[]{:S(2)}) copy-start(f32[2,64]{1,0:T(2,128)} %broadcast_subtract_fusion) | copy-start | bytes 1540
  690.8 5.7 collective-permute-start.1
  696.5 6.1 collective-permute-start.1
  702.6 6.6 collective-permute-start.1
  709.2 6.6 collective-permute-start.1
  715.8 6.8 collective-permute-start.1
  722.5 6.4 collective-permute-start.1
  728.9 6.6 collective-permute-start.1
  755.9 17.2 collective-permute-start.3
  783.7 10.6 copy-start.33
  794.2 10.6 copy-start.14
  794.2 10.6 copy-start.18
  804.8 10.6 copy-start.16
  821.2 1671.4 %reduce-scatter.11.cloned.1.call-start = ((), (), s32[]{:S(2)}) async-start(), calls=%async_computation.12 | async-start | bytes 33177600
  821.2 10.2 copy-start.123
  821.2 10.2 copy-start.126
  (100 other events, 325.3 us)
Sparse Core Ops, SparseCore 0:
  9.6 87.7 all-gather.7
  98.9 18.1 all-gather.11
  118.7 18.1 all-gather.9
  138.4 85.0 all-gather.13
  224.9 85.0 all-gather.15
  311.4 25.5 all-gather.19
  364.3 28.0 all-gather.17
  437.2 51.3 reduce-scatter.8
  491.4 34.6 reduce-scatter.6
  821.3 1199.3 all-reduce.58
  2025.1 467.3 reduce-scatter.10
where the time goes:
time: 2540 us; the launch traced here: 2530 us
  waiting for transfers between devices  1780 us (70%)
  local copies, waits for them, and re-layouts  369 us (15%)
  matrix products  184 us (7%)
  other arithmetic  134 us (5%)
  starting transfers between devices  46.5 us (2%)
    unnamed x13, waiting for transfers between devices  1570 us
    slice x41, local copies, waits for them, and re-layouts, local(): lax.associative_scan(combine, (following, grad_direct), axis=1, reverse=T...  97.4 us
    all_gather x1, waiting for transfers between devices, local(): lax.all_gather(w_x, 'wt', axis=0, tiled=True)  84.2 us
    unnamed x289, local copies, waits for them, and re-layouts  80.1 us
    slice x36, local copies, waits for them, and re-layouts, local(): lax.associative_scan(combine, (decay, driven), axis=1)  64.1 us
  transfers between devices with their start and end apart: 27, of which 23 were waited for; matrix products, arithmetic and copies ran while one was open for 15% of the time, Pallas kernels for 0%

commit v1 on v0

v1 whole, which is shorter than its diff:
```python
from functools import partial

import jax
import jax.numpy as jnp
from jax import lax
from jax.experimental import pallas as pl
from jax.experimental.pallas import tpu as pltpu
from jax.sharding import Mesh
from jax.sharding import PartitionSpec as P

SZ, SY, WX, WC = ("sz", "sy", "wx", "wc")
F32, BF16 = (jnp.float32, jnp.bfloat16)
HALO = 8
ROOT_2_PI = 0.7978845608028654
CUBIC = 0.044715
MIB = 1 << 20


def swap(value, axis):
    return lax.ppermute(value, axis, [(0, 1), (1, 0)])


def shift(value, axis, steps):
    count = lax.axis_size(axis)
    initial, last = (max(0, -steps), min(count, count - steps))
    return lax.ppermute(value, axis, [(source, source + steps) for source in range(initial, last)])


def along_seq(value, steps):
    count = lax.axis_size(SZ) * lax.axis_size(SY)
    initial, last = (max(0, -steps), min(count, count - steps))
    return lax.ppermute(
        value, (SZ, SY), [(source, source + steps) for source in range(initial, last)]
    )


def pick(bit, zero, one):
    return jnp.where(bit == 0, zero, one)


def after(value, *others):
    return lax.optimization_barrier((value, *others))[0]


def gelu_pair(value):
    square = value * value
    tanh = jnp.tanh(ROOT_2_PI * value * (1.0 + CUBIC * square))
    half = 0.5 * (1.0 + tanh)
    slope = half + 0.5 * value * (1.0 - tanh * tanh) * (
        ROOT_2_PI * (1.0 + 3.0 * CUBIC * square)
    )
    return value * half, slope


def dot(left, right):
    return jnp.dot(left, right, preferred_element_type=F32)


def dot_nt(left, right):
    return lax.dot_general(left, right, (((1,), (1,)), ((), ())), preferred_element_type=F32)


def dot_tn(left, right):
    return lax.dot_general(left, right, (((0,), (0,)), ((), ())), preferred_element_type=F32)


def params(mib):
    return pltpu.CompilerParams(
        dimension_semantics=("arbitrary",), vmem_limit_bytes=mib * MIB
    )


def cost(flops, nbytes):
    return pl.CostEstimate(flops=int(flops), bytes_accessed=int(nbytes), transcendentals=0)


def split_columns(value, wx, wc):
    quarter = value.shape[-1] // 4
    parts = [value[..., i * quarter : (i + 1) * quarter] for i in range(4)]
    near = [pick(wx, parts[0], parts[2]), pick(wx, parts[1], parts[3])]
    far = [pick(wx, parts[2], parts[0]), pick(wx, parts[3], parts[1])]
    keep = jnp.concatenate([pick(wc, near[0], near[1]), pick(wc, near[1], near[0])], axis=-1)
    send = jnp.concatenate([pick(wc, far[0], far[1]), pick(wc, far[1], far[0])], axis=-1)
    return keep, send


def join_columns(near, far, wx, wc):
    near = [pick(wc, near[0], near[1]), pick(wc, near[1], near[0])]
    far = [pick(wc, far[0], far[1]), pick(wc, far[1], far[0])]
    return jnp.concatenate(
        [
            pick(wx, near[0], far[0]),
            pick(wx, near[1], far[1]),
            pick(wx, far[0], near[0]),
            pick(wx, far[1], near[1]),
        ],
        axis=-1,
    )


def project_kernel(recv, keep, w_own, w_oth, send_out, own_out, left):
    rows, quarter = recv.shape[0], w_own.shape[0]

    @pl.when(pl.program_id(0) == 0)
    def _():
        left[:rows] = recv[...]
        left[rows:] = keep[...]

    total = dot(left[:, :quarter], w_own[...]) + dot(left[:, quarter:], w_oth[...])
    send_out[...] = total[:rows].astype(BF16)
    own_out[...] = total[rows:]


def project(recv, keep, w_own, w_oth):
    rows, half = recv.shape
    quarter, width = w_own.shape
    tile = 512
    whole = pl.BlockSpec((rows, half), lambda j: (0, 0))
    column = pl.BlockSpec((quarter, tile), lambda j: (0, j))
    out = pl.BlockSpec((rows, tile), lambda j: (0, j))
    return pl.pallas_call(
        project_kernel,
        grid=(width // tile,),
        in_specs=[whole, whole, column, column],
        out_specs=[out, out],
        out_shape=[
            jax.ShapeDtypeStruct((rows, width), BF16),
            jax.ShapeDtypeStruct((rows, width), F32),
        ],
        scratch_shapes=[pltpu.VMEM((2 * rows, half), BF16)],
        compiler_params=params(32),
        cost_estimate=cost(4 * rows * half * width, 4 * half * width),
        name="project",
    )(recv, keep, w_own, w_oth)


def project_back_kernel(count, *refs):
    tokens, weights = refs[: 2 * count], refs[2 * count : 4 * count]
    send_out, own_out = refs[4 * count : 4 * count + 2]
    lefts = refs[4 * count + 2 :]
    rows = tokens[0].shape[0]

    @pl.when(pl.program_id(0) == 0)
    def _():
        for i in range(count):
            lefts[i][:rows] = tokens[2 * i][...]
            lefts[i][rows:] = tokens[2 * i + 1][...]

    total = None
    for i in range(count):
        right = jnp.concatenate([weights[2 * i][...], weights[2 * i + 1][...]], axis=0)
        term = dot_nt(lefts[i][...], right)
        total = term if total is None else total + term
    tile = total.shape[1] // 2
    for i in range(2):
        send_out[i] = total[:rows, i * tile : (i + 1) * tile].astype(BF16)
        own_out[i] = total[rows:, i * tile : (i + 1) * tile]


def project_back(terms):
    count = len(terms)
    rows, width = terms[0][0].shape
    quarter = terms[0][2].shape[0]
    tile = 128
    whole = pl.BlockSpec((rows, width), lambda j: (0, 0))
    row = pl.BlockSpec((tile, width), lambda j: (j, 0))
    out = pl.BlockSpec((2, rows, tile), lambda j: (0, 0, j))
    return pl.pallas_call(
        partial(project_back_kernel, count),
        grid=(quarter // tile,),
        in_specs=[whole] * (2 * count) + [row] * (2 * count),
        out_specs=[out, out],
        out_shape=[
            jax.ShapeDtypeStruct((2, rows, quarter), BF16),
            jax.ShapeDtypeStruct((2, rows, quarter), F32),
        ],
        scratch_shapes=[pltpu.VMEM((2 * rows, width), BF16)] * count,
        compiler_params=params(40),
        cost_estimate=cost(
            8 * count * rows * quarter * width, 4 * count * quarter * width
        ),
        name="project_back",
    )(*[t for term in terms for t in term[:2]], *[w for term in terms for w in term[2:]])


def less_one_exp(value):
    series = 1.0
    for n in (9, 8, 7, 6, 5, 4, 3, 2):
        series = 1.0 + value * (1.0 / n) * series
    return jnp.where(value > -0.5, -value * series, 1.0 - jnp.exp(value))


def shifted_down(value, steps, fill):
    edge = jnp.full((value.shape[0], steps, value.shape[2]), fill, F32)
    return jnp.concatenate([edge, value[:, : value.shape[1] - steps]], axis=1)


def shifted_up(value, steps, fill):
    edge = jnp.full((value.shape[0], steps, value.shape[2]), fill, F32)
    return jnp.concatenate([value[:, steps:], edge], axis=1)


def scan_rows(decay, driven, mover):
    steps = 1
    while steps < decay.shape[1]:
        driven = driven + decay * mover(driven, steps, 0.0)
        decay = decay * mover(decay, steps, 1.0)
        steps *= 2
    return decay, driven


def tap_mask(places, offset):
    return (places >= offset).astype(F32)


def recur_kernel(
    own,
    recv,
    halo,
    places,
    conv_w,
    conv_b,
    gate_a,
    gate_i,
    bias_a,
    bias_i,
    decay_log,
    branch_out,
    conv_out,
    rec_out,
    in_out,
    run_out,
    state_out,
    ends_out,
):
    batches, length, width = own.shape
    branch = (own[...] + recv[...].astype(F32)).astype(BF16)
    branch_out[...] = branch
    extended = jnp.concatenate([halo[...], branch.astype(F32)], axis=1)
    spot = places[...]
    total = jnp.zeros((batches, length, width), F32) + conv_b[...][None]
    for offset in range(conv_w.shape[0]):
        moved = extended[:, HALO - offset : HALO - offset + length]
        total = total + conv_w[offset : offset + 1][None] * moved * tap_mask(spot, offset)
    conv = total.astype(BF16)
    conv_out[...] = conv
    flat = conv.reshape(batches * length, width)
    shape = (batches, length, width)
    gate_rec = jax.nn.sigmoid(dot(flat, gate_a[...]) + bias_a[...]).reshape(shape)
    gate_in = jax.nn.sigmoid(dot(flat, gate_i[...]) + bias_i[...]).reshape(shape)
    rec_out[...] = gate_rec
    in_out[...] = gate_in
    log_a = -8.0 * gate_rec * jnp.exp(decay_log[...])[None]
    alive = tap_mask(spot, 1)
    root = jnp.sqrt(less_one_exp(2.0 * log_a))
    multiplier = alive * root + (1.0 - alive)
    decay = jnp.exp(log_a) * alive
    driven = conv.astype(F32) * gate_in * multiplier
    running, state = scan_rows(decay, driven, shifted_down)
    run_out[...] = running
    state_out[...] = state
    for b in range(batches):
        ends_out[b : b + 1] = running[b, length - 1 :]
        ends_out[batches + b : batches + b + 1] = state[b, length - 1 :]


def head_specs(batches, length, head, taps):
    tokens = pl.BlockSpec((batches, length, head), lambda h: (0, 0, h))
    edge = pl.BlockSpec((batches, HALO, head), lambda h: (0, 0, h))
    place = pl.BlockSpec((batches, length, 1), lambda h: (0, 0, 0))
    row = pl.BlockSpec((1, head), lambda h: (0, h))
    tap = pl.BlockSpec((taps, head), lambda h: (0, h))
    gates = [
        pl.BlockSpec((head, head), lambda h: (h, 0)),
        pl.BlockSpec((head, head), lambda h: (h, 1)),
    ]
    ends = pl.BlockSpec((2 * batches, head), lambda h: (0, h))
    carry = pl.BlockSpec((batches, 1, head), lambda h: (0, 0, h))
    return tokens, edge, place, row, tap, gates, ends, carry


def recur(own, recv, halo, places, conv_w, conv_b, gates, bias_a, bias_i, decay_log):
    batches, length, features = own.shape
    head = gates.shape[1] // 2
    tokens, edge, place, row, tap, gate, ends, _ = head_specs(
        batches, length, head, conv_w.shape[0]
    )
    full = lambda dtype: jax.ShapeDtypeStruct((batches, length, features), dtype)
    return pl.pallas_call(
        recur_kernel,
        grid=(features // head,),
        in_specs=[tokens, tokens, edge, place, tap, row, *gate, row, row, row],
        out_specs=[tokens] * 6 + [ends],
        out_shape=[full(BF16), full(BF16)]
        + [full(F32)] * 4
        + [jax.ShapeDtypeStruct((2 * batches, features), F32)],
        compiler_params=params(32),
        cost_estimate=cost(200 * batches * length * features, 40 * batches * length * features),
        name="recur",
    )(own, recv, halo, places, conv_w, conv_b, gates, gates, bias_a, bias_i, decay_log)


def unroll_kernel(
    mixed_grad,
    own_y,
    recv_y,
    running,
    local_state,
    carry,
    gate_rec,
    places,
    decay_log,
    pre_out,
    behind_out,
    local_out,
    ends_out,
):
    batches, length, _ = mixed_grad.shape
    pulled = mixed_grad[...].astype(F32)
    branch_y, slope = gelu_pair(own_y[...] + recv_y[...].astype(F32))
    state = local_state[...] + running[...] * carry[...]
    pre_out[...] = (pulled * state * slope).astype(BF16)
    log_a = -8.0 * gate_rec[...] * jnp.exp(decay_log[...])[None]
    decay = jnp.exp(log_a) * tap_mask(places[...], 1)
    following = shifted_up(decay, 1, 1.0)
    behind, local = scan_rows(following, pulled * branch_y, shifted_up)
    behind_out[...] = behind
    local_out[...] = local
    for b in range(batches):
        ends_out[b : b + 1] = running[b, length - 1 :, :]
        ends_out[batches + b : batches + b + 1] = decay[b, :1] * local[b, :1]


def unroll(mixed_grad, own_y, recv_y, running, local_state, carry, gate_rec, places, decay_log, head):
    batches, length, features = mixed_grad.shape
    tokens, _, place, row, _, _, ends, carried = head_specs(batches, length, head, 1)
    full = lambda dtype: jax.ShapeDtypeStruct((batches, length, features), dtype)
    return pl.pallas_call(
        unroll_kernel,
        grid=(features // head,),
        in_specs=[tokens] * 5 + [carried, tokens, place, row],
        out_specs=[tokens] * 3 + [ends],
        out_shape=[full(BF16), full(F32), full(F32)]
        + [jax.ShapeDtypeStruct((2 * batches, features), F32)],
        compiler_params=params(32),
        cost_estimate=cost(200 * batches * length * features, 40 * batches * length * features),
        name="unroll",
    )(mixed_grad, own_y, recv_y, running, local_state, carry, gate_rec, places, decay_log)


def recur_back_kernel(
    behind,
    local_grad,
    carry_back,
    running,
    local_state,
    carry,
    gate_rec,
    gate_in,
    conv,
    branch,
    halo,
    places,
    conv_w,
    gate_a,
    gate_i,
    decay_log,
    spread_out,
    earlier_out,
    wa_out,
    wi_out,
    sums_out,
):
    batches, length, width = behind.shape
    shape = (batches, length, width)
    rows = batches * length
    spot = places[...]
    alive = tap_mask(spot, 1)
    rate = jnp.exp(decay_log[...])[None]
    rec, inner = gate_rec[...], gate_in[...]
    log_a = -8.0 * rec * rate
    raw = jnp.exp(log_a)
    root = jnp.sqrt(less_one_exp(2.0 * log_a))
    multiplier = alive * root + (1.0 - alive)
    conv_low = conv[...]
    conv_full = conv_low.astype(F32)
    grad_state = local_grad[...] + behind[...] * carry_back[...]
    state = local_state[...] + running[...] * carry[...]
    before = jnp.concatenate([carry[...], state[:, : length - 1]], axis=1)
    scaled = grad_state * conv_full * inner
    grad_log = alive * raw * (grad_state * before - scaled * raw / root)
    grad_a = grad_log * (-8.0 * rate) * rec * (1.0 - rec)
    grad_i = scaled * multiplier * (1.0 - inner)
    low_a = grad_a.astype(BF16).reshape(rows, width)
    low_i = grad_i.astype(BF16).reshape(rows, width)
    pulled = grad_state * inner * multiplier
    pulled = pulled + (dot_nt(low_a, gate_a[...]) + dot_nt(low_i, gate_i[...])).reshape(shape)
    pulled = pulled.astype(BF16).astype(F32)
    flat = conv_low.reshape(rows, width)
    wa_out[...] = dot_tn(flat, low_a).astype(BF16)
    wi_out[...] = dot_tn(flat, low_i).astype(BF16)
    extended = jnp.concatenate([halo[...], branch[...].astype(F32)], axis=1)
    taps = conv_w.shape[0]
    spread = jnp.zeros((batches, length + HALO, width), F32)
    blank = jnp.zeros((batches, HALO, width), F32)
    sums = []
    add = lambda value: jnp.sum(value.reshape(rows, width), axis=0, keepdims=True)
    for offset in range(taps):
        masked = pulled * tap_mask(spot, offset)
        weighted = jnp.concatenate([blank, conv_w[offset : offset + 1][None] * masked], axis=1)
        spread = spread + (shifted_up(weighted, offset, 0.0) if offset else weighted)
        sums.append(add(masked * extended[:, HALO - offset : HALO - offset + length]))
    earlier_out[...] = spread[:, :HALO]
    spread_out[...] = spread[:, HALO:]
    sums += [add(pulled), add(grad_a), add(grad_i), add(grad_log * log_a)]
    sums_out[...] = jnp.concatenate(sums, axis=0)


def recur_back(
    behind,
    local_grad,
    carry_back,
    running,
    local_state,
    carry,
    gate_rec,
    gate_in,
    conv,
    branch,
    halo,
    places,
    conv_w,
    gates,
    decay_log,
):
    batches, length, features = behind.shape
    head = gates.shape[1] // 2
    taps = conv_w.shape[0]
    tokens, edge, place, row, tap, gate, _, carried = head_specs(batches, length, head, taps)
    block = pl.BlockSpec((head, head), lambda h: (h, 0))
    return pl.pallas_call(
        recur_back_kernel,
        grid=(features // head,),
        in_specs=[tokens, tokens, carried, tokens, tokens, carried]
        + [tokens] * 4
        + [edge, place, tap, *gate, row],
        out_specs=[
            tokens,
            edge,
            block,
            block,
            pl.BlockSpec((taps + 4, head), lambda h: (0, h)),
        ],
        out_shape=[
            jax.ShapeDtypeStruct((batches, length, features), F32),
            jax.ShapeDtypeStruct((batches, HALO, features), F32),
            jax.ShapeDtypeStruct((features, head), BF16),
            jax.ShapeDtypeStruct((features, head), BF16),
            jax.ShapeDtypeStruct((taps + 4, features), F32),
        ],
        compiler_params=params(40),
        cost_estimate=cost(300 * batches * length * features, 50 * batches * length * features),
        name="recur_back",
    )(
        behind,
        local_grad,
        carry_back,
        running,
        local_state,
        carry,
        gate_rec,
        gate_in,
        conv,
        branch,
        halo,
        places,
        conv_w,
        gates,
        gates,
        decay_log,
    )


def units_kernel(*refs):
    normed, cots = refs[:4], refs[4:8]
    w_gate, w_up, w_down, hidden_out, gate_out, up_out, tokens, pulls = refs[8:]
    rows = normed[0].shape[0]

    @pl.when(pl.program_id(0) == 0)
    def _():
        for i in range(4):
            tokens[i * rows : (i + 1) * rows] = normed[i][...]
            pulls[i * rows : (i + 1) * rows] = cots[i][...]

    gate_pre = dot(tokens[...], w_gate[...])
    up_pre = dot(tokens[...], w_up[...])
    pulled = dot_nt(pulls[...], w_down[...])
    act, slope = gelu_pair(gate_pre)
    hidden_out[...] = (act * up_pre).astype(BF16)
    gate_out[...] = (pulled * up_pre * slope).astype(BF16)
    up_out[...] = (pulled * act).astype(BF16)


def units(normed, cots, w_gate, w_up, w_down, begin, count, tile):
    rows, width = normed[0].shape
    whole = pl.BlockSpec((rows, width), lambda j: (0, 0))
    column = pl.BlockSpec((width, tile), lambda j: (0, begin + j))
    out = pl.BlockSpec((4 * rows, tile), lambda j: (0, j))
    return pl.pallas_call(
        units_kernel,
        grid=(count,),
        in_specs=[whole] * 8
        + [column, column, pl.BlockSpec((tile, width), lambda j: (begin + j, 0))],
        out_specs=[out] * 3,
        out_shape=[jax.ShapeDtypeStruct((4 * rows, count * tile), BF16)] * 3,
        scratch_shapes=[pltpu.VMEM((4 * rows, width), BF16)] * 2,
        compiler_params=params(52),
        cost_estimate=cost(24 * rows * width * count * tile, 6 * width * count * tile),
        name="units",
    )(*normed, *cots, w_gate, w_up, w_down)


def units_back_kernel(parts, *refs):
    hidden, gate, up = refs[:parts], refs[parts : 2 * parts], refs[2 * parts : 3 * parts]
    w_gate, w_up, w_down, normed_out, ffn_out = refs[3 * parts :]
    pulled, made, start = None, None, 0
    for i in range(parts):
        span = slice(start, start + hidden[i].shape[1])
        term = dot_nt(gate[i][...], w_gate[:, span]) + dot_nt(up[i][...], w_up[:, span])
        piece = dot(hidden[i][...], w_down[span])
        pulled = term if pulled is None else pulled + term
        made = piece if made is None else made + piece
        start = span.stop
    normed_out[...] = pulled.astype(BF16)
    ffn_out[...] = made.astype(BF16)


def units_back(hidden, gate, up, w_gate, w_up, w_down):
    tile = 256
    rows = hidden[0].shape[0]
    width, held = w_gate.shape
    blocks = [pl.BlockSpec(v.shape, lambda j: (0, 0)) for v in (*hidden, *gate, *up)]
    row = pl.BlockSpec((tile, held), lambda j: (j, 0))
    out = pl.BlockSpec((rows, tile), lambda j: (0, j))
    return pl.pallas_call(
        partial(units_back_kernel, len(hidden)),
        grid=(width // tile,),
        in_specs=blocks + [row, row, pl.BlockSpec((held, tile), lambda j: (0, j))],
        out_specs=[out, out],
        out_shape=[jax.ShapeDtypeStruct((rows, width), BF16)] * 2,
        compiler_params=params(48),
        cost_estimate=cost(6 * rows * width * held, 6 * width * held),
        name="units_back",
    )(*hidden, *gate, *up, w_gate, w_up, w_down)


def token_sum(value):
    half = value.shape[0] // 2
    quarter = half // 2
    pair = value[:half].astype(F32) + swap(value[half:], WC).astype(F32)
    return pair[:quarter] + swap(pair[quarter:].astype(BF16), WX).astype(F32)


def carry_over(ends, bit, direction):
    half = ends.shape[0] // 2
    other = swap(ends, SY)
    own_run, own_end = ends[:half], ends[half:]
    oth_run, oth_end = other[:half], other[half:]
    is_last = bit if direction > 0 else 1 - bit
    ahead = pick(is_last, oth_run, own_run) * pick(is_last, own_end, oth_end)
    joined = jnp.concatenate([own_run * oth_run, ahead + pick(is_last, oth_end, own_end)], axis=0)
    entering = jnp.zeros_like(own_end)
    arrived = [shift(joined, SZ, direction * k) for k in range(1, lax.axis_size(SZ))]
    for far in reversed(arrived):
        entering = far[half:] + far[:half] * entering
    return pick(is_last, entering, oth_end + oth_run * entering)


def rows_of_eight(value):
    far = lax.axis_size(SZ)
    features, rows = value.shape
    held = [value.reshape(far, 2, 2, 2, features // (8 * far), rows)]
    for axis, place in ((WX, 2), (SY, 1), (WC, 1)):
        bit = lax.axis_index(axis)
        halves = [[lax.index_in_dim(v, i, place, keepdims=False) for i in (0, 1)] for v in held]
        mine = [pick(bit, low, high) for low, high in halves]
        sent = [pick(bit, high, low) for low, high in halves]
        got = swap(jnp.stack(sent), axis)
        held = mine + [got[i] for i in range(len(sent))]
    return jnp.concatenate([v.reshape(-1, rows) for v in held], axis=1)


def sum_of_eight(value):
    bits = [lax.axis_index(a) for a in (WC, WX, SY)]
    far = lax.axis_size(SZ)
    features, width = value.shape
    held = value.reshape(far, 2, 2, 2, features // (8 * far), width)
    for place, (bit, axis) in zip((3, 2, 1), zip(bits, (WC, WX, SY))):
        low, high = (lax.index_in_dim(held, i, place, keepdims=False) for i in (0, 1))
        got = swap(pick(bit, high, low), axis)
        held = (pick(bit, low, high).astype(F32) + got.astype(F32)).astype(BF16)
    return held.reshape(-1, width)


def eight_of(own, x_part):
    pair = jnp.concatenate([own, x_part], axis=0)
    four = jnp.concatenate([pair, swap(pair, SY)], axis=0)
    return jnp.concatenate([four, swap(four, WC)], axis=0)


def scatter_far(value):
    return lax.psum_scatter(value, SZ, scatter_dimension=0, tiled=True)


def local(
    inputs,
    positions,
    cotangent,
    gain,
    w_x,
    w_y,
    conv_w,
    conv_b,
    gate_a,
    bias_a,
    gate_i,
    bias_i,
    decay_log,
    w_out,
    gain2,
    w_gate,
    w_up,
    w_down,
):
    batches, length, features = inputs.shape
    rows = batches * length
    head = gate_a.shape[1]
    taps = conv_w.shape[0]
    held = w_gate.shape[1]
    far = lax.axis_size(SZ)
    wx, wc, sy = (lax.axis_index(a) for a in (WX, WC, SY))
    as_row = lambda v: v.reshape(1, features)
    cube = lambda v: v.reshape(batches, length, features)
    flat = lambda v: v.reshape(rows, features)

    source = flat(inputs).astype(F32)
    norm_scale = lax.rsqrt(jnp.mean(source * source, axis=-1, keepdims=True) + 1e-06)
    normed = (source * norm_scale * gain).astype(BF16)
    keep, send = split_columns(normed, wx, wc)
    recv = swap(send, WX)
    oth_x, oth_y, oth_out = swap(w_x, WC), swap(w_y, WC), swap(w_out, WC)
    gates = lax.all_gather(
        jnp.concatenate([gate_a, gate_i], axis=1), (WX, WC), axis=0, tiled=True
    )
    sent_x, own_x = project(recv, keep, w_x, oth_x)
    recv_x = swap(sent_x, WX)
    sent_y, own_y = project(recv, keep, w_y, oth_y)
    recv_y = swap(after(sent_y, recv_x), WX)

    own_x, recv_x, own_y, recv_y = cube(own_x), cube(recv_x), cube(own_y), cube(recv_y)
    edge = length - (taps - 1)
    tail = (own_x[:, edge:] + recv_x[:, edge:].astype(F32)).astype(BF16)
    halo = jnp.pad(along_seq(tail, 1).astype(F32), ((0, 0), (HALO - (taps - 1), 0), (0, 0)))
    places = positions[..., None]
    branch_x, conv, gate_rec, gate_in, running, local_state, ends = recur(
        own_x,
        recv_x,
        halo,
        places,
        conv_w,
        as_row(conv_b),
        gates,
        as_row(bias_a),
        as_row(bias_i),
        as_row(decay_log),
    )
    carry = carry_over(ends, sy, 1)[:, None]

    cot = flat(cotangent)
    cot_x = swap(after(cot, recv_y), WX)
    cots = [cot, cot_x, swap(cot, WC), swap(cot_x, WC)]
    every_cot = jnp.concatenate(cots, axis=0)

    branch_y = gelu_pair(own_y + recv_y.astype(F32))[0]
    mixed = flat(((local_state + running * carry) * branch_y).astype(BF16))
    keep, send = split_columns(mixed, wx, wc)
    sent, own = project(swap(send, WX), keep, w_out, oth_out)
    stream = source + own + swap(sent, WX).astype(F32)
    second_scale = lax.rsqrt(jnp.mean(stream * stream, axis=-1, keepdims=True) + 1e-06)
    normed_two = (stream * second_scale * gain2).astype(BF16)
    normed_x = swap(normed_two, WX)
    tokens = [normed_two, normed_x, swap(normed_two, WC), swap(normed_x, WC)]
    every_normed = jnp.concatenate(tokens, axis=0)

    def half_of_rows(value):
        turned = value.T.reshape(far, 2, features // (2 * far), -1)
        mine = pick(sy, turned[:, 0], turned[:, 1])
        got = swap(pick(sy, turned[:, 1], turned[:, 0]), SY)
        return jnp.concatenate([mine, got], axis=-1).reshape(features // 2, -1)

    cot_rows = half_of_rows(every_cot)

    tile = 384
    tiles = held // tile
    cuts = [(0, 1), (1, tiles - 1)]
    acted = [units(tokens, cots, w_gate, w_up, w_down, b, n, tile) for b, n in cuts]
    hidden, gate_grad, up_grad = zip(*acted)

    def whole_units(parts):
        got = [swap(v, SY) for v in parts]
        return [jnp.concatenate([a, b], axis=0) for a, b in zip(parts, got)]

    def far_sum(left, parts):
        return [scatter_far(dot(left, v).astype(BF16)) for v in parts]

    down_sums = far_sum(cot_rows, whole_units(hidden))
    normed_rows = half_of_rows(every_normed)

    pulled, made = units_back(hidden, gate_grad, up_grad, w_gate, w_up, w_down)
    grad_normed_two = token_sum(pulled)
    ffn_out = token_sum(made)
    output = (stream + ffn_out).astype(BF16)
    weighted_two = grad_normed_two * gain2
    grad_stream = (
        cot.astype(F32)
        + weighted_two * second_scale
        - stream * second_scale**3 * jnp.mean(weighted_two * stream, axis=-1, keepdims=True)
    )
    grad_proj = grad_stream.astype(BF16)

    whole_gate = jnp.concatenate(whole_units(gate_grad), axis=1)
    gate_sums = far_sum(normed_rows, [whole_gate])[0]
    whole_up = jnp.concatenate(whole_units(up_grad), axis=1)
    up_sums = far_sum(normed_rows, [whole_up])[0]

    proj_x = swap(grad_proj, WX)
    sent, own = project_back([(proj_x, grad_proj, w_out, oth_out)])
    grad_mixed = cube(join_columns(own, swap(sent, WX).astype(F32), wx, wc))
    grad_pre, behind, local_grad, back_ends = unroll(
        grad_mixed,
        own_y,
        recv_y,
        running,
        local_state,
        carry,
        gate_rec,
        places,
        as_row(decay_log),
        head,
    )
    carry_back = carry_over(back_ends, sy, -1)[:, None]
    spread, earlier, grad_wa, grad_wi, sums = recur_back(
        behind,
        local_grad,
        carry_back,
        running,
        local_state,
        carry,
        gate_rec,
        gate_in,
        conv,
        branch_x,
        halo,
        places,
        conv_w,
        gates,
        as_row(decay_log),
    )
    later = along_seq(earlier[:, HALO - (taps - 1) :].astype(BF16), -1).astype(F32)
    grad_branch = flat(
        (spread + jnp.pad(later, ((0, 0), (edge, 0), (0, 0)))).astype(BF16)
    )
    grad_pre = flat(grad_pre)
    pre_x, branch_grad_x = swap(grad_pre, WX), swap(grad_branch, WX)
    sent, own = project_back(
        [(branch_grad_x, grad_branch, w_x, oth_x), (pre_x, grad_pre, w_y, oth_y)]
    )
    grad_normed = join_columns(own, swap(sent, WX).astype(F32), wx, wc)
    weighted = grad_normed * gain
    input_grad = (
        grad_stream
        + weighted * norm_scale
        - source * norm_scale**3 * jnp.mean(weighted * source, axis=-1, keepdims=True)
    )

    normed_eight = rows_of_eight(normed.T)
    mixed_eight = rows_of_eight(mixed.T)
    out_sums = scatter_far(dot(mixed_eight, eight_of(grad_proj, proj_x)).astype(BF16))
    y_sums = scatter_far(dot(normed_eight, eight_of(grad_pre, pre_x)).astype(BF16))
    x_sums = scatter_far(dot(normed_eight, eight_of(grad_branch, branch_grad_x)).astype(BF16))
    small = jnp.concatenate(
        [
            jnp.sum(grad_normed * source * norm_scale, axis=0)[None],
            jnp.sum(grad_normed_two * stream * second_scale, axis=0)[None],
            sums,
        ],
        axis=0,
    )
    small = jnp.pad(small.T, ((0, 0), (0, 128 - small.shape[0]))).astype(BF16)
    rest = scatter_far(
        sum_of_eight(jnp.concatenate([grad_wa, grad_wi, small], axis=1))
    ).astype(F32)
    grads = rest[:, 2 * head :]
    return (
        cube(output),
        cube(input_grad),
        grads[:, 0],
        x_sums.astype(F32),
        y_sums.astype(F32),
        grads[:, 2 : 2 + taps].T,
        grads[:, 2 + taps],
        rest[:, :head],
        grads[:, 3 + taps],
        rest[:, head : 2 * head],
        grads[:, 4 + taps],
        grads[:, 5 + taps],
        out_sums.astype(F32),
        grads[:, 1],
        gate_sums.astype(F32),
        up_sums.astype(F32),
        jnp.concatenate([v.T for v in down_sums], axis=0).astype(F32),
    )


def solution(mesh):
    seq, wt = mesh.devices.shape
    split = Mesh(mesh.devices.reshape(seq // 2, 2, wt // 2, 2), (SZ, SY, WX, WC))
    s, w = (SZ, SY), (WX, WC)
    everywhere = (SZ, SY, WX, WC)
    return jax.shard_map(
        local,
        mesh=split,
        in_specs=(
            P(w, s, None),
            P(w, s),
            P(w, s, None),
            P(),
            P(w, None),
            P(w, None),
            P(),
            P(),
            P(w, None),
            P(),
            P(w, None),
            P(),
            P(),
            P(w, None),
            P(),
            P(None, w),
            P(None, w),
            P(w, None),
        ),
        out_specs=(
            P(w, s, None),
            P(w, s, None),
            P(everywhere),
            P(everywhere, None),
            P(everywhere, None),
            P(None, everywhere),
            P(everywhere),
            P(everywhere, None),
            P(everywhere),
            P(everywhere, None),
            P(everywhere),
            P(everywhere),
            P(everywhere, None),
            P(everywhere),
            P(s, w),
            P(s, w),
            P(w, s),
        ),
        check_vma=False,
    )
```

time: 2540 us -> 909 us (0.36)
  waiting for transfers between devices: 1780 us -> 544 us
  local copies, waits for them, and re-layouts: 369 us -> 66.2 us
  matrix products: 184 us -> 46.1 us
  Pallas kernels: 0 us -> 105 us
  other arithmetic: 134 us -> 52.6 us
  starting transfers between devices: 46.5 us -> 72.7 us
    unnamed x13 -> x9, waiting for transfers between devices: 1570 us -> 0.15 us
    ppermute x16 -> x56, waiting for transfers between devices: 47.2 us -> 441 us  [the longest x48 432 us: swap(): return lax.ppermute(value, axis, [(0, 1), (1, 0)])]
    slice x84 -> x10, local copies, waits for them, and re-layouts: 175 us -> 5.23 us  [the longest x2 1.64 us: token_sum(): pair = value[:half].astype(F32) + swap(value[half:], WC).astype(F32)]
    dot_general x24 -> x7, matrix products: 184 us -> 46.1 us  [dot(): return jnp.dot(left, right, preferred_element_type=F32)]
    all_gather x7 -> x1, waiting for transfers between devices: 125 us -> 0.02 us  [local(): lax.all_gather(jnp.concatenate([gate_a, gate_i], axis=1), (WX, WC), axis=...]
    pallas_call x0 -> x11, Pallas kernels: none -> 105 us  [the longest x2 31.2 us: units(): pl.pallas_call(units_kernel, grid=(count,), in_specs=[whole] * 8 + [colum...]
    pad x40 -> x0, local copies, waits for them, and re-layouts: 75.2 us -> none  [the longest x20 47.3 us: local(): lax.associative_scan(combine, (decay, driven), axis=1)]
    reduce_scatter x2 -> x8, waiting for transfers between devices: 37.9 us -> 104 us  [scatter_far(): return lax.psum_scatter(value, SZ, scatter_dimension=0, tiled=True)]
  transfers between devices with their start and end apart: 27 -> 65, of which waited for: 23 -> 41; matrix products, arithmetic and copies ran while one was open for 15% -> 12% of each run, Pallas kernels for 0% -> 2%
where the time goes in v1:
time: 909 us; the launch traced here: 903 us
  waiting for transfers between devices  544 us (60%)
  Pallas kernels  105 us (12%)
  starting transfers between devices  72.7 us (8%)
  local copies, waits for them, and re-layouts  66.2 us (7%)
  other arithmetic  52.6 us (6%)
  matrix products  46.1 us (5%)
  between operations  15.6 us (2%)
    ppermute x48, waiting for transfers between devices, swap(): return lax.ppermute(value, axis, [(0, 1), (1, 0)])  432 us
    reduce_scatter x8, waiting for transfers between devices, scatter_far(): return lax.psum_scatter(value, SZ, scatter_dimension=0, tiled=True)  104 us
    ppermute x48, starting transfers between devices, swap(): return lax.ppermute(value, axis, [(0, 1), (1, 0)])  52.1 us
    unnamed x245, local copies, waits for them, and re-layouts  49 us
    dot_general x7, matrix products, dot(): return jnp.dot(left, right, preferred_element_type=F32)  46.1 us
    pallas_call x2, Pallas kernels, units(): pl.pallas_call(units_kernel, grid=(count,), in_specs=[whole] * 8 + [colum...  31.2 us
    pallas_call x1, Pallas kernels, units_back(): pl.pallas_call(partial(units_back_kernel, len(hidden)), grid=(width // ti...  21.5 us
  transfers between devices with their start and end apart: 65, of which 41 were waited for; matrix products, arithmetic and copies ran while one was open for 12% of the time, Pallas kernels for 2%

profile of v1, /device:TPU:0, one launch (start us, length us, event | category | flops | bytes accessed | tf_op | source)
XLA Modules:
  0.0 902.5 jit_solution(16404030421298977482)
XLA Ops:
  12.9 3.2 collective-permute-start
  16.2 10.3 %collective-permute-done.recv = bf16[128,1280]{1,0:T(8,128)(2,1)S(1)} collective-permute-done((bf16[128,1280]{1,0:T(8,128)(2,1)S(1)}, bf16[128,1280]{1,0:T(8,128)(2,1)S(1)}, u32[]{:S(2)}, u32[]{:S(2)}) %collective-permute-start) | collective-permute-done | bytes 327712 | tf_op jit(solution)/shard_map/ppermute | solution.py:20
  26.5 5.3 project.3
  31.9 2.5 collective-permute-start.2
  34.4 17.5 %collective-permute-done.2 = bf16[128,2560]{1,0:T(8,128)(2,1)S(1)} collective-permute-done((bf16[128,2560]{1,0:T(8,128)(2,1)S(1)}, bf16[128,2560]{1,0:T(8,128)(2,1)S(1)}, u32[]{:S(2)}, u32[]{:S(2)}) %collective-permute-start.2) | collective-permute-done | bytes 655392 | tf_op jit(solution)/shard_map/ppermute | solution.py:20
  53.9 3.7 collective-permute-start.3
  64.9 8.4 recur.1
  84.8 6.9 collective-permute-start.7
  93.0 2.6 collective-permute-start.5
  99.5 5.4 project.4
  107.4 10.9 %collective-permute-done.9 = bf16[128,2560]{1,0:T(8,128)(2,1)S(1)} collective-permute-done((bf16[128,2560]{1,0:T(8,128)(2,1)S(1)}, bf16[128,2560]{1,0:T(8,128)(2,1)S(1)}, u32[]{:S(2)}, u32[]{:S(2)}) %collective-permute-start.9) | collective-permute-done | bytes 655392 | tf_op jit(solution)/shard_map/ppermute | solution.py:20
  121.5 5.5 collective-permute-done.10.recv
  127.0 5.3 project.5
  134.4 15.6 %collective-permute-done.12 = bf16[128,2560]{1,0:T(8,128)(2,1)S(1)} collective-permute-done((bf16[128,2560]{1,0:T(8,128)(2,1)S(1)}, bf16[128,2560]{1,0:T(8,128)(2,1)S(1)}, u32[]{:S(2)}, u32[]{:S(2)}) %collective-permute-start.12) | collective-permute-done | bytes 655392 | tf_op jit(solution)/shard_map/ppermute | solution.py:20
  152.1 11.9 %collective-permute-done.16.refs_5_ = bf16[128,2560]{1,0:T(8,128)(2,1)S(1)} collective-permute-done((bf16[128,2560]{1,0:T(8,128)(2,1)S(1)}, bf16[128,2560]{1,0:T(8,128)(2,1)S(1)}, u32[]{:S(2)}, u32[]{:S(2)}) %collective-permute-start.16) | collective-permute-done | bytes 655392 | tf_op jit(solution)/shard_map/ppermute | solution.py:20
  164.6 6.8 collective-permute-done.13.refs_1_
  174.3 8.4 units.2
  186.3 22.8 %units.3 = (bf16[512,1536]{1,0:T(8,128)(2,1)}, bf16[512,1536]{1,0:T(8,128)(2,1)}, bf16[512,1536]{1,0:T(8,128)(2,1)}) custom-call(bf16[128,2560]{1,0:T(8,128)(2,1)S(1)} %multiply_convert_fusion.refs_0_, bf16[128,2560]{1,0:T(8,128)(2,1)S(1)} %copy-done.27, bf16[128,2560]{1,0:T(8,128)(2,1)S(1)} %copy-done.30, bf16[128,2560]{1,0:T(8,128)(2,1)} %copy-done.92, ...), custom_call_target="tpu_custom_call" | custom-call | flops 12079595520 | bytes 23592960 | tf_op jit(solution)/shard_map/units/pallas_call | solution.py:509
  215.4 21.5 %units_back.1 = (bf16[512,2560]{1,0:T(8,128)(2,1)}, bf16[512,2560]{1,0:T(8,128)(2,1)}) custom-call(bf16[512,384]{1,0:T(8,128)(2,1)S(1)} %copy-done.64, bf16[512,1536]{1,0:T(8,128)(2,1)S(1)} %copy-done.57, bf16[512,384]{1,0:T(8,128)(2,1)S(1)} %copy-done.61, bf16[512,1536]{1,0:T(8,128)(2,1)S(1)} %copy-done.55, bf16[512,384]{1,0:T(8,128)(2,1)S(1)} %get-tuple-element.68.refs_4_, ...), custom_call_target="tpu_custom_call" | custom-call | flops 15099494400 | bytes 29491200 | tf_op jit(solution)/shard_map/units_back/pallas_call | solution.py:545
  245.5 14.2 %collective-permute-done.22 = bf16[128,2560]{1,0:T(8,128)(2,1)S(1)} collective-permute-done((bf16[128,2560]{1,0:T(8,128)(2,1)S(1)}, bf16[128,2560]{1,0:T(8,128)(2,1)S(1)}, u32[]{:S(2)}, u32[]{:S(2)}) %collective-permute-start.22) | collective-permute-done | bytes 655392 | tf_op jit(solution)/shard_map/ppermute | solution.py:20
  260.1 13.0 %collective-permute-done.20 = bf16[128,2560]{1,0:T(8,128)(2,1)S(1)} collective-permute-done((bf16[128,2560]{1,0:T(8,128)(2,1)S(1)}, bf16[128,2560]{1,0:T(8,128)(2,1)S(1)}, u32[]{:S(2)}, u32[]{:S(2)}) %collective-permute-start.20) | collective-permute-done | bytes 655392 | tf_op jit(solution)/shard_map/ppermute | solution.py:20
  276.7 14.7 %collective-permute-done.23.refs_0_ = bf16[128,2560]{1,0:T(8,128)(2,1)S(1)} collective-permute-done((bf16[128,2560]{1,0:T(8,128)(2,1)S(1)}, bf16[128,2560]{1,0:T(8,128)(2,1)S(1)}, u32[]{:S(2)}, u32[]{:S(2)}) %collective-permute-start.23) | collective-permute-done | bytes 655392 | tf_op jit(solution)/shard_map/ppermute | solution.py:20
  291.3 5.3 project_back.2
  298.2 6.7 collective-permute-done.24
  306.3 5.6 unroll.1
  315.7 2.6 collective-permute-done.25
  323.1 3.8 collective-permute-done.28
  337.0 10.2 %recur_back.1 = (f32[2,64,2560]{2,1,0:T(8,128)S(1)}, f32[2,8,2560]{2,1,0:T(8,128)S(1)}, bf16[2560,256]{1,0:T(8,128)(2,1)S(1)}, bf16[2560,256]{1,0:T(8,128)(2,1)S(1)}, f32[8,2560]{1,0:T(8,128)S(1)}) custom-call(f32[2,64,2560]{2,1,0:T(8,128)S(1)} %copy-done.41, f32[2,64,2560]{2,1,0:T(8,128)S(1)} %copy-done.43, f32[2,1,2560]{2,1,0:T(1,128)S(1)} %copy.77.carry_back, ...), custom_call_target="tpu_custom_call" | custom-call | flops 98304000 | bytes 16384000 | tf_op jit(solution)/shard_map/recur_back/pallas_call | solution.py:441
  350.1 3.0 collective-permute-done.29
  354.7 11.5 %collective-permute-done.31.refs_2_ = bf16[128,2560]{1,0:T(8,128)(2,1)S(1)} collective-permute-done((bf16[128,2560]{1,0:T(8,128)(2,1)S(1)}, bf16[128,2560]{1,0:T(8,128)(2,1)S(1)}, u32[]{:S(2)}, u32[]{:S(2)}) %collective-permute-start.31) | collective-permute-done | bytes 655392 | tf_op jit(solution)/shard_map/ppermute | solution.py:20
  366.3 8.4 collective-permute-done.30.refs_0_
  374.6 6.8 project_back.3
  383.1 5.6 collective-permute-done.32
  392.2 3.5 collective-permute-done.33
  401.6 4.4 copy.126
  406.0 3.5 select_bitcast_fusion.1
  411.8 7.2 collective-permute-done.34
  420.6 2.4 collective-permute-start.35
  423.0 26.6 %collective-permute-done.35 = bf16[4,80,640]{2,1,0:T(8,128)(2,1)S(1)} collective-permute-done((bf16[4,80,640]{2,1,0:T(8,128)(2,1)S(1)}, bf16[4,80,640]{2,1,0:T(8,128)(2,1)S(1)}, u32[]{:S(2)}, u32[]{:S(2)}) %collective-permute-start.35) | collective-permute-done | bytes 409632 | tf_op jit(solution)/shard_map/ppermute | solution.py:20
  454.8 8.0 collective-permute-done.54
  462.7 2.6 convolution_convert_fusion.3
  465.4 29.4 %collective-permute-done.55 = bf16[512,1536]{1,0:T(8,128)(2,1)} collective-permute-done((bf16[512,1536]{1,0:T(8,128)(2,1)}, bf16[512,1536]{1,0:T(8,128)(2,1)}, u32[]{:S(2)}, u32[]{:S(2)}) %collective-permute-start.55) | collective-permute-done | bytes 1572896 | tf_op jit(solution)/shard_map/ppermute | solution.py:20
  494.8 8.8 convolution_convert_fusion
  507.3 5.9 collective-permute-done.36
  521.4 5.3 collective-permute-done.43
  528.0 24.5 %collective-permute-done.46 = bf16[256,2560]{1,0:T(8,128)(2,1)S(1)} collective-permute-done((bf16[256,2560]{1,0:T(8,128)(2,1)S(1)}, bf16[256,2560]{1,0:T(8,128)(2,1)S(1)}, u32[]{:S(2)}, u32[]{:S(2)}) %collective-permute-start.46) | collective-permute-done | bytes 1310752 | tf_op jit(solution)/shard_map/ppermute | solution.py:20
  552.8 3.7 collective-permute-done.44
  559.6 24.8 %collective-permute-done.41 = bf16[256,2560]{1,0:T(8,128)(2,1)S(1)} collective-permute-done((bf16[256,2560]{1,0:T(8,128)(2,1)S(1)}, bf16[256,2560]{1,0:T(8,128)(2,1)S(1)}, u32[]{:S(2)}, u32[]{:S(2)}) %collective-permute-start.41) | collective-permute-done | bytes 1310752 | tf_op jit(solution)/shard_map/ppermute | solution.py:20
  586.4 3.0 fusion.25
  593.8 28.1 %collective-permute-done.39 = bf16[256,2560]{1,0:T(8,128)(2,1)S(1)} collective-permute-done((bf16[256,2560]{1,0:T(8,128)(2,1)S(1)}, bf16[256,2560]{1,0:T(8,128)(2,1)S(1)}, u32[]{:S(2)}, u32[]{:S(2)}) %collective-permute-start.39) | collective-permute-done | bytes 1310752 | tf_op jit(solution)/shard_map/ppermute | solution.py:20
  623.8 4.3 fusion.28
  629.5 4.6 fusion.31
  634.2 2.6 maximum_bitcast_fusion
  636.8 3.0 copy.121
  642.2 51.6 %collective-permute-done.48 = bf16[4,320,512]{2,1,0:T(8,128)(2,1)S(1)} collective-permute-done((bf16[4,320,512]{2,1,0:T(8,128)(2,1)S(1)}, bf16[4,320,512]{2,1,0:T(8,128)(2,1)S(1)}, u32[]{:S(2)}, u32[]{:S(2)}) %collective-permute-start.48) | collective-permute-done | bytes 1310752 | tf_op jit(solution)/shard_map/ppermute | solution.py:20
  694.2 7.6 collective-permute-done.49
  701.8 8.7 convolution_convert_fusion.2
  713.9 42.5 %collective-permute-done.51 = bf16[512,384]{1,0:T(8,128)(2,1)S(1)} collective-permute-done((bf16[512,384]{1,0:T(8,128)(2,1)S(1)}, bf16[512,384]{1,0:T(8,128)(2,1)S(1)}, u32[]{:S(2)}, u32[]{:S(2)}) %collective-permute-start.51) | collective-permute-done | bytes 393248 | tf_op jit(solution)/shard_map/ppermute | solution.py:20
  756.4 14.1 %convolution_convert_fusion.1 = bf16[1280,1920]{1,0:T(8,128)(2,1)} fusion(bf16[1280,1024]{1,0:T(8,128)(2,1)} %bitcast.316, bf16[512,1536]{1,0:T(8,128)(2,1)S(1)} %collective-permute-done.52, bf16[512,1536]{1,0:T(8,128)(2,1)S(1)} %copy-done.54, bf16[512,384]{1,0:T(8,128)(2,1)S(1)} %collective-permute-done.51, bf16[512,384]{1,0:T(8,128)(2,1)S(1)} %copy-done.59), kind=kOutput, calls=%fused_computation.1 | convolution fusion | flops 5051351040 | bytes 11468800 | tf_op jit(solution)/shard_map/dot_general | solution.py:56
  777.8 2.8 maximum_convert_fusion
  786.5 15.1 %reduce-scatter.17.cloned.1.call-done = bf16[320,1920]{1,0:T(8,128)(2,1)} async-done(((bf16[1280,1920]{1,0:T(8,128)(2,1)}), bf16[320,1920]{1,0:T(8,128)(2,1)}) %reduce-scatter.17.cloned.1.call-update) | async-done | bytes 1228816 | tf_op jit(solution)/shard_map/reduce_scatter | solution.py:612
  801.6 2.9 convert_element_type.200
  804.5 88.4 %reduce-scatter.19.cloned.1.call-done = bf16[320,1920]{1,0:T(8,128)(2,1)} async-done(((bf16[1280,1920]{1,0:T(8,128)(2,1)}), bf16[320,1920]{1,0:T(8,128)(2,1)}) %reduce-scatter.19.cloned.1.call-update) | async-done | bytes 1228816 | tf_op jit(solution)/shard_map/reduce_scatter | solution.py:612
  892.9 2.9 convert_element_type.202
  (454 shorter events, 158.2 us)
Async XLA Ops:
  7.2 52.1 %all-gather.2.cloned.1.call-start = ((), (), s32[]{:S(2)}) async-start(), calls=%async_computation.8 | async-start | bytes 3276800 | tf_op jit(solution)/shard_map/all_gather | solution.py:652
  7.2 19.3 %collective-permute-start.1 = (bf16[640,2560]{1,0:T(8,128)(2,1)}, bf16[640,2560]{1,0:T(8,128)(2,1)}, u32[]{:S(2)}, u32[]{:S(2)}) collective-permute-start(bf16[640,2560]{1,0:T(8,128)(2,1)} %refs_4_.1), channel_id=1, source_target_pairs={{0,1},{1,0},{2,3},{3,2},{4,5},{5,4},{6,7},{7,6},{8,9},{9,8},{10,11... | collective-permute-start | bytes 9830408 | tf_op jit(solution)/shard_map/ppermute | solution.py:20
  9.8 764.1 %reduce-scatter.9.cloned.1.call-start = ((), (), s32[]{:S(2)}) async-start(), calls=%async_computation.9 | async-start | bytes 512000 | tf_op jit(solution)/shard_map/reduce_scatter | solution.py:612
  9.8 85.9 %collective-permute-start.8 = (bf16[640,2560]{1,0:T(8,128)(2,1)}, bf16[640,2560]{1,0:T(8,128)(2,1)}, u32[]{:S(2)}, u32[]{:S(2)}) collective-permute-start(bf16[640,2560]{1,0:T(8,128)(2,1)} %refs_6_.3), channel_id=1, source_target_pairs={{0,1},{1,0},{2,3},{3,2},{4,5},{5,4},{6,7},{7,6},{8,9},{9,8},{10,11... | collective-permute-start | bytes 9830408 | tf_op jit(solution)/shard_map/ppermute | solution.py:20
  12.9 13.5 %collective-permute-start = (bf16[128,1280]{1,0:T(8,128)(2,1)S(1)}, bf16[128,1280]{1,0:T(8,128)(2,1)S(1)}, u32[]{:S(2)}, u32[]{:S(2)}) collective-permute-start(bf16[128,1280]{1,0:T(8,128)(2,1)S(1)} %pad_maximum_fusion.11), channel_id=1, source_target_pairs={{0,2},{2,0},{1,3},{3,1},{4,6},{6,4},{5,7},{7,5},{8,10},{10,8},{9,1... | collective-permute-start | bytes 983048 | tf_op jit(solution)/shard_map/ppermute | solution.py:20
  31.9 20.1 %collective-permute-start.2 = (bf16[128,2560]{1,0:T(8,128)(2,1)S(1)}, bf16[128,2560]{1,0:T(8,128)(2,1)S(1)}, u32[]{:S(2)}, u32[]{:S(2)}) collective-permute-start(bf16[128,2560]{1,0:T(8,128)(2,1)S(1)} %get-tuple-element.54), channel_id=1, source_target_pairs={{0,2},{2,0},{1,3},{3,1},{4,6},{6,4},{5,7},{7,5},{8,10},{10,8},{9,1... | collective-permute-start | bytes 1966088 | tf_op jit(solution)/shard_map/ppermute | solution.py:20
  53.9 5.3 collective-permute-start.3
  79.2 4.6 collective-permute-start.4
  81.6 39.9 %collective-permute-start.11 = (bf16[640,2560]{1,0:T(8,128)(2,1)S(1)}, bf16[640,2560]{1,0:T(8,128)(2,1)}, u32[]{:S(2)}, u32[]{:S(2)}) collective-permute-start(bf16[640,2560]{1,0:T(8,128)(2,1)S(1)} %copy-done.1), channel_id=1, source_target_pairs={{0,1},{1,0},{2,3},{3,2},{4,5},{5,4},{6,7},{7,6},{8,9},{9,8},{10,11... | collective-permute-start | bytes 9830408 | tf_op jit(solution)/shard_map/ppermute | solution.py:20
  84.8 21.7 %collective-permute-start.7 = (f32[4,2560]{1,0:T(4,128)S(1)}, f32[4,2560]{1,0:T(4,128)S(1)}, u32[]{:S(2)}, u32[]{:S(2)}) collective-permute-start(f32[4,2560]{1,0:T(4,128)S(1)} %pad_maximum_fusion.19), channel_id=1, source_target_pairs={{0,24},{1,25},{2,26},{3,27},{4,28},{5,29},{6,30},{7,31}} | collective-permute-start | bytes 122888 | tf_op jit(solution)/shard_map/ppermute | solution.py:26
  91.7 14.8 %collective-permute-start.6 = (f32[4,2560]{1,0:T(4,128)S(1)}, f32[4,2560]{1,0:T(4,128)S(1)}, u32[]{:S(2)}, u32[]{:S(2)}) collective-permute-start(f32[4,2560]{1,0:T(4,128)S(1)} %pad_maximum_fusion.19), channel_id=1, source_target_pairs={{0,16},{8,24},{1,17},{9,25},{2,18},{10,26},{3,19},{11,27},{4,20},{... | collective-permute-start | bytes 122888 | tf_op jit(solution)/shard_map/ppermute | solution.py:26
  93.0 13.5 %collective-permute-start.5 = (f32[4,2560]{1,0:T(4,128)S(1)}, f32[4,2560]{1,0:T(4,128)S(1)}, u32[]{:S(2)}, u32[]{:S(2)}) collective-permute-start(f32[4,2560]{1,0:T(4,128)S(1)} %pad_maximum_fusion.19), channel_id=1, source_target_pairs={{0,8},{8,16},{16,24},{1,9},{9,17},{17,25},{2,10},{10,18},{18,26},{... | collective-permute-start | bytes 122888 | tf_op jit(solution)/shard_map/ppermute | solution.py:26
  105.0 13.4 %collective-permute-start.9 = (bf16[128,2560]{1,0:T(8,128)(2,1)S(1)}, bf16[128,2560]{1,0:T(8,128)(2,1)S(1)}, u32[]{:S(2)}, u32[]{:S(2)}) collective-permute-start(bf16[128,2560]{1,0:T(8,128)(2,1)S(1)} %get-tuple-element.60), channel_id=1, source_target_pairs={{0,2},{2,0},{1,3},{3,1},{4,6},{6,4},{5,7},{7,5},{8,10},{10,8},{9,1... | collective-permute-start | bytes 1966088 | tf_op jit(solution)/shard_map/ppermute | solution.py:20
  119.9 7.1 collective-permute-start.10
  132.3 17.7 %collective-permute-start.12 = (bf16[128,2560]{1,0:T(8,128)(2,1)S(1)}, bf16[128,2560]{1,0:T(8,128)(2,1)S(1)}, u32[]{:S(2)}, u32[]{:S(2)}) collective-permute-start(bf16[128,2560]{1,0:T(8,128)(2,1)S(1)} %get-tuple-element.62), channel_id=1, source_target_pairs={{0,2},{2,0},{1,3},{3,1},{4,6},{6,4},{5,7},{7,5},{8,10},{10,8},{9,1... | collective-permute-start | bytes 1966088 | tf_op jit(solution)/shard_map/ppermute | solution.py:20
  133.8 30.2 %collective-permute-start.16 = (bf16[128,2560]{1,0:T(8,128)(2,1)S(1)}, bf16[128,2560]{1,0:T(8,128)(2,1)S(1)}, u32[]{:S(2)}, u32[]{:S(2)}) collective-permute-start(bf16[128,2560]{1,0:T(8,128)(2,1)S(1)} %bitcast.304), channel_id=1, source_target_pairs={{0,2},{2,0},{1,3},{3,1},{4,6},{6,4},{5,7},{7,5},{8,10},{10,8},{9,1... | collective-permute-start | bytes 1966088 | tf_op jit(solution)/shard_map/ppermute | solution.py:20
  150.6 20.7 %collective-permute-start.13 = (bf16[128,2560]{1,0:T(8,128)(2,1)S(1)}, bf16[128,2560]{1,0:T(8,128)(2,1)S(1)}, u32[]{:S(2)}, u32[]{:S(2)}) collective-permute-start(bf16[128,2560]{1,0:T(8,128)(2,1)S(1)} %multiply_convert_fusion.refs_0_), channel_id=1, source_target_pairs={{0,2},{2,0},{1,3},{3,1},{4,6},{6,4},{5,7},{7,5},{8,10},{10,8},{9,1... | collective-permute-start | bytes 1966088 | tf_op jit(solution)/shard_map/ppermute | solution.py:20
  152.1 19.2 %collective-permute-start.17 = (bf16[128,2560]{1,0:T(8,128)(2,1)S(1)}, bf16[128,2560]{1,0:T(8,128)(2,1)S(1)}, u32[]{:S(2)}, u32[]{:S(2)}) collective-permute-start(bf16[128,2560]{1,0:T(8,128)(2,1)S(1)} %bitcast.305), channel_id=1, source_target_pairs={{0,1},{1,0},{2,3},{3,2},{4,5},{5,4},{6,7},{7,6},{8,9},{9,8},{10,11... | collective-permute-start | bytes 1966088 | tf_op jit(solution)/shard_map/ppermute | solution.py:20
  164.0 7.3 collective-permute-start.18
  164.1 7.3 collective-permute-start.14
  171.3 2.1 collective-permute-start.15
  238.5 3.1 collective-permute-start.21
  239.1 4.5 collective-permute-start.19
  242.0 17.6 %collective-permute-start.22 = (bf16[128,2560]{1,0:T(8,128)(2,1)S(1)}, bf16[128,2560]{1,0:T(8,128)(2,1)S(1)}, u32[]{:S(2)}, u32[]{:S(2)}) collective-permute-start(bf16[128,2560]{1,0:T(8,128)(2,1)S(1)} %slice.878), channel_id=1, source_target_pairs={{0,2},{2,0},{1,3},{3,1},{4,6},{6,4},{5,7},{7,5},{8,10},{10,8},{9,1... | collective-permute-start | bytes 1966088 | tf_op jit(solution)/shard_map/ppermute | solution.py:20
  244.1 29.0 %collective-permute-start.20 = (bf16[128,2560]{1,0:T(8,128)(2,1)S(1)}, bf16[128,2560]{1,0:T(8,128)(2,1)S(1)}, u32[]{:S(2)}, u32[]{:S(2)}) collective-permute-start(bf16[128,2560]{1,0:T(8,128)(2,1)S(1)} %slice.879), channel_id=1, source_target_pairs={{0,2},{2,0},{1,3},{3,1},{4,6},{6,4},{5,7},{7,5},{8,10},{10,8},{9,1... | collective-permute-start | bytes 1966088 | tf_op jit(solution)/shard_map/ppermute | solution.py:20
  275.2 16.2 %collective-permute-start.23 = (bf16[128,2560]{1,0:T(8,128)(2,1)S(1)}, bf16[128,2560]{1,0:T(8,128)(2,1)S(1)}, u32[]{:S(2)}, u32[]{:S(2)}) collective-permute-start(bf16[128,2560]{1,0:T(8,128)(2,1)S(1)} %get-tuple-element.133.refs_1_), channel_id=1, source_target_pairs={{0,2},{2,0},{1,3},{3,1},{4,6},{6,4},{5,7},{7,5},{8,10},{10,8},{9,1... | collective-permute-start | bytes 1966088 | tf_op jit(solution)/shard_map/ppermute | solution.py:20
  296.6 8.3 collective-permute-start.24
  314.0 4.3 collective-permute-start.25
  319.2 7.7 collective-permute-start.28
  320.5 6.8 collective-permute-start.27
  321.8 6.0 collective-permute-start.26
  347.2 5.9 collective-permute-start.29
  348.5 17.7 %collective-permute-start.31 = (bf16[128,2560]{1,0:T(8,128)(2,1)S(1)}, bf16[128,2560]{1,0:T(8,128)(2,1)S(1)}, u32[]{:S(2)}, u32[]{:S(2)}) collective-permute-start(bf16[128,2560]{1,0:T(8,128)(2,1)S(1)} %bitcast.281), channel_id=1, source_target_pairs={{0,2},{2,0},{1,3},{3,1},{4,6},{6,4},{5,7},{7,5},{8,10},{10,8},{9,1... | collective-permute-start | bytes 1966088 | tf_op jit(solution)/shard_map/ppermute | solution.py:20
  353.2 21.5 %collective-permute-start.30 = (bf16[128,2560]{1,0:T(8,128)(2,1)S(1)}, bf16[128,2560]{1,0:T(8,128)(2,1)S(1)}, u32[]{:S(2)}, u32[]{:S(2)}) collective-permute-start(bf16[128,2560]{1,0:T(8,128)(2,1)S(1)} %bitcast.276), channel_id=1, source_target_pairs={{0,2},{2,0},{1,3},{3,1},{4,6},{6,4},{5,7},{7,5},{8,10},{10,8},{9,1... | collective-permute-start | bytes 1966088 | tf_op jit(solution)/shard_map/ppermute | solution.py:20
  381.5 7.1 collective-permute-start.32
  392.1 3.6 collective-permute-start.33
  398.5 20.6 %collective-permute-start.34 = (bf16[4,2,80,640]{3,2,1,0:T(8,128)(2,1)}, bf16[4,2,80,640]{3,2,1,0:T(8,128)(2,1)}, u32[]{:S(2)}, u32[]{:S(2)}) collective-permute-start(bf16[4,2,80,640]{3,2,1,0:T(8,128)(2,1)} %fusion.71), channel_id=1, source_target_pairs={{0,2},{2,0},{1,3},{3,1},{4,6},{6,4},{5,7},{7,5},{8,10},{10,8},{9,1... | collective-permute-start | bytes 2457608 | tf_op jit(solution)/shard_map/ppermute | solution.py:20
  409.5 43.2 %collective-permute-start.53 = (bf16[4,320,512]{2,1,0:T(8,128)(2,1)}, bf16[4,320,512]{2,1,0:T(8,128)(2,1)}, u32[]{:S(2)}, u32[]{:S(2)}) collective-permute-start(bf16[4,320,512]{2,1,0:T(8,128)(2,1)} %get-tuple-element.138), channel_id=1, source_target_pairs={{0,4},{4,0},{1,5},{5,1},{2,6},{6,2},{3,7},{7,3},{8,12},{12,8},{9,1... | collective-permute-start | bytes 3932168 | tf_op jit(solution)/shard_map/ppermute | solution.py:20
  420.6 29.0 %collective-permute-start.35 = (bf16[4,80,640]{2,1,0:T(8,128)(2,1)S(1)}, bf16[4,80,640]{2,1,0:T(8,128)(2,1)S(1)}, u32[]{:S(2)}, u32[]{:S(2)}) collective-permute-start(bf16[4,80,640]{2,1,0:T(8,128)(2,1)S(1)} %fusion.77), channel_id=1, source_target_pairs={{0,4},{4,0},{1,5},{5,1},{2,6},{6,2},{3,7},{7,3},{8,12},{12,8},{9,1... | collective-permute-start | bytes 1228808 | tf_op jit(solution)/shard_map/ppermute | solution.py:20
  450.6 327.2 %reduce-scatter.21.cloned.1.call-start = ((), (), s32[]{:S(2)}) async-start(), calls=%async_computation.15 | async-start | bytes 1228800 | tf_op jit(solution)/shard_map/reduce_scatter | solution.py:612
  450.6 12.1 %collective-permute-start.54 = (bf16[512,384]{1,0:T(8,128)(2,1)S(1)}, bf16[512,384]{1,0:T(8,128)(2,1)S(1)}, u32[]{:S(2)}, u32[]{:S(2)}) collective-permute-start(bf16[512,384]{1,0:T(8,128)(2,1)S(1)} %copy-done.65), channel_id=1, source_target_pairs={{0,4},{4,0},{1,5},{5,1},{2,6},{6,2},{3,7},{7,3},{8,12},{12,8},{9,1... | collective-permute-start | bytes 1179656 | tf_op jit(solution)/shard_map/ppermute | solution.py:20
  452.4 42.4 %collective-permute-start.55 = (bf16[512,1536]{1,0:T(8,128)(2,1)}, bf16[512,1536]{1,0:T(8,128)(2,1)}, u32[]{:S(2)}, u32[]{:S(2)}) collective-permute-start(bf16[512,1536]{1,0:T(8,128)(2,1)} %get-tuple-element.65.refs_1_), channel_id=1, source_target_pairs={{0,4},{4,0},{1,5},{5,1},{2,6},{6,2},{3,7},{7,3},{8,12},{12,8},{9,1... | collective-permute-start | bytes 4718600 | tf_op jit(solution)/shard_map/ppermute | solution.py:20
  465.3 312.5 %reduce-scatter.23.cloned.1.call-start = ((), (), s32[]{:S(2)}) async-start(), calls=%async_computation.16 | async-start | bytes 4915200 | tf_op jit(solution)/shard_map/reduce_scatter | solution.py:612
  503.7 277.0 %reduce-scatter.15.cloned.1.call-start = ((), (), s32[]{:S(2)}) async-start(), calls=%async_computation.12 | async-start | bytes 2048000 | tf_op jit(solution)/shard_map/reduce_scatter | solution.py:612
  505.1 8.1 collective-permute-start.36
  514.0 75.5 %collective-permute-start.37 = (bf16[2,4,2,80,128]{4,3,2,1,0:T(8,128)(2,1)}, bf16[2,4,2,80,128]{4,3,2,1,0:T(8,128)(2,1)}, u32[]{:S(2)}, u32[]{:S(2)}) collective-permute-start(bf16[2,4,2,80,128]{4,3,2,1,0:T(8,128)(2,1)} %pad_maximum_fusion.15), channel_id=1, source_target_pairs={{0,4},{4,0},{1,5},{5,1},{2,6},{6,2},{3,7},{7,3},{8,12},{12,8},{9,1... | collective-permute-start | bytes 983048 | tf_op jit(solution)/shard_map/ppermute | solution.py:20
  518.5 34.0 %collective-permute-start.46 = (bf16[256,2560]{1,0:T(8,128)(2,1)S(1)}, bf16[256,2560]{1,0:T(8,128)(2,1)S(1)}, u32[]{:S(2)}, u32[]{:S(2)}) collective-permute-start(bf16[256,2560]{1,0:T(8,128)(2,1)S(1)} %pad_maximum_fusion.9), channel_id=1, source_target_pairs={{0,4},{4,0},{1,5},{5,1},{2,6},{6,2},{3,7},{7,3},{8,12},{12,8},{9,1... | collective-permute-start | bytes 3932168 | tf_op jit(solution)/shard_map/ppermute | solution.py:20
  519.5 7.1 collective-permute-start.43
  526.7 29.7 %collective-permute-start.44 = (bf16[2,4,2,80,128]{4,3,1,2,0:T(8,128)(2,1)S(1)}, bf16[2,4,2,80,128]{4,3,1,2,0:T(8,128)(2,1)S(1)}, u32[]{:S(2)}, u32[]{:S(2)}) collective-permute-start(bf16[2,4,2,80,128]{4,3,1,2,0:T(8,128)(2,1)S(1)} %pad_maximum_fusion.17), channel_id=1, source_target_pairs={{0,4},{4,0},{1,5},{5,1},{2,6},{6,2},{3,7},{7,3},{8,12},{12,8},{9,1... | collective-permute-start | bytes 983048 | tf_op jit(solution)/shard_map/ppermute | solution.py:20
  552.7 33.7 %collective-permute-start.47 = (bf16[512,2560]{1,0:T(8,128)(2,1)S(1)}, bf16[512,2560]{1,0:T(8,128)(2,1)S(1)}, u32[]{:S(2)}, u32[]{:S(2)}) collective-permute-start(bf16[512,2560]{1,0:T(8,128)(2,1)S(1)} %pad_maximum_fusion.2), channel_id=1, source_target_pairs={{0,1},{1,0},{2,3},{3,2},{4,5},{5,4},{6,7},{7,6},{8,9},{9,8},{10,11... | collective-permute-start | bytes 7864328 | tf_op jit(solution)/shard_map/ppermute | solution.py:20
  556.6 27.9 %collective-permute-start.41 = (bf16[256,2560]{1,0:T(8,128)(2,1)S(1)}, bf16[256,2560]{1,0:T(8,128)(2,1)S(1)}, u32[]{:S(2)}, u32[]{:S(2)}) collective-permute-start(bf16[256,2560]{1,0:T(8,128)(2,1)S(1)} %pad_maximum_fusion.8), channel_id=1, source_target_pairs={{0,4},{4,0},{1,5},{5,1},{2,6},{6,2},{3,7},{7,3},{8,12},{12,8},{9,1... | collective-permute-start | bytes 3932168 | tf_op jit(solution)/shard_map/ppermute | solution.py:20
  557.7 1.7 collective-permute-start.45
  586.4 37.4 %collective-permute-start.42 = (bf16[512,2560]{1,0:T(8,128)(2,1)}, bf16[512,2560]{1,0:T(8,128)(2,1)}, u32[]{:S(2)}, u32[]{:S(2)}) collective-permute-start(bf16[512,2560]{1,0:T(8,128)(2,1)} %pad_maximum_fusion.1), channel_id=1, source_target_pairs={{0,1},{1,0},{2,3},{3,2},{4,5},{5,4},{6,7},{7,6},{8,9},{9,8},{10,11... | collective-permute-start | bytes 7864328 | tf_op jit(solution)/shard_map/ppermute | solution.py:20
  589.4 193.2 %reduce-scatter.13.cloned.1.call-start = ((), (), s32[]{:S(2)}) async-start(), calls=%async_computation.11 | async-start | bytes 2048000 | tf_op jit(solution)/shard_map/reduce_scatter | solution.py:612
  590.6 31.3 %collective-permute-start.39 = (bf16[256,2560]{1,0:T(8,128)(2,1)S(1)}, bf16[256,2560]{1,0:T(8,128)(2,1)S(1)}, u32[]{:S(2)}, u32[]{:S(2)}) collective-permute-start(bf16[256,2560]{1,0:T(8,128)(2,1)S(1)} %pad_maximum_fusion.7), channel_id=1, source_target_pairs={{0,4},{4,0},{1,5},{5,1},{2,6},{6,2},{3,7},{7,3},{8,12},{12,8},{9,1... | collective-permute-start | bytes 3932168 | tf_op jit(solution)/shard_map/ppermute | solution.py:20
  623.8 5.7 collective-permute-start.40
  628.2 156.4 %reduce-scatter.11.cloned.1.call-start = ((), (), s32[]{:S(2)}) async-start(), calls=%async_computation.10 | async-start | bytes 2048000 | tf_op jit(solution)/shard_map/reduce_scatter | solution.py:612
  628.2 73.6 %collective-permute-start.50 = (bf16[512,1536]{1,0:T(8,128)(2,1)}, bf16[512,1536]{1,0:T(8,128)(2,1)}, u32[]{:S(2)}, u32[]{:S(2)}) collective-permute-start(bf16[512,1536]{1,0:T(8,128)(2,1)} %get-tuple-element.67.refs_3_), channel_id=1, source_target_pairs={{0,4},{4,0},{1,5},{5,1},{2,6},{6,2},{3,7},{7,3},{8,12},{12,8},{9,1... | collective-permute-start | bytes 4718600 | tf_op jit(solution)/shard_map/ppermute | solution.py:20
  634.1 167.5 %reduce-scatter.17.cloned.1.call-start = ((), (), s32[]{:S(2)}) async-start(), calls=%async_computation.13 | async-start | bytes 6144000 | tf_op jit(solution)/shard_map/reduce_scatter | solution.py:612
  640.0 53.8 %collective-permute-start.48 = (bf16[4,320,512]{2,1,0:T(8,128)(2,1)S(1)}, bf16[4,320,512]{2,1,0:T(8,128)(2,1)S(1)}, u32[]{:S(2)}, u32[]{:S(2)}) collective-permute-start(bf16[4,320,512]{2,1,0:T(8,128)(2,1)S(1)} %fusion.56), channel_id=1, source_target_pairs={{0,4},{4,0},{1,5},{5,1},{2,6},{6,2},{3,7},{7,3},{8,12},{12,8},{9,1... | collective-permute-start | bytes 3932168 | tf_op jit(solution)/shard_map/ppermute | solution.py:20
  641.0 60.8 %collective-permute-start.49 = (bf16[512,384]{1,0:T(8,128)(2,1)S(1)}, bf16[512,384]{1,0:T(8,128)(2,1)S(1)}, u32[]{:S(2)}, u32[]{:S(2)}) collective-permute-start(bf16[512,384]{1,0:T(8,128)(2,1)S(1)} %copy-done.62), channel_id=1, source_target_pairs={{0,4},{4,0},{1,5},{5,1},{2,6},{6,2},{3,7},{7,3},{8,12},{12,8},{9,1... | collective-permute-start | bytes 1179656 | tf_op jit(solution)/shard_map/ppermute | solution.py:20
  710.5 182.4 %reduce-scatter.19.cloned.1.call-start = ((), (), s32[]{:S(2)}) async-start(), calls=%async_computation.14 | async-start | bytes 6144000 | tf_op jit(solution)/shard_map/reduce_scatter | solution.py:612
  711.9 44.5 %collective-permute-start.52 = (bf16[512,1536]{1,0:T(8,128)(2,1)S(1)}, bf16[512,1536]{1,0:T(8,128)(2,1)S(1)}, u32[]{:S(2)}, u32[]{:S(2)}) collective-permute-start(bf16[512,1536]{1,0:T(8,128)(2,1)S(1)} %copy-done.54), channel_id=1, source_target_pairs={{0,4},{4,0},{1,5},{5,1},{2,6},{6,2},{3,7},{7,3},{8,12},{12,8},{9,1... | collective-permute-start | bytes 4718600 | tf_op jit(solution)/shard_map/ppermute | solution.py:20
  713.0 43.4 %collective-permute-start.51 = (bf16[512,384]{1,0:T(8,128)(2,1)S(1)}, bf16[512,384]{1,0:T(8,128)(2,1)S(1)}, u32[]{:S(2)}, u32[]{:S(2)}) collective-permute-start(bf16[512,384]{1,0:T(8,128)(2,1)S(1)} %copy-done.59), channel_id=1, source_target_pairs={{0,4},{4,0},{1,5},{5,1},{2,6},{6,2},{3,7},{7,3},{8,12},{12,8},{9,1... | collective-permute-start | bytes 1179656 | tf_op jit(solution)/shard_map/ppermute | solution.py:20
  (115 other events, 1117.2 us)
Sparse Core Ops, SparseCore 0:
  10.2 33.7 all-gather.1
  450.7 22.5 reduce-scatter.8
  475.7 24.4 reduce-scatter.20
  503.8 74.4 reduce-scatter.22
  589.5 38.9 reduce-scatter.14
  631.3 35.8 reduce-scatter.12
  670.1 35.2 reduce-scatter.10
  710.6 90.9 reduce-scatter.16
  803.9 88.9 reduce-scatter.18

commit v2 on v1

v2 whole, which is shorter than its diff:
```python
from functools import partial

import jax
import jax.numpy as jnp
from jax import lax
from jax.experimental import pallas as pl
from jax.experimental.pallas import tpu as pltpu
from jax.sharding import Mesh
from jax.sharding import PartitionSpec as P

SZ, SY, WX, WC = ("sz", "sy", "wx", "wc")
F32, BF16 = (jnp.float32, jnp.bfloat16)
HALO = 8
ROOT_2_PI = 0.7978845608028654
CUBIC = 0.044715
VMEM_GRANT = 58 << 20
COST_SHARE = 0.02
HEADS_EACH = 2


def swap(value, axis):
    return lax.ppermute(value, axis, [(0, 1), (1, 0)])


def shift(value, axis, steps):
    count = lax.axis_size(axis)
    initial, last = (max(0, -steps), min(count, count - steps))
    return lax.ppermute(value, axis, [(source, source + steps) for source in range(initial, last)])


def around(value, steps):
    count = lax.axis_size(SZ)
    return lax.ppermute(value, SZ, [((to + steps) % count, to) for to in range(count)])


def partner_far(value):
    count = lax.axis_size(SZ)
    return lax.ppermute(value, SZ, [(source, source ^ 1) for source in range(count)])


def along_seq(value, steps):
    count = lax.axis_size(SZ) * lax.axis_size(SY)
    initial, last = (max(0, -steps), min(count, count - steps))
    return lax.ppermute(
        value, (SZ, SY), [(source, source + steps) for source in range(initial, last)]
    )


def pick(bit, zero, one):
    return jnp.where(bit == 0, zero, one)


def after(value, *others):
    return lax.optimization_barrier((value, *others))[0]


def tie(*values):
    return lax.optimization_barrier(values)


class Line:
    def __init__(self):
        self.last = None

    def __call__(self, *values):
        if self.last is None:
            return values
        return lax.optimization_barrier((*values, self.last))[:-1]

    def mark(self, value):
        self.last = value
        return value


def gelu_pair(value):
    square = value * value
    tanh = jnp.tanh(ROOT_2_PI * value * (1.0 + CUBIC * square))
    half = 0.5 * (1.0 + tanh)
    slope = half + 0.5 * value * (1.0 - tanh * tanh) * (
        ROOT_2_PI * (1.0 + 3.0 * CUBIC * square)
    )
    return value * half, slope


def dot(left, right):
    return jnp.dot(left, right, preferred_element_type=F32)


def dot_nt(left, right):
    return lax.dot_general(left, right, (((1,), (1,)), ((), ())), preferred_element_type=F32)


def dot_tn(left, right):
    return lax.dot_general(left, right, (((0,), (0,)), ((), ())), preferred_element_type=F32)


def params():
    return pltpu.CompilerParams(
        dimension_semantics=("arbitrary",), vmem_limit_bytes=VMEM_GRANT
    )


def cost(flops, nbytes):
    return pl.CostEstimate(
        flops=int(flops * COST_SHARE), bytes_accessed=int(nbytes * COST_SHARE), transcendentals=0
    )


def split_columns(value, wx, wc):
    quarter = value.shape[-1] // 4
    parts = [value[..., i * quarter : (i + 1) * quarter] for i in range(4)]
    near = [pick(wx, parts[0], parts[2]), pick(wx, parts[1], parts[3])]
    far = [pick(wx, parts[2], parts[0]), pick(wx, parts[3], parts[1])]
    keep = jnp.concatenate([pick(wc, near[0], near[1]), pick(wc, near[1], near[0])], axis=-1)
    send = jnp.concatenate([pick(wc, far[0], far[1]), pick(wc, far[1], far[0])], axis=-1)
    return keep, send


def join_columns(near, far, wx, wc):
    near = [pick(wc, near[0], near[1]), pick(wc, near[1], near[0])]
    far = [pick(wc, far[0], far[1]), pick(wc, far[1], far[0])]
    return jnp.concatenate(
        [
            pick(wx, near[0], far[0]),
            pick(wx, near[1], far[1]),
            pick(wx, far[0], near[0]),
            pick(wx, far[1], near[1]),
        ],
        axis=-1,
    )


def project(recv, keep, w_own, w_oth):
    rows = recv.shape[0]
    left = jnp.concatenate([recv, keep], axis=0)
    total = dot(left, jnp.concatenate([w_own, w_oth], axis=0))
    return total[:rows].astype(BF16), total[rows:]


def project_back(terms):
    rows = terms[0][0].shape[0]
    total = 0.0
    for recv, own, w_own, w_oth in terms:
        left = jnp.concatenate([recv, own], axis=0)
        total = total + dot_nt(left, jnp.concatenate([w_own, w_oth], axis=0))
    half = total.shape[1] // 2
    total = jnp.stack([total[:, :half], total[:, half:]])
    return total[:, :rows].astype(BF16), total[:, rows:]


def less_one_exp(value):
    series = 1.0
    for n in (9, 8, 7, 6, 5, 4, 3, 2):
        series = 1.0 + value * (1.0 / n) * series
    return jnp.where(value > -0.5, -value * series, 1.0 - jnp.exp(value))


def shifted_down(value, steps, fill):
    edge = jnp.full((value.shape[0], steps, value.shape[2]), fill, F32)
    return jnp.concatenate([edge, value[:, : value.shape[1] - steps]], axis=1)


def shifted_up(value, steps, fill):
    edge = jnp.full((value.shape[0], steps, value.shape[2]), fill, F32)
    return jnp.concatenate([value[:, steps:], edge], axis=1)


def scan_rows(decay, driven, mover):
    steps = 1
    while steps < decay.shape[1]:
        driven = driven + decay * mover(driven, steps, 0.0)
        decay = decay * mover(decay, steps, 1.0)
        steps *= 2
    return decay, driven


def tap_mask(places, offset):
    return (places >= offset).astype(F32)


def by_head(flat, gate, product):
    head = gate.shape[1]
    spans = [slice(i, i + head) for i in range(0, flat.shape[1], head)]
    return jnp.concatenate([product(flat[:, s], gate[s]) for s in spans], axis=1)


def recur_kernel(
    own,
    recv,
    halo,
    places,
    conv_w,
    conv_b,
    gate_a,
    gate_i,
    bias_a,
    bias_i,
    decay_log,
    branch_out,
    conv_out,
    rec_out,
    in_out,
    run_out,
    state_out,
    ends_out,
):
    batches, length, width = own.shape
    branch = (own[...] + recv[...].astype(F32)).astype(BF16)
    branch_out[...] = branch
    extended = jnp.concatenate([halo[...], branch.astype(F32)], axis=1)
    spot = places[...]
    total = jnp.zeros((batches, length, width), F32) + conv_b[...][None]
    for offset in range(conv_w.shape[0]):
        moved = extended[:, HALO - offset : HALO - offset + length]
        total = total + conv_w[offset : offset + 1][None] * moved * tap_mask(spot, offset)
    conv = total.astype(BF16)
    conv_out[...] = conv
    flat = conv.reshape(batches * length, width)
    shape = (batches, length, width)
    gate_rec = jax.nn.sigmoid(by_head(flat, gate_a, dot) + bias_a[...]).reshape(shape)
    gate_in = jax.nn.sigmoid(by_head(flat, gate_i, dot) + bias_i[...]).reshape(shape)
    rec_out[...] = gate_rec
    in_out[...] = gate_in
    log_a = -8.0 * gate_rec * jnp.exp(decay_log[...])[None]
    alive = tap_mask(spot, 1)
    root = jnp.sqrt(less_one_exp(2.0 * log_a))
    multiplier = alive * root + (1.0 - alive)
    decay = jnp.exp(log_a) * alive
    driven = conv.astype(F32) * gate_in * multiplier
    running, state = scan_rows(decay, driven, shifted_down)
    run_out[...] = running
    state_out[...] = state
    for b in range(batches):
        ends_out[b : b + 1] = running[b, length - 1 :]
        ends_out[batches + b : batches + b + 1] = state[b, length - 1 :]


def head_specs(batches, length, head, taps, group=1):
    head = head * group
    tokens = pl.BlockSpec((batches, length, head), lambda h: (0, 0, h))
    edge = pl.BlockSpec((batches, HALO, head), lambda h: (0, 0, h))
    place = pl.BlockSpec((batches, length, 1), lambda h: (0, 0, 0))
    row = pl.BlockSpec((1, head), lambda h: (0, h))
    tap = pl.BlockSpec((taps, head), lambda h: (0, h))
    gates = [
        pl.BlockSpec((head, head // group), lambda h: (h, 0)),
        pl.BlockSpec((head, head // group), lambda h: (h, 1)),
    ]
    ends = pl.BlockSpec((2 * batches, head), lambda h: (0, h))
    carry = pl.BlockSpec((batches, 1, head), lambda h: (0, 0, h))
    return tokens, edge, place, row, tap, gates, ends, carry


def recur(own, recv, halo, places, conv_w, conv_b, gates, bias_a, bias_i, decay_log):
    batches, length, features = own.shape
    head = gates.shape[1] // 2
    tokens, edge, place, row, tap, gate, ends, _ = head_specs(
        batches, length, head, conv_w.shape[0], HEADS_EACH
    )
    full = lambda dtype: jax.ShapeDtypeStruct((batches, length, features), dtype)
    return pl.pallas_call(
        recur_kernel,
        grid=(features // (head * HEADS_EACH),),
        in_specs=[tokens, tokens, edge, place, tap, row, *gate, row, row, row],
        out_specs=[tokens] * 6 + [ends],
        out_shape=[full(BF16), full(BF16)]
        + [full(F32)] * 4
        + [jax.ShapeDtypeStruct((2 * batches, features), F32)],
        compiler_params=params(),
        cost_estimate=cost(200 * batches * length * features, 40 * batches * length * features),
        name="recur",
    )(own, recv, halo, places, conv_w, conv_b, gates, gates, bias_a, bias_i, decay_log)


def unroll_kernel(
    mixed_grad,
    own_y,
    recv_y,
    running,
    local_state,
    carry,
    gate_rec,
    places,
    decay_log,
    pre_out,
    behind_out,
    local_out,
    ends_out,
):
    batches, length, _ = mixed_grad.shape
    pulled = mixed_grad[...].astype(F32)
    branch_y, slope = gelu_pair(own_y[...] + recv_y[...].astype(F32))
    state = local_state[...] + running[...] * carry[...]
    pre_out[...] = (pulled * state * slope).astype(BF16)
    log_a = -8.0 * gate_rec[...] * jnp.exp(decay_log[...])[None]
    decay = jnp.exp(log_a) * tap_mask(places[...], 1)
    following = shifted_up(decay, 1, 1.0)
    behind, local = scan_rows(following, pulled * branch_y, shifted_up)
    behind_out[...] = behind
    local_out[...] = local
    for b in range(batches):
        ends_out[b : b + 1] = running[b, length - 1 :, :]
        ends_out[batches + b : batches + b + 1] = decay[b, :1] * local[b, :1]


def unroll(mixed_grad, own_y, recv_y, running, local_state, carry, gate_rec, places, decay_log, head):
    batches, length, features = mixed_grad.shape
    tokens, _, place, row, _, _, ends, carried = head_specs(batches, length, head, 1, HEADS_EACH)
    full = lambda dtype: jax.ShapeDtypeStruct((batches, length, features), dtype)
    return pl.pallas_call(
        unroll_kernel,
        grid=(features // (head * HEADS_EACH),),
        in_specs=[tokens] * 5 + [carried, tokens, place, row],
        out_specs=[tokens] * 3 + [ends],
        out_shape=[full(BF16), full(F32), full(F32)]
        + [jax.ShapeDtypeStruct((2 * batches, features), F32)],
        compiler_params=params(),
        cost_estimate=cost(200 * batches * length * features, 40 * batches * length * features),
        name="unroll",
    )(mixed_grad, own_y, recv_y, running, local_state, carry, gate_rec, places, decay_log)


def recur_back_kernel(
    behind,
    local_grad,
    carry_back,
    running,
    local_state,
    carry,
    gate_rec,
    gate_in,
    conv,
    branch,
    halo,
    places,
    conv_w,
    gate_a,
    gate_i,
    decay_log,
    spread_out,
    earlier_out,
    wa_out,
    wi_out,
    sums_out,
):
    batches, length, width = behind.shape
    shape = (batches, length, width)
    rows = batches * length
    spot = places[...]
    alive = tap_mask(spot, 1)
    rate = jnp.exp(decay_log[...])[None]
    rec, inner = gate_rec[...], gate_in[...]
    log_a = -8.0 * rec * rate
    raw = jnp.exp(log_a)
    root = jnp.sqrt(less_one_exp(2.0 * log_a))
    multiplier = alive * root + (1.0 - alive)
    conv_low = conv[...]
    conv_full = conv_low.astype(F32)
    grad_state = local_grad[...] + behind[...] * carry_back[...]
    state = local_state[...] + running[...] * carry[...]
    before = jnp.concatenate([carry[...], state[:, : length - 1]], axis=1)
    scaled = grad_state * conv_full * inner
    grad_log = alive * raw * (grad_state * before - scaled * raw / root)
    grad_a = grad_log * (-8.0 * rate) * rec * (1.0 - rec)
    grad_i = scaled * multiplier * (1.0 - inner)
    low_a = grad_a.astype(BF16).reshape(rows, width)
    low_i = grad_i.astype(BF16).reshape(rows, width)
    pulled = grad_state * inner * multiplier
    pulled = pulled + (
        by_head(low_a, gate_a, dot_nt) + by_head(low_i, gate_i, dot_nt)
    ).reshape(shape)
    pulled = pulled.astype(BF16).astype(F32)
    flat = conv_low.reshape(rows, width)
    head = gate_a.shape[1]
    for i in range(0, width, head):
        span = slice(i, i + head)
        wa_out[span] = dot_tn(flat[:, span], low_a[:, span]).astype(BF16)
        wi_out[span] = dot_tn(flat[:, span], low_i[:, span]).astype(BF16)
    extended = jnp.concatenate([halo[...], branch[...].astype(F32)], axis=1)
    taps = conv_w.shape[0]
    spread = jnp.zeros((batches, length + HALO, width), F32)
    blank = jnp.zeros((batches, HALO, width), F32)
    sums = []
    add = lambda value: jnp.sum(value.reshape(rows, width), axis=0, keepdims=True)
    for offset in range(taps):
        masked = pulled * tap_mask(spot, offset)
        weighted = jnp.concatenate([blank, conv_w[offset : offset + 1][None] * masked], axis=1)
        spread = spread + (shifted_up(weighted, offset, 0.0) if offset else weighted)
        sums.append(add(masked * extended[:, HALO - offset : HALO - offset + length]))
    earlier_out[...] = spread[:, :HALO]
    spread_out[...] = spread[:, HALO:]
    sums += [add(pulled), add(grad_a), add(grad_i), add(grad_log * log_a)]
    sums_out[...] = jnp.concatenate(sums, axis=0)


def recur_back(
    behind,
    local_grad,
    carry_back,
    running,
    local_state,
    carry,
    gate_rec,
    gate_in,
    conv,
    branch,
    halo,
    places,
    conv_w,
    gates,
    decay_log,
):
    batches, length, features = behind.shape
    head = gates.shape[1] // 2
    taps = conv_w.shape[0]
    tokens, edge, place, row, tap, gate, _, carried = head_specs(
        batches, length, head, taps, HEADS_EACH
    )
    block = pl.BlockSpec((head * HEADS_EACH, head), lambda h: (h, 0))
    return pl.pallas_call(
        recur_back_kernel,
        grid=(features // (head * HEADS_EACH),),
        in_specs=[tokens, tokens, carried, tokens, tokens, carried]
        + [tokens] * 4
        + [edge, place, tap, *gate, row],
        out_specs=[
            tokens,
            edge,
            block,
            block,
            pl.BlockSpec((taps + 4, head * HEADS_EACH), lambda h: (0, h)),
        ],
        out_shape=[
            jax.ShapeDtypeStruct((batches, length, features), F32),
            jax.ShapeDtypeStruct((batches, HALO, features), F32),
            jax.ShapeDtypeStruct((features, head), BF16),
            jax.ShapeDtypeStruct((features, head), BF16),
            jax.ShapeDtypeStruct((taps + 4, features), F32),
        ],
        compiler_params=params(),
        cost_estimate=cost(300 * batches * length * features, 50 * batches * length * features),
        name="recur_back",
    )(
        behind,
        local_grad,
        carry_back,
        running,
        local_state,
        carry,
        gate_rec,
        gate_in,
        conv,
        branch,
        halo,
        places,
        conv_w,
        gates,
        gates,
        decay_log,
    )


def unit_step(gate_pre, up_pre, pulled, hidden_out, gate_out, up_out):
    act, slope = gelu_pair(gate_pre)
    hidden_out[...] = (act * up_pre).astype(BF16)
    gate_out[...] = (pulled * up_pre * slope).astype(BF16)
    up_out[...] = (pulled * act).astype(BF16)


def fill(target, pieces):
    start = 0
    for piece in pieces:
        target[start : start + piece.shape[0]] = piece
        start += piece.shape[0]


def units_kernel(count, *refs):
    pieces, (w_gate, w_up, pulled, hidden_out, gate_out, up_out, tokens) = refs[:count], refs[count:]

    @pl.when(pl.program_id(0) == 0)
    def _():
        fill(tokens, [p[...] for p in pieces])

    gate_pre, up_pre = dot(tokens[...], w_gate[...]), dot(tokens[...], w_up[...])
    unit_step(gate_pre, up_pre, pulled[...].astype(F32), hidden_out, gate_out, up_out)


def units(pieces, w_gate, w_up, pulled):
    count = len(pieces)
    rows, width = pieces[0].shape
    held = w_gate.shape[1]
    tile = 640
    whole = pl.BlockSpec((rows, width), lambda j: (0, 0), pipeline_mode=pl.Buffered(1))
    column = pl.BlockSpec((width, tile), lambda j: (0, j))
    out = pl.BlockSpec((count * rows, tile), lambda j: (0, j))
    return pl.pallas_call(
        partial(units_kernel, count),
        grid=(held // tile,),
        in_specs=[whole] * count + [column, column, out],
        out_specs=[out] * 3,
        out_shape=[jax.ShapeDtypeStruct((count * rows, held), BF16)] * 3,
        scratch_shapes=[pltpu.VMEM((count * rows, width), BF16)],
        compiler_params=params(),
        cost_estimate=cost(4 * count * rows * width * held, 4 * width * held),
        name="units",
    )(*pieces, w_gate, w_up, pulled)


def pull_units_kernel(count, *refs):
    pieces, (w_down, out, tokens) = refs[:count], refs[count:]

    @pl.when(pl.program_id(0) == 0)
    def _():
        fill(tokens, [p[...] for p in pieces])

    out[...] = dot_nt(tokens[...], w_down[...]).astype(BF16)


def pull_units(pieces, w_down):
    count = len(pieces)
    rows, width = pieces[0].shape
    held = w_down.shape[0]
    tile = 640
    whole = pl.BlockSpec((rows, width), lambda j: (0, 0), pipeline_mode=pl.Buffered(1))
    return pl.pallas_call(
        partial(pull_units_kernel, count),
        grid=(held // tile,),
        in_specs=[whole] * count + [pl.BlockSpec((tile, width), lambda j: (j, 0))],
        out_specs=pl.BlockSpec((count * rows, tile), lambda j: (0, j)),
        out_shape=jax.ShapeDtypeStruct((count * rows, held), BF16),
        scratch_shapes=[pltpu.VMEM((count * rows, width), BF16)],
        compiler_params=params(),
        cost_estimate=cost(2 * count * rows * width * held, 2 * width * held),
        name="pull_units",
    )(*pieces, w_down)


def units_back_kernel(gate, up, w_gate, w_up, out):
    out[...] = (dot_nt(gate[...], w_gate[...]) + dot_nt(up[...], w_up[...])).astype(BF16)


def units_back(gate, up, w_gate, w_up):
    tile = 640
    rows = gate.shape[0]
    width, held = w_gate.shape
    whole = pl.BlockSpec((rows, held), lambda j: (0, 0), pipeline_mode=pl.Buffered(1))
    row = pl.BlockSpec((tile, held), lambda j: (j, 0))
    return pl.pallas_call(
        units_back_kernel,
        grid=(width // tile,),
        in_specs=[whole, whole, row, row],
        out_specs=pl.BlockSpec((rows, tile), lambda j: (0, j)),
        out_shape=jax.ShapeDtypeStruct((rows, width), BF16),
        compiler_params=params(),
        cost_estimate=cost(4 * rows * width * held, 4 * width * held),
        name="units_back",
    )(gate, up, w_gate, w_up)


def units_made_kernel(hidden, w_down, out):
    out[...] = dot(hidden[...], w_down[...]).astype(BF16)


def units_made(hidden, w_down):
    tile = 1280
    rows, held = hidden.shape
    width = w_down.shape[1]
    return pl.pallas_call(
        units_made_kernel,
        grid=(width // tile,),
        in_specs=[
            pl.BlockSpec((rows, held), lambda j: (0, 0), pipeline_mode=pl.Buffered(1)),
            pl.BlockSpec((held, tile), lambda j: (0, j)),
        ],
        out_specs=pl.BlockSpec((rows, tile), lambda j: (0, j)),
        out_shape=jax.ShapeDtypeStruct((rows, width), BF16),
        compiler_params=params(),
        cost_estimate=cost(2 * rows * width * held, 2 * width * held),
        name="units_made",
    )(hidden, w_down)


def window_of(held):
    width = -(-held // 2 // 128) * 128
    return width, held - width


def others(places, gathered, pieces):
    count = len(pieces)
    return [gathered[(places[0] + j) % (count + 1)] for j in range(1, count + 1)] + [
        p[...] for p in pieces
    ]


def share_pull_kernel(count, places, *refs):
    gathered, pieces, (w_down, out, tokens) = refs[0], refs[1 : 1 + count], refs[1 + count :]

    @pl.when(pl.program_id(0) == 0)
    def _():
        fill(tokens, others(places, gathered, pieces))

    out[...] = dot_nt(tokens[...], w_down[...]).astype(BF16)


def share_kernel(count, places, *refs):
    gathered, pieces = refs[0], refs[1 : 1 + count]
    w_gate, w_up, pulled, hidden_out, gate_out, up_out, tokens = refs[1 + count :]

    @pl.when(pl.program_id(0) == 0)
    def _():
        fill(tokens, others(places, gathered, pieces))

    gate_pre, up_pre = dot(tokens[...], w_gate[...]), dot(tokens[...], w_up[...])
    unit_step(gate_pre, up_pre, pulled[...].astype(F32), hidden_out, gate_out, up_out)


def share_call(kernel, places, gathered, pieces, weights, more, outs, name):
    count = len(pieces)
    rows, width = pieces[0].shape
    tile = 512
    held = weights[0].shape[0] if weights[0].shape[1] == width else weights[0].shape[1]
    window, offset = window_of(held)
    total = 2 * count * rows
    specs = []
    for weight in weights:
        if weight.shape[1] == width:
            specs.append(
                pl.BlockSpec(
                    (pl.Element(tile), pl.Element(width)),
                    lambda j, places: (pl.multiple_of(places[1] * offset + j * tile, 128), 0),
                )
            )
        else:
            specs.append(
                pl.BlockSpec(
                    (pl.Element(width), pl.Element(tile)),
                    lambda j, places: (0, pl.multiple_of(places[1] * offset + j * tile, 128)),
                )
            )
    out = pl.BlockSpec((total, tile), lambda j, places: (0, j))
    result = pl.pallas_call(
        partial(kernel, count),
        grid_spec=pltpu.PrefetchScalarGridSpec(
            num_scalar_prefetch=1,
            grid=(window // tile,),
            in_specs=[
                pl.BlockSpec(
                    gathered.shape, lambda j, places: (0, 0, 0), pipeline_mode=pl.Buffered(1)
                )
            ]
            + [
                pl.BlockSpec((rows, width), lambda j, places: (0, 0), pipeline_mode=pl.Buffered(1))
            ]
            * count
            + specs
            + [out] * len(more),
            out_specs=[out] * outs,
            scratch_shapes=[pltpu.VMEM((total, width), BF16)],
        ),
        out_shape=[jax.ShapeDtypeStruct((total, window), BF16)] * outs,
        compiler_params=params(),
        cost_estimate=cost(
            2 * len(weights) * total * width * window, 2 * len(weights) * width * window
        ),
        name=name,
    )(places, gathered, *pieces, *weights, *more)
    return result


def share_pull(places, gathered, pieces, w_down):
    return share_call(share_pull_kernel, places, gathered, pieces, [w_down], [], 1, "share_pull")[0]


def share(places, gathered, pieces, w_gate, w_up, pulled):
    return share_call(
        share_kernel, places, gathered, pieces, [w_gate, w_up], [pulled], 3, "share"
    )


def unit_grad_kernel(count, kinds, places, *refs):
    token_refs, refs = refs[: 2 * (1 + count)], refs[2 * (1 + count) :]
    own_x, acts, outs = refs[:2], refs[2 : 2 + 3 * kinds], refs[2 + 3 * kinds : 2 + 5 * kinds]
    left, whole = refs[2 + 5 * kinds :]
    block = whole.shape[0] // 2
    here, there = token_refs[: 1 + count], token_refs[1 + count :]
    me = places[0]
    fill(
        left,
        [here[0][me], there[0][me], own_x[0][...], own_x[1][...]]
        + others(places, here[0], here[1:])
        + others(places, there[0], there[1:]),
    )
    own = pl.multiple_of(places[2] * block, block)
    other = pl.multiple_of((1 - places[2]) * block, block)
    for kind in range(kinds):
        parts = acts[3 * kind : 3 * kind + 3]
        total, start = None, 0
        for part in parts:
            size = part.shape[0]
            term = dot_tn(left[start : start + size], part[...])
            total = term if total is None else total + term
            start += size
        whole[...] = total
        outs[2 * kind][0] = whole[pl.ds(own, block)]
        outs[2 * kind + 1][0] = whole[pl.ds(other, block)].astype(BF16)


def unit_grad(places, here, there, own_x, acts):
    count, kinds = len(here[1]), len(acts)
    rows, features = own_x[0].shape
    window, offset = window_of(acts[0][0].shape[1])
    width = features // (count + 1)
    total = 4 * (count + 1) * rows
    once = pl.Buffered(1)
    gathered = pl.BlockSpec((count + 1, rows, width), lambda i, p: (0, 0, 2 * (p[0] // 2) + i))
    piece = pl.BlockSpec((rows, width), lambda i, p: (0, 2 * (p[0] // 2) + i))
    mine = pl.BlockSpec(
        (pl.Element(4 * rows), pl.Element(window)),
        lambda i, p: (0, pl.multiple_of(p[1] * offset, 128)),
        pipeline_mode=once,
    )
    act = pl.BlockSpec((2 * count * rows, window), lambda i, p: (0, 0), pipeline_mode=once)
    out = pl.BlockSpec((1, width // 2, window), lambda i, p: (i, 0, 0))
    shape = (2, width // 2, window)
    return pl.pallas_call(
        partial(unit_grad_kernel, count, kinds),
        grid_spec=pltpu.PrefetchScalarGridSpec(
            num_scalar_prefetch=1,
            grid=(2,),
            in_specs=([gathered] + [piece] * count) * 2 + [piece] * 2 + [mine, act, act] * kinds,
            out_specs=[out] * (2 * kinds),
            scratch_shapes=[
                pltpu.VMEM((total, width), BF16),
                pltpu.VMEM((width, window), F32),
            ],
        ),
        out_shape=[jax.ShapeDtypeStruct(shape, d) for d in (F32, BF16)] * kinds,
        compiler_params=params(),
        cost_estimate=cost(4 * kinds * total * width * window, 2 * kinds * total * window),
        name="unit_grad",
    )(places, here[0], *here[1], there[0], *there[1], *own_x, *[a for v in acts for a in v])


def window_part(value, places, axis):
    window, offset = window_of(value.shape[axis])
    return lax.dynamic_slice_in_dim(value, places[1] * offset, window, axis=axis)


def others_plain(places, gathered, pieces):
    count = len(pieces)
    rolled = jnp.roll(gathered, -places[0], axis=0)[1:].reshape(-1, gathered.shape[2])
    return jnp.concatenate([rolled, *pieces], axis=0)


def share_pull_plain(places, gathered, pieces, w_down):
    tokens = others_plain(places, gathered, pieces)
    return dot_nt(tokens, window_part(w_down, places, 0)).astype(BF16)


def share_plain(places, gathered, pieces, w_gate, w_up, pulled):
    tokens = others_plain(places, gathered, pieces)
    act, slope = gelu_pair(dot(tokens, window_part(w_gate, places, 1)))
    up_pre = dot(tokens, window_part(w_up, places, 1))
    pulled = pulled.astype(F32)
    return [v.astype(BF16) for v in (act * up_pre, pulled * up_pre * slope, pulled * act)]


def unit_grad_plain(places, here, there, own_x, acts):
    features = own_x[0].shape[1]
    block = features // (2 * (len(here[1]) + 1))
    at = lambda v: lax.dynamic_index_in_dim(v, places[0], 0, keepdims=False)
    tokens = [at(here[0]), at(there[0]), *own_x]
    tokens = jnp.concatenate(
        tokens + [others_plain(places, *here), others_plain(places, *there)], axis=0
    )
    tokens = lax.dynamic_slice_in_dim(tokens, places[0] // 2 * 4 * block, 4 * block, axis=1)
    outs = []
    for own, *rest in acts:
        right = jnp.concatenate([window_part(own, places, 1), *rest], axis=0)
        whole = dot_tn(tokens, right).reshape(2, 2, block, -1)
        outs.append(pick(places[2], whole[:, 0], whole[:, 1]))
        outs.append(pick(places[2], whole[:, 1], whole[:, 0]).astype(BF16))
    return outs


def carry_join(ends, other, bit, direction):
    half = ends.shape[0] // 2
    is_last = bit if direction > 0 else 1 - bit
    first_end = pick(is_last, ends[half:], other[half:])
    last_end = pick(is_last, other[half:], ends[half:])
    last_run = pick(is_last, other[:half], ends[:half])
    return jnp.concatenate(
        [ends[:half] * other[:half], last_run * first_end + last_end], axis=0
    )


def carry_shifts(joined, direction):
    return [shift(joined, SZ, direction * k) for k in range(1, lax.axis_size(SZ))]


def line_tree(line, *values):
    leaves, tree = jax.tree.flatten(values)
    return jax.tree.unflatten(tree, line(*leaves))


def tied_carry(line, other, arrived):
    other, *arrived = line(other, *arrived)
    return other, arrived


def carry_finish(other, arrived, bit, direction):
    half = other.shape[0] // 2
    is_last = bit if direction > 0 else 1 - bit
    entering = jnp.zeros_like(other[half:])
    for far in reversed(arrived):
        entering = far[half:] + far[:half] * entering
    return pick(is_last, entering, other[half:] + other[:half] * entering)[:, None]


def rows_for(axis, place, stack):
    bit = lax.axis_index(axis)
    low, high = (lax.index_in_dim(stack, i, place, keepdims=False) for i in (0, 1))
    return pick(bit, low, high), pick(bit, high, low)


def token_grad_kernel(offset, *refs):
    pieces, (near, away, out, left, right) = refs[:8], refs[8:]
    rows = pieces[0].shape[0]

    @pl.when(pl.program_id(0) == 0)
    def _():
        for i in range(8):
            held = (near if i < 4 else away)[i % 4]
            left[:, i * rows : (i + 1) * rows] = held[:, offset : offset + rows]

    fill(right, [p[...] for p in pieces])
    out[...] = dot(left[...], right[...]).astype(BF16)


def token_grad(near, away, second, pieces):
    rows, width = pieces[0].shape
    held = near.shape[1]
    tile = 640
    piece = pl.BlockSpec((rows, tile), lambda j: (0, j))
    whole = pl.BlockSpec(near.shape, lambda j: (0, 0, 0), pipeline_mode=pl.Buffered(1))
    return pl.pallas_call(
        partial(token_grad_kernel, second * rows),
        grid=(width // tile,),
        in_specs=[piece] * 8 + [whole, whole],
        out_specs=pl.BlockSpec((held, tile), lambda j: (0, j)),
        out_shape=jax.ShapeDtypeStruct((held, width), BF16),
        scratch_shapes=[pltpu.VMEM((held, 8 * rows), BF16), pltpu.VMEM((8 * rows, tile), BF16)],
        compiler_params=params(),
        cost_estimate=cost(16 * held * rows * width, 20 * rows * width),
        name="token_grad",
    )(*pieces, near, away)


def total_of_all(value):
    far = lax.axis_size(SZ)
    held = value.reshape(far, 2, 2, 2, -1)
    for place, axis in ((3, WC), (2, WX), (1, SY)):
        bit = lax.axis_index(axis)
        low, high = (lax.index_in_dim(held, i, place, keepdims=False) for i in (0, 1))
        held = pick(bit, low, high) + swap(pick(bit, high, low), axis)
    here = lax.axis_index(SZ)
    mine = lax.dynamic_index_in_dim(held, here, 0, keepdims=False)
    for steps in range(1, far):
        block = lax.dynamic_index_in_dim(held, (here - steps) % far, 0, keepdims=False)
        mine = mine + around(block, steps)
    return mine


def join_gates(own, core, x_part, both, wx, wc):
    parts = [[pick(wc, p, q), pick(wc, q, p)] for p, q in ((own, core), (x_part, both))]
    return jnp.concatenate(
        [pick(wx, parts[0][i], parts[1][i]) for i in (0, 1)]
        + [pick(wx, parts[1][i], parts[0][i]) for i in (0, 1)],
        axis=0,
    )


def scatter_far(value):
    return lax.psum_scatter(value, SZ, scatter_dimension=0, tiled=True)


def local(
    inputs,
    positions,
    cotangent,
    gain,
    w_x,
    w_y,
    conv_w,
    conv_b,
    gate_a,
    bias_a,
    gate_i,
    bias_i,
    decay_log,
    w_out,
    gain2,
    w_gate,
    w_up,
    w_down,
):
    batches, length, features = inputs.shape
    rows = batches * length
    head = gate_a.shape[1]
    taps = conv_w.shape[0]
    held = w_gate.shape[1]
    far = lax.axis_size(SZ)
    wx, wc, sy = (lax.axis_index(a) for a in (WX, WC, SY))
    as_row = lambda v: v.reshape(1, features)
    cube = lambda v: v.reshape(batches, length, features)
    flat = lambda v: v.reshape(rows, features)

    line = Line()
    sz = lax.axis_index(SZ)
    parity = sz % 2
    spots = jnp.stack([sz, parity, sy]).astype(jnp.int32)
    edge = length - (taps - 1)
    places = positions[..., None]
    half = 2 * rows
    low = lambda v: v.astype(BF16)
    wide = lambda v: v.astype(F32)
    plain = (features // far) % 128 != 0 or far > 4
    pull_of, share_of, grad_of = (
        (share_pull_plain, share_plain, unit_grad_plain) if plain else (share_pull, share, unit_grad)
    )

    oth_x, oth_y, oth_out = swap(w_x, WC), swap(w_y, WC), swap(w_out, WC)
    own_gates = jnp.concatenate([gate_a, gate_i], axis=1)
    gates = lax.all_gather(own_gates, (WX, WC), axis=0, tiled=True)
    cot = flat(cotangent)
    cot_all = lax.all_gather(cot, SZ)
    cot_core = swap(cot, WC)
    source = wide(flat(inputs))
    norm_scale = lax.rsqrt(jnp.mean(source * source, axis=-1, keepdims=True) + 1e-06)
    normed = low(source * norm_scale * gain)
    keep, send = split_columns(normed, wx, wc)
    line.mark(send)
    recv = swap(send, WX)
    normed_turned = line.mark(line(normed)[0].T)

    sent, own_x = project(*line(recv, keep, w_x, oth_x))
    line.mark(sent)
    recv_x = swap(sent, WX)
    sent, own_y = project(*line(recv, keep, w_y, oth_y))
    line.mark(sent)
    recv_y, cot_x = swap(after(sent, recv_x), WX), swap(after(cot, recv_x), WX)
    own_x, recv_x, own_y, recv_y = cube(own_x), cube(recv_x), cube(own_y), cube(recv_y)
    tail_own, tail_recv = line(own_x[:, edge:], recv_x[:, edge:])
    tail = along_seq(line.mark(low(tail_own + wide(tail_recv))), 1)
    own_x, recv_x, tail, gates = line(own_x, recv_x, tail, gates)
    halo = jnp.pad(wide(tail), ((0, 0), (HALO - (taps - 1), 0), (0, 0)))
    branch_x, conv, gate_rec, gate_in, running, local_state, ends = recur(
        own_x,
        recv_x,
        halo,
        places,
        conv_w,
        as_row(conv_b),
        gates,
        as_row(bias_a),
        as_row(bias_i),
        as_row(decay_log),
    )
    line.mark(ends)
    other_ends = swap(ends, SY)
    ends, other_ends = line(ends, other_ends)
    joined = line.mark(carry_join(ends, other_ends, sy, 1))
    arrived = carry_shifts(joined, 1)
    own_y, recv_y = line(own_y, recv_y)
    branch_y = line.mark(gelu_pair(own_y + wide(recv_y))[0])
    carry = carry_finish(*tied_carry(line, other_ends, arrived), sy, 1)
    mixed = flat(low((local_state + running * carry) * branch_y))
    keep, send = split_columns(mixed, wx, wc)
    line.mark(send)
    recv = swap(send, WX)
    cot_x, mixed = line(cot_x, mixed)
    cot_both = swap(cot_x, WC)
    cot_x_far = [None if 2 * j == far else around(cot_x, j) for j in range(1, far)]
    both_turned = line.mark(jnp.concatenate([normed_turned, mixed.T], axis=1))
    recv, keep, oth_out, cot_all = line(recv, keep, oth_out, cot_all)
    sent, own = project(recv, keep, w_out, oth_out)
    line.mark(sent)
    recv = swap(sent, WX)
    pulled_units = line.mark(pull_units(line(cot, cot_core, cot_x, cot_both), w_down))
    own, recv = line(own, recv)
    stream = source + own + wide(recv)
    second_scale = lax.rsqrt(jnp.mean(stream * stream, axis=-1, keepdims=True) + 1e-06)
    normed_two = line.mark(low(stream * second_scale * gain2))

    normed_x, normed_core = swap(normed_two, WX), swap(normed_two, WC)
    normed_all = lax.all_gather(normed_two, SZ)
    core_of = lambda values: [swap(v, WC) for v in values]
    turned = both_turned.reshape(far, 2, 2, 2, features // (8 * far), half)
    turned, cot_x_far = line_tree(line, turned, cot_x_far)
    mine_x, send_x = rows_for(WX, 2, turned)
    got_x = swap(line.mark(send_x), WX)
    normed_both = swap(normed_x, WC)
    opposite = lambda v: lax.dynamic_index_in_dim(v, (sz + far // 2) % far, 0, keepdims=False)
    across = lambda pieces, gathered: [
        swap(opposite(gathered), WX) if v is None else v for v in pieces
    ]
    tied = line(normed_two, normed_core, normed_x, normed_both)
    normed_x_far = [None if 2 * j == far else around(tied[2], j) for j in range(1, far)]
    cot_x_far = across(cot_x_far, after(cot_all, tied[2]))
    acted = units(tied, w_gate, w_up, pulled_units)
    hidden, gate_grad, up_grad = acted
    line.mark(hidden)
    mine_y, send_y = rows_for(SY, 2, jnp.stack(line(mine_x, got_x)))
    got_y = swap(line.mark(send_y), SY)
    pulled = line.mark(units_back(*line(gate_grad, up_grad), w_gate, w_up))
    pulled_both, pulled_core = swap(pulled[half + rows :], WC), swap(pulled[rows:half], WC)
    pulled_there, pulled_both, got_y, normed_all, cot_x_far = line_tree(
        line, pulled[half : half + rows], pulled_both, got_y, normed_all, cot_x_far
    )
    for_x = line.mark(low(wide(pulled_there) + wide(pulled_both)))
    from_x = swap(for_x, WX)
    made = line.mark(units_made(*line(hidden), w_down))
    mine_y, got_y = line(mine_y, got_y)
    near, send = rows_for(WC, 2, jnp.concatenate([mine_y, got_y], axis=0))
    near, send = (v.reshape(4, features // 8, half) for v in (near, send))
    away = swap(line.mark(send), WC)
    pulled_here, pulled_core, from_x, normed_x_far = line_tree(
        line, pulled[:rows], pulled_core, from_x, normed_x_far
    )
    grad_normed_two = wide(pulled_here) + wide(pulled_core) + wide(from_x)
    weighted_two = grad_normed_two * gain2
    grad_stream = (
        wide(cot)
        + weighted_two * second_scale
        - stream * second_scale**3 * jnp.mean(weighted_two * stream, axis=-1, keepdims=True)
    )
    grad_gain2 = jnp.sum(grad_normed_two * stream * second_scale, axis=0)
    grad_proj = line.mark(low(grad_stream))
    proj_x, proj_y = swap(grad_proj, WX), swap(grad_proj, SY)
    normed_x_far = across(normed_x_far, normed_all)
    tied = line(cot_all, *cot_x_far)
    pull_here = line.mark(pull_of(spots, tied[0], tied[1:], w_down))

    cot_core_all, cot_both_far = swap(cot_all, WC), core_of(cot_x_far)
    normed_core_all = swap(normed_all, WC)
    cot_here, cot_there = (cot_all, cot_x_far), (cot_core_all, cot_both_far)

    def shared(gathered, pieces, pulled):
        gathered, pulled, *pieces = line(gathered, pulled, *pieces)
        acts = share_of(spots, gathered, pieces, w_gate, w_up, pulled)
        line.mark(acts[0])
        return acts

    def unit_sums(here, there, own_x, kinds):
        acts = [line(acted[k], acts_here[k], acts_there[k]) for k in kinds]
        outs = grad_of(spots, here, there, line(*own_x), acts)
        line.mark(outs[0])
        return [(outs[2 * i], swap(outs[2 * i + 1], SY)) for i in range(len(kinds))]

    def unit_join(mine, got):
        mine, got = line(mine, got)
        both = low(mine + wide(got))
        own, other = pick(parity, both[0], both[1]), pick(parity, both[1], both[0])
        line.mark(other)
        return own, partner_far(other)

    window, offset = window_of(held)

    def unit_final(own, other):
        own, other = line(own, other)
        parts = pick(parity, own, other), pick(parity, other, own)
        return wide(jnp.concatenate([parts[0], parts[1][:, window - offset :]], axis=1))

    def token_grad_of(second, *pieces):
        pieces = [*pieces, *core_of(pieces)]
        return line.mark(token_grad(*line(near, away), second, line(*pieces)))

    proj_x, proj_y, grad_proj = line(proj_x, proj_y, grad_proj)
    sent, own = project_back([(proj_x, grad_proj, w_out, oth_out)])
    line.mark(sent)
    sent, proj_xy = swap(sent, WX), swap(proj_x, SY)
    tied = line(cot_core_all, *cot_both_far)
    pull_there = line.mark(pull_of(spots, tied[0], tied[1:], w_down))
    sent, own, proj_xy, normed_x_far = line_tree(line, sent, own, proj_xy, normed_x_far)
    normed_both_far = core_of(normed_x_far)
    normed_here, normed_there = (normed_all, normed_x_far), (normed_core_all, normed_both_far)
    grad_mixed = cube(join_columns(own, wide(sent), wx, wc))
    line.mark(grad_mixed)
    grad_pre, behind, local_grad, back_ends = unroll(
        *line(grad_mixed, own_y, recv_y, running, local_state, carry, gate_rec),
        places,
        as_row(decay_log),
        head,
    )
    line.mark(back_ends)
    grad_pre = flat(grad_pre)
    other_ends = swap(back_ends, SY)
    pre_x, pre_y = swap(grad_pre, WX), swap(grad_pre, SY)
    back_ends, other_ends = line(back_ends, other_ends)
    joined = line.mark(carry_join(back_ends, other_ends, sy, -1))
    arrived = carry_shifts(joined, -1)
    acts_here = shared(*normed_here, pull_here)
    other_ends, pre_x, pre_y, *arrived = line(other_ends, pre_x, pre_y, *arrived)
    carry_back = carry_finish(other_ends, arrived, sy, -1)
    line.mark(carry_back)
    spread, earlier, grad_wa, grad_wi, sums = recur_back(
        *line(behind, local_grad, carry_back, running, local_state, carry),
        gate_rec,
        gate_in,
        conv,
        branch_x,
        halo,
        places,
        conv_w,
        gates,
        as_row(decay_log),
    )
    line.mark(earlier)
    pre_xy = swap(pre_x, SY)
    later = along_seq(low(earlier[:, HALO - (taps - 1) :]), -1)
    out_sums = scatter_far(token_grad_of(1, grad_proj, proj_x, proj_y, proj_xy))
    grad_wa, grad_wi, sums, grad_gain2 = line(grad_wa, grad_wi, sums, grad_gain2)
    small = jnp.concatenate([grad_gain2[None], sums], axis=0)
    small = low(jnp.pad(small.T, ((0, 0), (0, 128 - small.shape[0]))))
    rest = jnp.concatenate([grad_wa, grad_wi, small], axis=1)
    rest = line.mark(rest).reshape(far, 2, 2, 2, features // (8 * far), -1)

    def rest_step(axis, place, value):
        mine, send = rows_for(axis, place, value)
        line.mark(send)
        return mine, swap(send, axis)

    def rest_join(mine, got):
        mine, got = line(mine, got)
        return low(wide(mine) + wide(got))

    rest = rest_step(WC, 3, rest)
    spread, later = line(spread, later)
    grad_branch = flat(low(spread + jnp.pad(wide(later), ((0, 0), (edge, 0), (0, 0)))))
    line.mark(grad_branch)
    branch_x_part, branch_y_part = swap(grad_branch, WX), swap(grad_branch, SY)
    rest = rest_step(WX, 2, rest_join(*rest))
    acts_there = shared(*normed_there, pull_there)
    branch_x_part, branch_y_part, pre_xy = line(branch_x_part, branch_y_part, pre_xy)
    sent, own = project_back(
        [
            line(branch_x_part, grad_branch, w_x, oth_x),
            line(pre_x, grad_pre, w_y, oth_y),
        ]
    )
    line.mark(sent)
    sent = swap(sent, WX)
    branch_xy_part = swap(branch_y_part, WX)
    (down,) = unit_sums(cot_here, cot_there, (cot_x, cot_both), [0])
    rest = rest_step(SY, 1, rest_join(*rest))
    sent, own, branch_xy_part, out_sums = line(sent, own, branch_xy_part, out_sums)
    grad_normed = join_columns(own, wide(sent), wx, wc)
    weighted = grad_normed * gain
    input_grad = (
        grad_stream
        + weighted * norm_scale
        - source * norm_scale**3 * jnp.mean(weighted * source, axis=-1, keepdims=True)
    )
    grad_gain = jnp.sum(grad_normed * source * norm_scale, axis=0)
    line.mark(grad_gain)

    y_sums = scatter_far(token_grad_of(0, grad_pre, pre_x, pre_y, pre_xy))
    (gate,) = unit_sums(normed_here, normed_there, (normed_x, normed_both), [1])
    x_grad = token_grad_of(0, grad_branch, branch_x_part, branch_y_part, branch_xy_part)

    down = unit_join(*down)
    (up,) = unit_sums(normed_here, normed_there, (normed_x, normed_both), [2])
    rest = rest_join(*rest).reshape(features // 8, -1)
    late_sums = scatter_far(line.mark(jnp.concatenate([x_grad, rest], axis=1)))
    gate = unit_join(*gate)
    (y_sums,) = line(y_sums)
    up = unit_join(*up)
    grad_gain = total_of_all(*line(grad_gain))
    made_there, made_both = line(made[half : half + rows], swap(after(made, grad_mixed)[half + rows :], WC))
    made_x = swap(line.mark(low(wide(made_there) + wide(made_both))), WX)
    made_core = swap(after(made, grad_mixed)[rows:half], WC)
    down_grad = line.mark(unit_final(*down).T)
    made_here, made_core, made_x = line(made[:rows], made_core, made_x)
    output = line.mark(low(stream + wide(made_here) + wide(made_core) + wide(made_x)))
    gate_grad = line.mark(unit_final(*gate))
    up_grad = line.mark(unit_final(*up))
    x_sums, rest = late_sums[:, :features], wide(late_sums[:, features:])
    grads = rest[:, 2 * head :]
    return (
        cube(output),
        cube(input_grad),
        grad_gain,
        wide(x_sums),
        wide(y_sums),
        grads[:, 1 : 1 + taps].T,
        grads[:, 1 + taps],
        rest[:, :head],
        grads[:, 2 + taps],
        rest[:, head : 2 * head],
        grads[:, 3 + taps],
        grads[:, 4 + taps],
        wide(out_sums),
        grads[:, 0],
        gate_grad,
        up_grad,
        down_grad,
    )


def solution(mesh):
    seq, wt = mesh.devices.shape
    split = Mesh(mesh.devices.reshape(seq // 2, 2, wt // 2, 2), (SZ, SY, WX, WC))
    s, w = (SZ, SY), (WX, WC)
    everywhere = (SZ, SY, WX, WC)
    return jax.shard_map(
        local,
        mesh=split,
        in_specs=(
            P(w, s, None),
            P(w, s),
            P(w, s, None),
            P(),
            P(w, None),
            P(w, None),
            P(),
            P(),
            P(w, None),
            P(),
            P(w, None),
            P(),
            P(),
            P(w, None),
            P(),
            P(None, w),
            P(None, w),
            P(w, None),
        ),
        out_specs=(
            P(w, s, None),
            P(w, s, None),
            P(everywhere),
            P(everywhere, None),
            P(everywhere, None),
            P(None, everywhere),
            P(everywhere),
            P(everywhere, None),
            P(everywhere),
            P(everywhere, None),
            P(everywhere),
            P(everywhere),
            P(everywhere, None),
            P(everywhere),
            P(s, w),
            P(s, w),
            P(w, s),
        ),
        check_vma=False,
    )
```

time: 909 us -> 642 us (0.71)
  waiting for transfers between devices: 544 us -> 203 us
  Pallas kernels: 105 us -> 191 us
  local copies, waits for them, and re-layouts: 66.2 us -> 40 us
  matrix products: 46.1 us -> 26.7 us
  starting transfers between devices: 72.7 us -> 91.3 us
  other arithmetic: 52.6 us -> 65.1 us
    ppermute x48 -> x67, waiting for transfers between devices: 432 us -> 130 us  [swap(): return lax.ppermute(value, axis, [(0, 1), (1, 0)])]
    reduce_scatter x8 -> x3, waiting for transfers between devices: 104 us -> 0.01 us  [scatter_far(): return lax.psum_scatter(value, SZ, scatter_dimension=0, tiled=True)]
    pallas_call x11 -> x17, Pallas kernels: 105 us -> 191 us  [the longest x4 50.9 us: share_call(): pl.pallas_call(partial(kernel, count), grid_spec=pltpu.PrefetchScalarGrid...]
    ppermute x0 -> x10, waiting for transfers between devices: none -> 68.9 us  [the longest x7 50.7 us: around(): lax.ppermute(value, SZ, [((to + steps) % count, to) for to in range(count)])]
    unnamed x245 -> x134, local copies, waits for them, and re-layouts: 49 us -> 13.2 us
    dot_general x7 -> x3, matrix products: 46.1 us -> 12.3 us  [dot(): return jnp.dot(left, right, preferred_element_type=F32)]
    ppermute x0 -> x10, starting transfers between devices: none -> 20.7 us  [the longest x7 15.9 us: around(): lax.ppermute(value, SZ, [((to + steps) % count, to) for to in range(count)])]
    dot_general x0 -> x3, matrix products: none -> 14.3 us  [dot_nt(): lax.dot_general(left, right, (((1,), (1,)), ((), ())), preferred_element_...]
  transfers between devices with their start and end apart: 65 -> 91, of which waited for: 41 -> 25; matrix products, arithmetic and copies ran while one was open for 12% -> 18% of each run, Pallas kernels for 2% -> 28%
where the time goes in v2:
time: 642 us; the launch traced here: 632 us
  waiting for transfers between devices  203 us (32%)
  Pallas kernels  191 us (30%)
  starting transfers between devices  91.3 us (14%)
  other arithmetic  65.1 us (10%)
  local copies, waits for them, and re-layouts  40 us (6%)
  matrix products  26.7 us (4%)
  between operations  15.6 us (2%)
    ppermute x67, waiting for transfers between devices, swap(): return lax.ppermute(value, axis, [(0, 1), (1, 0)])  130 us
    pallas_call x4, Pallas kernels, share_call(): pl.pallas_call(partial(kernel, count), grid_spec=pltpu.PrefetchScalarGrid...  50.9 us
    ppermute x7, waiting for transfers between devices, around(): lax.ppermute(value, SZ, [((to + steps) % count, to) for to in range(count)])  50.7 us
    ppermute x67, starting transfers between devices, swap(): return lax.ppermute(value, axis, [(0, 1), (1, 0)])  49.9 us
    pallas_call x3, Pallas kernels, unit_grad(): pl.pallas_call(partial(unit_grad_kernel, count, kinds), grid_spec=pltpu.P...  35.1 us
    convert_element_type x15, other arithmetic, local(): low = lambda v: v.astype(BF16)  21 us
    pallas_call x3, Pallas kernels, token_grad(): pl.pallas_call(partial(token_grad_kernel, second * rows), grid=(width //...  20 us
    pallas_call x1, Pallas kernels, units(): pl.pallas_call(partial(units_kernel, count), grid=(held // tile,), in_spe...  19.3 us
  transfers between devices with their start and end apart: 91, of which 25 were waited for; matrix products, arithmetic and copies ran while one was open for 18% of the time, Pallas kernels for 28%

profile of v2, /device:TPU:0, one launch (start us, length us, event | category | flops | bytes accessed | tf_op | source)
XLA Modules:
  0.0 632.4 jit_solution(1287084889565097476)
XLA Ops:
  11.6 3.0 collective-permute-start
  14.6 9.0 %collective-permute-done = bf16[128,1280]{1,0:T(8,128)(2,1)S(1)} collective-permute-done((bf16[128,1280]{1,0:T(8,128)(2,1)S(1)}, bf16[128,1280]{1,0:T(8,128)(2,1)S(1)}, u32[]{:S(2)}, u32[]{:S(2)}) %collective-permute-start) | collective-permute-done | bytes 327712 | tf_op jit(solution)/shard_map/ppermute | solution.py:22
  23.6 3.5 fusion
  27.2 2.6 collective-permute-start.2
  29.9 4.0 fusion.4
  35.6 15.3 %collective-permute-done.2 = bf16[128,2560]{1,0:T(8,128)(2,1)S(1)} collective-permute-done((bf16[128,2560]{1,0:T(8,128)(2,1)S(1)}, bf16[128,2560]{1,0:T(8,128)(2,1)S(1)}, u32[]{:S(2)}, u32[]{:S(2)}) %collective-permute-start.2) | collective-permute-done | bytes 655392 | tf_op jit(solution)/shard_map/ppermute | solution.py:22
  51.0 3.4 collective-permute-start.4
  58.9 9.3 %recur.1 = (bf16[2,64,2560]{2,1,0:T(8,128)(2,1)}, bf16[2,64,2560]{2,1,0:T(8,128)(2,1)}, f32[2,64,2560]{2,1,0:T(8,128)}, f32[2,64,2560]{2,1,0:T(8,128)}, f32[2,64...) custom-call(f32[2,64,2560]{2,1,0:T(8,128)} %bitcast.179, bf16[2,64,2560]{2,1,0:T(8,128)(2,1)} %bitcast.197, ...), custom_call_target="tpu_custom_call" | custom-call | flops 1310720 | bytes 262144 | tf_op jit(solution)/shard_map/recur/pallas_call | solution.py:261
  69.8 3.9 constant_dynamic-update-slice_fusion.1
  76.7 3.5 collective-permute-start.6
  80.2 3.2 collective-permute-start.7
  83.4 8.2 %collective-permute-done.9 = bf16[128,2560]{1,0:T(8,128)(2,1)S(1)} collective-permute-done((bf16[128,2560]{1,0:T(8,128)(2,1)S(1)}, bf16[128,2560]{1,0:T(8,128)(2,1)S(1)}, u32[]{:S(2)}, u32[]{:S(2)}) %collective-permute-start.9) | collective-permute-done | bytes 655392 | tf_op jit(solution)/shard_map/ppermute | solution.py:22
  91.6 4.3 collective-permute-start.8
  100.6 13.9 %collective-permute-done.12.refs_2_.refs_8_ = bf16[128,2560]{1,0:T(8,128)(2,1)} collective-permute-done((bf16[128,2560]{1,0:T(8,128)(2,1)}, bf16[128,2560]{1,0:T(8,128)(2,1)}, u32[]{:S(2)}, u32[]{:S(2)}) %collective-permute-start.12) | collective-permute-done | bytes 655392 | tf_op jit(solution)/shard_map/ppermute | solution.py:22
  115.7 3.7 collective-permute-done.10
  119.4 3.9 constant_dynamic-update-slice_fusion
  123.3 4.8 fusion.55
  130.6 10.4 %pull_units.1.refs_6_ = bf16[512,1920]{1,0:T(8,128)(2,1)} custom-call(bf16[128,2560]{1,0:T(8,128)(2,1)} %bitcast.9.refs_0_, bf16[128,2560]{1,0:T(8,128)(2,1)} %collective-permute-done.14.refs_1_, bf16[128,2560]{1,0:T(8,128)(2,1)} %collective-permute-done.12.refs_2_.refs_8_, bf16[128,2560]{1,0:T(8,128)(2,1)} %copy-done.24, bf16[1920,2560]{1,0:T(8,128)(2,1)} %refs_4_.9), custom_call_target="tpu_custom_call" | custom-call | flops 100663296 | bytes 196608 | tf_op jit(solution)/shard_map/pull_units/pallas_call | solution.py:525
  144.4 2.5 collective-permute-start.20
  150.1 43.3 %collective-permute-done.19.refs_1_ = bf16[128,2560]{1,0:T(8,128)(2,1)} collective-permute-done((bf16[128,2560]{1,0:T(8,128)(2,1)}, bf16[128,2560]{1,0:T(8,128)(2,1)}, u32[]{:S(2)}, u32[]{:S(2)}) %collective-permute-start.19) | collective-permute-done | bytes 655392 | tf_op jit(solution)/shard_map/ppermute | solution.py:33
  195.9 19.3 %units.1 = (bf16[512,1920]{1,0:T(8,128)(2,1)}, bf16[512,1920]{1,0:T(8,128)(2,1)}, bf16[512,1920]{1,0:T(8,128)(2,1)}) custom-call(bf16[128,2560]{1,0:T(8,128)(2,1)} %multiply_convert_fusion.refs_0_, bf16[128,2560]{1,0:T(8,128)(2,1)} %collective-permute-done.16.refs_1_, bf16[128,2560]{1,0:T(8,128)(2,1)} %collective-permute-done.17.refs_2_.refs_8_, ...), custom_call_target="tpu_custom_call" | custom-call | flops 201326592 | bytes 393216 | tf_op jit(solution)/shard_map/units/pallas_call | solution.py:496
  218.7 18.1 %units_back.1 = bf16[512,2560]{1,0:T(8,128)(2,1)} custom-call(bf16[512,1920]{1,0:T(8,128)(2,1)} %get-tuple-element.441.gate.refs_10_, bf16[512,1920]{1,0:T(8,128)(2,1)} %get-tuple-element.461.up.refs_10_, bf16[2560,1920]{1,0:T(8,128)(2,1)} %refs_4_.11, bf16[2560,1920]{1,0:T(8,128)(2,1)} %refs_5_.5), custom_call_target="tpu_custom_call" | custom-call | flops 201326592 | bytes 393216 | tf_op jit(solution)/shard_map/units_back/pallas_call | solution.py:548
  236.8 3.0 fusion.79
  241.3 7.0 %collective-permute-start.27 = (bf16[128,2560]{1,0:T(8,128)(2,1)}, bf16[128,2560]{1,0:T(8,128)(2,1)S(1)}, u32[]{:S(2)}, u32[]{:S(2)}) collective-permute-start(bf16[128,2560]{1,0:T(8,128)(2,1)} %collective-permute-done.17.refs_2_.refs_8_), channel_id=1, source_target_pairs={{8,0},{16,8},{24,16},{0,24},{9,1},{17,9},{25,17},{1,25},{10,2},{18... | collective-permute-start | bytes 1966088 | tf_op jit(solution)/shard_map/ppermute | solution.py:33
  249.4 7.7 %collective-permute-done.23 = bf16[2,4,2,80,256]{4,3,2,1,0:T(8,128)(2,1)} collective-permute-done((bf16[2,4,2,80,256]{4,3,2,1,0:T(8,128)(2,1)S(1)}, bf16[2,4,2,80,256]{4,3,2,1,0:T(8,128)(2,1)}, u32[]{:S(2)}, u32[]{:S(2)}) %collective-permute-start.23) | collective-permute-done | bytes 655392 | tf_op jit(solution)/shard_map/ppermute | solution.py:22
  260.8 10.0 %units_made.1 = bf16[512,2560]{1,0:T(8,128)(2,1)} custom-call(bf16[512,1920]{1,0:T(8,128)(2,1)} %get-tuple-element.414.hidden.refs_10_, bf16[1920,2560]{1,0:T(8,128)(2,1)} %refs_4_.9), custom_call_target="tpu_custom_call" | custom-call | flops 100663296 | bytes 196608 | tf_op jit(solution)/shard_map/units_made/pallas_call | solution.py:568
  273.1 7.1 %collective-permute-done.28.refs_3_ = bf16[128,2560]{1,0:T(8,128)(2,1)S(1)} collective-permute-done((bf16[128,2560]{1,0:T(8,128)(2,1)}, bf16[128,2560]{1,0:T(8,128)(2,1)S(1)}, u32[]{:S(2)}, u32[]{:S(2)}) %collective-permute-start.28) | collective-permute-done | bytes 655392 | tf_op jit(solution)/shard_map/ppermute | solution.py:33
  280.2 2.5 multiply_reduce_fusion
  282.7 3.0 fusion.74
  290.6 9.3 %share_pull.2.refs_6_ = bf16[768,1024]{1,0:T(8,128)(2,1)} custom-call(s32[3]{0:T(128)} %pad_add_fusion.places, bf16[4,128,2560]{2,1,0:T(8,128)(2,1)} %all-gather.7.cloned.1.call-done.refs_0_, bf16[128,2560]{1,0:T(8,128)(2,1)} %collective-permute-done.19.refs_1_, bf16[128,2560]{1,0:T(8,128)(2,1)} %collective-permute-done.24.refs_2_, ...), custom_call_target="tpu_custom_call" | custom-call | flops 80530640 | bytes 104857 | tf_op jit(solution)/shard_map/share_pull/pallas_call | solution.py:641
  303.7 5.0 fusion.21
  313.8 9.4 %share_pull.3.refs_6_ = bf16[768,1024]{1,0:T(8,128)(2,1)} custom-call(s32[3]{0:T(128)} %pad_add_fusion.places, bf16[4,128,2560]{2,1,0:T(8,128)(2,1)} %collective-permute-done.34.refs_0_.refs_4_, bf16[128,2560]{1,0:T(8,128)(2,1)} %copy-done.25, bf16[128,2560]{1,0:T(8,128)(2,1)} %copy-done.26, bf16[128,2560]{1,0:T(8,128)(2,1)} %copy-done.27, ...), custom_call_target="tpu_custom_call" | custom-call | flops 80530640 | bytes 104857 | tf_op jit(solution)/shard_map/share_pull/pallas_call | solution.py:641
  323.2 3.1 collective-permute-done.31
  327.7 7.8 %unroll.1 = (bf16[2,64,2560]{2,1,0:T(8,128)(2,1)}, f32[2,64,2560]{2,1,0:T(8,128)}, f32[2,64,2560]{2,1,0:T(8,128)}, f32[4,2560]{1,0:T(4,128)}) custom-call(f32[2,64,2560]{2,1,0:T(8,128)} %pad_maximum_fusion.2.mixed_grad, f32[2,64,2560]{2,1,0:T(8,128)} %bitcast.167, bf16[2,64,2560]{2,1,0:T(8,128)(2,1)} %bitcast.189, ...), custom_call_target="tpu_custom_call" | custom-call | flops 1310720 | bytes 262144 | tf_op jit(solution)/shard_map/unroll/pallas_call | solution.py:310
  345.4 16.1 %share.2 = (bf16[768,1024]{1,0:T(8,128)(2,1)}, bf16[768,1024]{1,0:T(8,128)(2,1)}, bf16[768,1024]{1,0:T(8,128)(2,1)}) custom-call(s32[3]{0:T(128)} %pad_add_fusion.places, bf16[4,128,2560]{2,1,0:T(8,128)(2,1)} %bitcast.21.refs_0_, bf16[128,2560]{1,0:T(8,128)(2,1)} %copy-done.6, bf16[128,2560]{1,0:T(8,128)(2,1)} %collective-permute-done.33.refs_2_, ...), custom_call_target="tpu_custom_call" | custom-call | flops 161061280 | bytes 209715 | tf_op jit(solution)/shard_map/share/pallas_call | solution.py:641
  363.4 9.9 %recur_back.1 = (f32[2,64,2560]{2,1,0:T(8,128)}, f32[2,8,2560]{2,1,0:T(8,128)}, bf16[2560,256]{1,0:T(8,128)(2,1)}, bf16[2560,256]{1,0:T(8,128)(2,1)}, f32[8,2560]{1,0:T(8,128)}) custom-call(f32[2,64,2560]{2,1,0:T(8,128)} %get-tuple-element.362.behind, f32[2,64,2560]{2,1,0:T(8,128)} %get-tuple-element.363.local_grad, f32[2,1,2560]{2,1,0:T(1,128)} %copy.93.carry_back, ...), custom_call_target="tpu_custom_call" | custom-call | flops 1966080 | bytes 327680 | tf_op jit(solution)/shard_map/recur_back/pallas_call | solution.py:420
  374.8 6.7 %token_grad.3 = bf16[320,2560]{1,0:T(8,128)(2,1)} custom-call(bf16[128,2560]{1,0:T(8,128)(2,1)} %copy-done.32, bf16[128,2560]{1,0:T(8,128)(2,1)} %collective-permute-done.29.refs_1_, bf16[128,2560]{1,0:T(8,128)(2,1)} %collective-permute-done.30.refs_2_, bf16[128,2560]{1,0:T(8,128)(2,1)} %collective-permute-done.32.refs_3_, bf16[128,2560]{1,0:T(8,128)(2,1)} %copy-done.43, ...), custom_call_target="tpu_custom_call" | custom-call | flops 33554432 | bytes 131072 | tf_op jit(solution)/shard_map/token_grad/pallas_call | solution.py:846
  389.7 3.5 collective-permute-done.50
  393.2 2.3 add_convert_fusion.7
  398.5 2.6 add_convert_fusion
  402.7 16.1 %share.3 = (bf16[768,1024]{1,0:T(8,128)(2,1)}, bf16[768,1024]{1,0:T(8,128)(2,1)}, bf16[768,1024]{1,0:T(8,128)(2,1)}) custom-call(s32[3]{0:T(128)} %pad_add_fusion.places, bf16[4,128,2560]{2,1,0:T(8,128)(2,1)} %collective-permute-done.40.refs_0_.refs_4_, bf16[128,2560]{1,0:T(8,128)(2,1)} %collective-permute-done.41.refs_1_.refs_5_, ...), custom_call_target="tpu_custom_call" | custom-call | flops 161061280 | bytes 209715 | tf_op jit(solution)/shard_map/share/pallas_call | solution.py:641
  419.8 7.2 %collective-permute-done.57.refs_2_ = bf16[128,2560]{1,0:T(8,128)(2,1)} collective-permute-done((bf16[128,2560]{1,0:T(8,128)(2,1)}, bf16[128,2560]{1,0:T(8,128)(2,1)}, u32[]{:S(2)}, u32[]{:S(2)}) %collective-permute-start.57) | collective-permute-done | bytes 655392 | tf_op jit(solution)/shard_map/ppermute | solution.py:22
  427.0 5.2 fusion.12
  432.2 4.2 fusion.18
  439.3 11.6 %unit_grad.3 = (f32[2,320,1024]{2,1,0:T(8,128)}, bf16[2,320,1024]{2,1,0:T(8,128)(2,1)}) custom-call(s32[3]{0:T(128)} %pad_add_fusion.places, bf16[4,128,2560]{2,1,0:T(8,128)(2,1)} %all-gather.7.cloned.1.call-done.refs_0_, bf16[128,2560]{1,0:T(8,128)(2,1)} %collective-permute-done.19.refs_1_, bf16[128,2560]{1,0:T(8,128)(2,1)} %collective-permute-done.24.refs_2_, ...), custom_call_target="tpu_custom_call" | custom-call | flops 107374184 | bytes 83886 | tf_op jit(solution)/shard_map/unit_grad/pallas_call | solution.py:725
  452.8 8.2 %collective-permute-done.62.refs_3_ = bf16[128,2560]{1,0:T(8,128)(2,1)} collective-permute-done((bf16[128,2560]{1,0:T(8,128)(2,1)}, bf16[128,2560]{1,0:T(8,128)(2,1)}, u32[]{:S(2)}, u32[]{:S(2)}) %collective-permute-start.62) | collective-permute-done | bytes 655392 | tf_op jit(solution)/shard_map/ppermute | solution.py:22
  463.3 6.6 %token_grad.4 = bf16[320,2560]{1,0:T(8,128)(2,1)} custom-call(bf16[128,2560]{1,0:T(8,128)(2,1)} %bitcast.201, bf16[128,2560]{1,0:T(8,128)(2,1)} %collective-permute-done.45.refs_1_, bf16[128,2560]{1,0:T(8,128)(2,1)} %copy-done.42, bf16[128,2560]{1,0:T(8,128)(2,1)} %collective-permute-done.58.refs_3_, bf16[128,2560]{1,0:T(8,128)(2,1)} %collective-permute-done.68.refs_4_, ...), custom_call_target="tpu_custom_call" | custom-call | flops 33554432 | bytes 131072 | tf_op jit(solution)/shard_map/token_grad/pallas_call | solution.py:846
  470.2 2.6 fusion.78
  476.2 11.9 %unit_grad.4 = (f32[2,320,1024]{2,1,0:T(8,128)}, bf16[2,320,1024]{2,1,0:T(8,128)(2,1)}) custom-call(s32[3]{0:T(128)} %pad_add_fusion.places, bf16[4,128,2560]{2,1,0:T(8,128)(2,1)} %bitcast.21.refs_0_, bf16[128,2560]{1,0:T(8,128)(2,1)} %copy-done.6, bf16[128,2560]{1,0:T(8,128)(2,1)} %collective-permute-done.33.refs_2_, bf16[128,2560]{1,0:T(8,128)(2,1)} %copy-done.8, ...), custom_call_target="tpu_custom_call" | custom-call | flops 107374184 | bytes 83886 | tf_op jit(solution)/shard_map/unit_grad/pallas_call | solution.py:725
  490.7 2.5 fusion.33
  495.7 6.7 %token_grad.5 = bf16[320,2560]{1,0:T(8,128)(2,1)} custom-call(bf16[128,2560]{1,0:T(8,128)(2,1)} %bitcast.43.refs_0_, bf16[128,2560]{1,0:T(8,128)(2,1)} %collective-permute-done.56.refs_1_, bf16[128,2560]{1,0:T(8,128)(2,1)} %collective-permute-done.57.refs_2_, bf16[128,2560]{1,0:T(8,128)(2,1)} %collective-permute-done.62.refs_3_, ...), custom_call_target="tpu_custom_call" | custom-call | flops 33554432 | bytes 131072 | tf_op jit(solution)/shard_map/token_grad/pallas_call | solution.py:846
  502.5 2.4 collective-permute-done.60
  507.5 2.1 collective-permute-start.76
  509.6 11.6 %unit_grad.5 = (f32[2,320,1024]{2,1,0:T(8,128)}, bf16[2,320,1024]{2,1,0:T(8,128)(2,1)}) custom-call(s32[3]{0:T(128)} %pad_add_fusion.places, bf16[4,128,2560]{2,1,0:T(8,128)(2,1)} %bitcast.21.refs_0_, bf16[128,2560]{1,0:T(8,128)(2,1)} %copy-done.6, bf16[128,2560]{1,0:T(8,128)(2,1)} %collective-permute-done.33.refs_2_, bf16[128,2560]{1,0:T(8,128)(2,1)} %copy-done.8, ...), custom_call_target="tpu_custom_call" | custom-call | flops 107374184 | bytes 83886 | tf_op jit(solution)/shard_map/unit_grad/pallas_call | solution.py:725
  524.6 17.1 %collective-permute-done.73 = bf16[2,320,1024]{2,1,0:T(8,128)(2,1)} collective-permute-done((bf16[2,320,1024]{2,1,0:T(8,128)(2,1)}, bf16[2,320,1024]{2,1,0:T(8,128)(2,1)}, u32[]{:S(2)}, u32[]{:S(2)}) %collective-permute-start.73) | collective-permute-done | bytes 1310752 | tf_op jit(solution)/shard_map/ppermute | solution.py:22
  541.7 2.6 add_convert_fusion.2
  545.2 22.3 %collective-permute-done.72 = bf16[2,320,1024]{2,1,0:T(8,128)(2,1)} collective-permute-done((bf16[2,320,1024]{2,1,0:T(8,128)(2,1)}, bf16[2,320,1024]{2,1,0:T(8,128)(2,1)}, u32[]{:S(2)}, u32[]{:S(2)}) %collective-permute-start.72) | collective-permute-done | bytes 1310752 | tf_op jit(solution)/shard_map/ppermute | solution.py:22
  573.2 2.5 collective-permute-done.78
  579.7 5.4 collective-permute-start.80
  587.6 2.7 collective-permute-start.83
  591.1 3.3 collective-permute-done.75
  594.4 2.2 add_convert_fusion.5
  596.6 9.3 %collective-permute-done.83 = bf16[320,1024]{1,0:T(8,128)(2,1)S(1)} collective-permute-done((bf16[320,1024]{1,0:T(8,128)(2,1)S(1)}, bf16[320,1024]{1,0:T(8,128)(2,1)S(1)}, u32[]{:S(2)}, u32[]{:S(2)}) %collective-permute-start.83) | collective-permute-done | bytes 655392 | tf_op jit(solution)/shard_map/ppermute | solution.py:38
  607.7 8.9 %collective-permute-done.84 = bf16[320,1024]{1,0:T(8,128)(2,1)S(1)} collective-permute-done((bf16[320,1024]{1,0:T(8,128)(2,1)S(1)}, bf16[320,1024]{1,0:T(8,128)(2,1)S(1)}, u32[]{:S(2)}, u32[]{:S(2)}) %collective-permute-start.84) | collective-permute-done | bytes 655392 | tf_op jit(solution)/shard_map/ppermute | solution.py:38
  (403 shorter events, 132.9 us)
Async XLA Ops:
  7.2 51.0 %all-gather.5.cloned.1.call-start = ((), (), s32[]{:S(2)}) async-start(), calls=%async_computation.3 | async-start | bytes 3276800 | tf_op jit(solution)/shard_map/all_gather | solution.py:934
  7.3 16.3 %collective-permute-start.1 = (bf16[640,2560]{1,0:T(8,128)(2,1)}, bf16[640,2560]{1,0:T(8,128)(2,1)}, u32[]{:S(2)}, u32[]{:S(2)}) collective-permute-start(bf16[640,2560]{1,0:T(8,128)(2,1)} %param.22), channel_id=1, source_target_pairs={{0,1},{1,0},{2,3},{3,2},{4,5},{5,4},{6,7},{7,6},{8,9},{9,8},{10,11... | collective-permute-start | bytes 9830408 | tf_op jit(solution)/shard_map/ppermute | solution.py:22
  7.8 22.1 %collective-permute-start.3 = (bf16[640,2560]{1,0:T(8,128)(2,1)}, bf16[640,2560]{1,0:T(8,128)(2,1)}, u32[]{:S(2)}, u32[]{:S(2)}) collective-permute-start(bf16[640,2560]{1,0:T(8,128)(2,1)} %param.23), channel_id=1, source_target_pairs={{0,1},{1,0},{2,3},{3,2},{4,5},{5,4},{6,7},{7,6},{8,9},{9,8},{10,11... | collective-permute-start | bytes 9830408 | tf_op jit(solution)/shard_map/ppermute | solution.py:22
  9.8 105.9 %all-gather.7.cloned.1.call-start = ((), (), s32[]{:S(2)}) async-start(), calls=%async_computation.4 | async-start | bytes 3276800 | tf_op jit(solution)/shard_map/all_gather | solution.py:936
  27.2 23.8 %collective-permute-start.2 = (bf16[128,2560]{1,0:T(8,128)(2,1)S(1)}, bf16[128,2560]{1,0:T(8,128)(2,1)S(1)}, u32[]{:S(2)}, u32[]{:S(2)}) collective-permute-start(bf16[128,2560]{1,0:T(8,128)(2,1)S(1)} %slice.793), channel_id=1, source_target_pairs={{0,2},{2,0},{1,3},{3,1},{4,6},{6,4},{5,7},{7,5},{8,10},{10,8},{9,1... | collective-permute-start | bytes 1966088 | tf_op jit(solution)/shard_map/ppermute | solution.py:22
  54.4 61.3 %collective-permute-start.11 = (bf16[640,2560]{1,0:T(8,128)(2,1)}, bf16[640,2560]{1,0:T(8,128)(2,1)}, u32[]{:S(2)}, u32[]{:S(2)}) collective-permute-start(bf16[640,2560]{1,0:T(8,128)(2,1)} %param.31), channel_id=1, source_target_pairs={{0,1},{1,0},{2,3},{3,2},{4,5},{5,4},{6,7},{7,6},{8,9},{9,8},{10,11... | collective-permute-start | bytes 9830408 | tf_op jit(solution)/shard_map/ppermute | solution.py:22
  54.5 75.2 %collective-permute-start.14 = (bf16[128,2560]{1,0:T(8,128)(2,1)}, bf16[128,2560]{1,0:T(8,128)(2,1)}, u32[]{:S(2)}, u32[]{:S(2)}) collective-permute-start(bf16[128,2560]{1,0:T(8,128)(2,1)} %bitcast.9.refs_0_), channel_id=1, source_target_pairs={{0,1},{1,0},{2,3},{3,2},{4,5},{5,4},{6,7},{7,6},{8,9},{9,8},{10,11... | collective-permute-start | bytes 1966088 | tf_op jit(solution)/shard_map/ppermute | solution.py:22
  55.0 202.0 %all-gather.9.cloned.1.call-start = ((), (), s32[]{:S(2)}) async-start(), calls=%async_computation.8 | async-start | bytes 3276800 | tf_op jit(solution)/shard_map/all_gather | solution.py:996
  75.1 16.5 %collective-permute-start.9 = (bf16[128,2560]{1,0:T(8,128)(2,1)S(1)}, bf16[128,2560]{1,0:T(8,128)(2,1)S(1)}, u32[]{:S(2)}, u32[]{:S(2)}) collective-permute-start(bf16[128,2560]{1,0:T(8,128)(2,1)S(1)} %copy-done.36), channel_id=1, source_target_pairs={{0,2},{2,0},{1,3},{3,1},{4,6},{6,4},{5,7},{7,5},{8,10},{10,8},{9,1... | collective-permute-start | bytes 1966088 | tf_op jit(solution)/shard_map/ppermute | solution.py:22
  76.7 19.7 %collective-permute-start.6 = (f32[4,2560]{1,0:T(4,128)S(1)}, f32[4,2560]{1,0:T(4,128)S(1)}, u32[]{:S(2)}, u32[]{:S(2)}) collective-permute-start(f32[4,2560]{1,0:T(4,128)S(1)} %pad_maximum_fusion.12), channel_id=1, source_target_pairs={{0,8},{8,16},{16,24},{1,9},{9,17},{17,25},{2,10},{10,18},{18,26},{... | collective-permute-start | bytes 122888 | tf_op jit(solution)/shard_map/ppermute | solution.py:28
  80.2 17.8 %collective-permute-start.7 = (f32[4,2560]{1,0:T(4,128)S(1)}, f32[4,2560]{1,0:T(4,128)S(1)}, u32[]{:S(2)}, u32[]{:S(2)}) collective-permute-start(f32[4,2560]{1,0:T(4,128)S(1)} %pad_maximum_fusion.12), channel_id=1, source_target_pairs={{0,16},{8,24},{1,17},{9,25},{2,18},{10,26},{3,19},{11,27},{4,20},{... | collective-permute-start | bytes 122888 | tf_op jit(solution)/shard_map/ppermute | solution.py:28
  96.5 18.1 %collective-permute-start.12 = (bf16[128,2560]{1,0:T(8,128)(2,1)}, bf16[128,2560]{1,0:T(8,128)(2,1)}, u32[]{:S(2)}, u32[]{:S(2)}) collective-permute-start(bf16[128,2560]{1,0:T(8,128)(2,1)} %bitcast.9.refs_0_), channel_id=1, source_target_pairs={{0,2},{2,0},{1,3},{3,1},{4,6},{6,4},{5,7},{7,5},{8,10},{10,8},{9,1... | collective-permute-start | bytes 1966088 | tf_op jit(solution)/shard_map/ppermute | solution.py:22
  99.1 20.3 %collective-permute-start.10 = (bf16[128,1280]{1,0:T(8,128)(2,1)S(1)}, bf16[128,1280]{1,0:T(8,128)(2,1)}, u32[]{:S(2)}, u32[]{:S(2)}) collective-permute-start(bf16[128,1280]{1,0:T(8,128)(2,1)S(1)} %pad_maximum_fusion.10), channel_id=1, source_target_pairs={{0,2},{2,0},{1,3},{3,1},{4,6},{6,4},{5,7},{7,5},{8,10},{10,8},{9,1... | collective-permute-start | bytes 983048 | tf_op jit(solution)/shard_map/ppermute | solution.py:22
  114.5 15.2 %collective-permute-start.15 = (bf16[128,2560]{1,0:T(8,128)(2,1)}, bf16[128,2560]{1,0:T(8,128)(2,1)S(1)}, u32[]{:S(2)}, u32[]{:S(2)}) collective-permute-start(bf16[128,2560]{1,0:T(8,128)(2,1)} %collective-permute-done.12.refs_2_.refs_8_), channel_id=1, source_target_pairs={{0,1},{1,0},{2,3},{3,2},{4,5},{5,4},{6,7},{7,6},{8,9},{9,8},{10,11... | collective-permute-start | bytes 1966088 | tf_op jit(solution)/shard_map/ppermute | solution.py:22
  128.2 14.7 %collective-permute-start.13 = (bf16[128,2560]{1,0:T(8,128)(2,1)S(1)}, bf16[128,2560]{1,0:T(8,128)(2,1)S(1)}, u32[]{:S(2)}, u32[]{:S(2)}) collective-permute-start(bf16[128,2560]{1,0:T(8,128)(2,1)S(1)} %slice.791), channel_id=1, source_target_pairs={{0,2},{2,0},{1,3},{3,1},{4,6},{6,4},{5,7},{7,5},{8,10},{10,8},{9,1... | collective-permute-start | bytes 1966088 | tf_op jit(solution)/shard_map/ppermute | solution.py:22
  144.3 316.7 %reduce-scatter.4.cloned.1.call-start = ((), (), s32[]{:S(2)}) async-start(), calls=%async_computation.5 | async-start | bytes 2048000 | tf_op jit(solution)/shard_map/reduce_scatter | solution.py:884
  144.4 49.0 %collective-permute-start.19 = (bf16[128,2560]{1,0:T(8,128)(2,1)}, bf16[128,2560]{1,0:T(8,128)(2,1)}, u32[]{:S(2)}, u32[]{:S(2)}) collective-permute-start(bf16[128,2560]{1,0:T(8,128)(2,1)} %collective-permute-done.12.refs_2_.refs_8_), channel_id=1, source_target_pairs={{8,0},{16,8},{24,16},{0,24},{9,1},{17,9},{25,17},{1,25},{10,2},{18... | collective-permute-start | bytes 1966088 | tf_op jit(solution)/shard_map/ppermute | solution.py:33
  144.4 49.0 %collective-permute-start.20 = (bf16[128,2560]{1,0:T(8,128)(2,1)}, bf16[128,2560]{1,0:T(8,128)(2,1)}, u32[]{:S(2)}, u32[]{:S(2)}) collective-permute-start(bf16[128,2560]{1,0:T(8,128)(2,1)} %collective-permute-done.12.refs_2_.refs_8_), channel_id=1, source_target_pairs={{24,0},{0,8},{8,16},{16,24},{25,1},{1,9},{9,17},{17,25},{26,2},{2,... | collective-permute-start | bytes 1966088 | tf_op jit(solution)/shard_map/ppermute | solution.py:33
  146.9 46.5 %collective-permute-start.17 = (bf16[128,2560]{1,0:T(8,128)(2,1)}, bf16[128,2560]{1,0:T(8,128)(2,1)}, u32[]{:S(2)}, u32[]{:S(2)}) collective-permute-start(bf16[128,2560]{1,0:T(8,128)(2,1)} %multiply_convert_fusion.refs_0_), channel_id=1, source_target_pairs={{0,2},{2,0},{1,3},{3,1},{4,6},{6,4},{5,7},{7,5},{8,10},{10,8},{9,1... | collective-permute-start | bytes 1966088 | tf_op jit(solution)/shard_map/ppermute | solution.py:22
  150.0 45.9 %collective-permute-start.16 = (bf16[128,2560]{1,0:T(8,128)(2,1)}, bf16[128,2560]{1,0:T(8,128)(2,1)}, u32[]{:S(2)}, u32[]{:S(2)}) collective-permute-start(bf16[128,2560]{1,0:T(8,128)(2,1)} %multiply_convert_fusion.refs_0_), channel_id=1, source_target_pairs={{0,1},{1,0},{2,3},{3,2},{4,5},{5,4},{6,7},{7,6},{8,9},{9,8},{10,11... | collective-permute-start | bytes 1966088 | tf_op jit(solution)/shard_map/ppermute | solution.py:22
  194.4 20.8 %collective-permute-start.21 = (bf16[4,2,2,80,256]{4,3,2,1,0:T(8,128)(2,1)}, bf16[4,2,2,80,256]{4,3,2,1,0:T(8,128)(2,1)}, u32[]{:S(2)}, u32[]{:S(2)}) collective-permute-start(bf16[4,2,2,80,256]{4,3,2,1,0:T(8,128)(2,1)} %fusion.60), channel_id=1, source_target_pairs={{0,2},{2,0},{1,3},{3,1},{4,6},{6,4},{5,7},{7,5},{8,10},{10,8},{9,1... | collective-permute-start | bytes 1966088 | tf_op jit(solution)/shard_map/ppermute | solution.py:22
  216.4 32.0 %collective-permute-start.24 = (bf16[128,2560]{1,0:T(8,128)(2,1)S(1)}, bf16[128,2560]{1,0:T(8,128)(2,1)}, u32[]{:S(2)}, u32[]{:S(2)}) collective-permute-start(bf16[128,2560]{1,0:T(8,128)(2,1)S(1)} %dynamic-slice_bitcast_fusion.1), channel_id=1, source_target_pairs={{0,2},{2,0},{1,3},{3,1},{4,6},{6,4},{5,7},{7,5},{8,10},{10,8},{9,1... | collective-permute-start | bytes 1966088 | tf_op jit(solution)/shard_map/ppermute | solution.py:22
  239.8 17.3 %collective-permute-start.23 = (bf16[2,4,2,80,256]{4,3,2,1,0:T(8,128)(2,1)S(1)}, bf16[2,4,2,80,256]{4,3,2,1,0:T(8,128)(2,1)}, u32[]{:S(2)}, u32[]{:S(2)}) collective-permute-start(bf16[2,4,2,80,256]{4,3,2,1,0:T(8,128)(2,1)S(1)} %fusion.59), channel_id=1, source_target_pairs={{0,4},{4,0},{1,5},{5,1},{2,6},{6,2},{3,7},{7,3},{8,12},{12,8},{9,1... | collective-permute-start | bytes 1966088 | tf_op jit(solution)/shard_map/ppermute | solution.py:22
  241.1 67.5 %collective-permute-start.34 = (bf16[4,128,2560]{2,1,0:T(8,128)(2,1)}, bf16[4,128,2560]{2,1,0:T(8,128)(2,1)}, u32[]{:S(2)}, u32[]{:S(2)}) collective-permute-start(bf16[4,128,2560]{2,1,0:T(8,128)(2,1)} %all-gather.7.cloned.1.call-done.refs_0_), channel_id=1, source_target_pairs={{0,1},{1,0},{2,3},{3,2},{4,5},{5,4},{6,7},{7,6},{8,9},{9,8},{10,11... | collective-permute-start | bytes 7864328 | tf_op jit(solution)/shard_map/ppermute | solution.py:22
  241.3 31.7 %collective-permute-start.27 = (bf16[128,2560]{1,0:T(8,128)(2,1)}, bf16[128,2560]{1,0:T(8,128)(2,1)S(1)}, u32[]{:S(2)}, u32[]{:S(2)}) collective-permute-start(bf16[128,2560]{1,0:T(8,128)(2,1)} %collective-permute-done.17.refs_2_.refs_8_), channel_id=1, source_target_pairs={{8,0},{16,8},{24,16},{0,24},{9,1},{17,9},{25,17},{1,25},{10,2},{18... | collective-permute-start | bytes 1966088 | tf_op jit(solution)/shard_map/ppermute | solution.py:33
  248.3 31.9 %collective-permute-start.28 = (bf16[128,2560]{1,0:T(8,128)(2,1)}, bf16[128,2560]{1,0:T(8,128)(2,1)S(1)}, u32[]{:S(2)}, u32[]{:S(2)}) collective-permute-start(bf16[128,2560]{1,0:T(8,128)(2,1)} %collective-permute-done.17.refs_2_.refs_8_), channel_id=1, source_target_pairs={{24,0},{0,8},{8,16},{16,24},{25,1},{1,9},{9,17},{17,25},{26,2},{2,... | collective-permute-start | bytes 1966088 | tf_op jit(solution)/shard_map/ppermute | solution.py:33
  249.4 23.7 %collective-permute-start.25 = (bf16[128,2560]{1,0:T(8,128)(2,1)}, bf16[128,2560]{1,0:T(8,128)(2,1)}, u32[]{:S(2)}, u32[]{:S(2)}) collective-permute-start(bf16[128,2560]{1,0:T(8,128)(2,1)} %get-tuple-element.559), channel_id=1, source_target_pairs={{0,1},{1,0},{2,3},{3,2},{4,5},{5,4},{6,7},{7,6},{8,9},{9,8},{10,11... | collective-permute-start | bytes 1966088 | tf_op jit(solution)/shard_map/ppermute | solution.py:22
  258.5 21.7 %collective-permute-start.26 = (bf16[128,2560]{1,0:T(8,128)(2,1)S(1)}, bf16[128,2560]{1,0:T(8,128)(2,1)S(1)}, u32[]{:S(2)}, u32[]{:S(2)}) collective-permute-start(bf16[128,2560]{1,0:T(8,128)(2,1)S(1)} %add_convert_fusion.8), channel_id=1, source_target_pairs={{0,2},{2,0},{1,3},{3,1},{4,6},{6,4},{5,7},{7,5},{8,10},{10,8},{9,1... | collective-permute-start | bytes 1966088 | tf_op jit(solution)/shard_map/ppermute | solution.py:22
  285.7 16.2 %collective-permute-start.29 = (bf16[128,2560]{1,0:T(8,128)(2,1)S(1)}, bf16[128,2560]{1,0:T(8,128)(2,1)}, u32[]{:S(2)}, u32[]{:S(2)}) collective-permute-start(bf16[128,2560]{1,0:T(8,128)(2,1)S(1)} %get-tuple-element.378.refs_0_), channel_id=1, source_target_pairs={{0,2},{2,0},{1,3},{3,1},{4,6},{6,4},{5,7},{7,5},{8,10},{10,8},{9,1... | collective-permute-start | bytes 1966088 | tf_op jit(solution)/shard_map/ppermute | solution.py:22
  286.7 15.9 %collective-permute-start.30 = (bf16[128,2560]{1,0:T(8,128)(2,1)S(1)}, bf16[128,2560]{1,0:T(8,128)(2,1)}, u32[]{:S(2)}, u32[]{:S(2)}) collective-permute-start(bf16[128,2560]{1,0:T(8,128)(2,1)S(1)} %get-tuple-element.378.refs_0_), channel_id=1, source_target_pairs={{0,4},{4,0},{1,5},{5,1},{2,6},{6,2},{3,7},{7,3},{8,12},{12,8},{9,1... | collective-permute-start | bytes 1966088 | tf_op jit(solution)/shard_map/ppermute | solution.py:22
  288.1 22.3 %collective-permute-start.35 = (bf16[128,2560]{1,0:T(8,128)(2,1)}, bf16[128,2560]{1,0:T(8,128)(2,1)S(1)}, u32[]{:S(2)}, u32[]{:S(2)}) collective-permute-start(bf16[128,2560]{1,0:T(8,128)(2,1)} %collective-permute-done.19.refs_1_), channel_id=1, source_target_pairs={{0,1},{1,0},{2,3},{3,2},{4,5},{5,4},{6,7},{7,6},{8,9},{9,8},{10,11... | collective-permute-start | bytes 1966088 | tf_op jit(solution)/shard_map/ppermute | solution.py:22
  288.1 23.9 %collective-permute-start.36 = (bf16[128,2560]{1,0:T(8,128)(2,1)}, bf16[128,2560]{1,0:T(8,128)(2,1)S(1)}, u32[]{:S(2)}, u32[]{:S(2)}) collective-permute-start(bf16[128,2560]{1,0:T(8,128)(2,1)} %collective-permute-done.24.refs_2_), channel_id=1, source_target_pairs={{0,1},{1,0},{2,3},{3,2},{4,5},{5,4},{6,7},{7,6},{8,9},{9,8},{10,11... | collective-permute-start | bytes 1966088 | tf_op jit(solution)/shard_map/ppermute | solution.py:22
  302.6 20.6 %collective-permute-start.33 = (bf16[128,2560]{1,0:T(8,128)(2,1)}, bf16[128,2560]{1,0:T(8,128)(2,1)}, u32[]{:S(2)}, u32[]{:S(2)}) collective-permute-start(bf16[128,2560]{1,0:T(8,128)(2,1)} %dynamic-slice_bitcast_fusion), channel_id=1, source_target_pairs={{0,2},{2,0},{1,3},{3,1},{4,6},{6,4},{5,7},{7,5},{8,10},{10,8},{9,1... | collective-permute-start | bytes 1966088 | tf_op jit(solution)/shard_map/ppermute | solution.py:22
  308.6 17.7 %collective-permute-start.32 = (bf16[128,2560]{1,0:T(8,128)(2,1)}, bf16[128,2560]{1,0:T(8,128)(2,1)}, u32[]{:S(2)}, u32[]{:S(2)}) collective-permute-start(bf16[128,2560]{1,0:T(8,128)(2,1)} %collective-permute-done.29.refs_1_), channel_id=1, source_target_pairs={{0,4},{4,0},{1,5},{5,1},{2,6},{6,2},{3,7},{7,3},{8,12},{12,8},{9,1... | collective-permute-start | bytes 1966088 | tf_op jit(solution)/shard_map/ppermute | solution.py:22
  310.4 15.9 %collective-permute-start.31 = (bf16[2,128,640]{2,1,0:T(8,128)(2,1)}, bf16[2,128,640]{2,1,0:T(8,128)(2,1)S(1)}, u32[]{:S(2)}, u32[]{:S(2)}) collective-permute-start(bf16[2,128,640]{2,1,0:T(8,128)(2,1)} %fusion.47), channel_id=1, source_target_pairs={{0,2},{2,0},{1,3},{3,1},{4,6},{6,4},{5,7},{7,5},{8,10},{10,8},{9,1... | collective-permute-start | bytes 983048 | tf_op jit(solution)/shard_map/ppermute | solution.py:22
  336.4 25.7 %collective-permute-start.45 = (bf16[128,2560]{1,0:T(8,128)(2,1)}, bf16[128,2560]{1,0:T(8,128)(2,1)}, u32[]{:S(2)}, u32[]{:S(2)}) collective-permute-start(bf16[128,2560]{1,0:T(8,128)(2,1)} %bitcast.199), channel_id=1, source_target_pairs={{0,2},{2,0},{1,3},{3,1},{4,6},{6,4},{5,7},{7,5},{8,10},{10,8},{9,1... | collective-permute-start | bytes 1966088 | tf_op jit(solution)/shard_map/ppermute | solution.py:22
  337.4 25.1 %collective-permute-start.46 = (bf16[128,2560]{1,0:T(8,128)(2,1)}, bf16[128,2560]{1,0:T(8,128)(2,1)S(1)}, u32[]{:S(2)}, u32[]{:S(2)}) collective-permute-start(bf16[128,2560]{1,0:T(8,128)(2,1)} %bitcast.200), channel_id=1, source_target_pairs={{0,4},{4,0},{1,5},{5,1},{2,6},{6,2},{3,7},{7,3},{8,12},{12,8},{9,1... | collective-permute-start | bytes 1966088 | tf_op jit(solution)/shard_map/ppermute | solution.py:22
  341.1 20.3 %collective-permute-start.47 = (f32[4,2560]{1,0:T(4,128)S(1)}, f32[4,2560]{1,0:T(4,128)S(1)}, u32[]{:S(2)}, u32[]{:S(2)}) collective-permute-start(f32[4,2560]{1,0:T(4,128)S(1)} %pad_maximum_fusion.13), channel_id=1, source_target_pairs={{8,0},{16,8},{24,16},{9,1},{17,9},{25,17},{10,2},{18,10},{26,18},{... | collective-permute-start | bytes 122888 | tf_op jit(solution)/shard_map/ppermute | solution.py:28
  342.5 19.0 %collective-permute-start.48 = (f32[4,2560]{1,0:T(4,128)S(1)}, f32[4,2560]{1,0:T(4,128)S(1)}, u32[]{:S(2)}, u32[]{:S(2)}) collective-permute-start(f32[4,2560]{1,0:T(4,128)S(1)} %pad_maximum_fusion.13), channel_id=1, source_target_pairs={{16,0},{24,8},{17,1},{25,9},{18,2},{26,10},{19,3},{27,11},{20,4},{... | collective-permute-start | bytes 122888 | tf_op jit(solution)/shard_map/ppermute | solution.py:28
  343.8 18.2 %collective-permute-start.49 = (f32[4,2560]{1,0:T(4,128)S(1)}, f32[4,2560]{1,0:T(4,128)S(1)}, u32[]{:S(2)}, u32[]{:S(2)}) collective-permute-start(f32[4,2560]{1,0:T(4,128)S(1)} %pad_maximum_fusion.13), channel_id=1, source_target_pairs={{24,0},{25,1},{26,2},{27,3},{28,4},{29,5},{30,6},{31,7}} | collective-permute-start | bytes 122888 | tf_op jit(solution)/shard_map/ppermute | solution.py:28
  373.3 22.2 %collective-permute-start.40 = (bf16[4,128,2560]{2,1,0:T(8,128)(2,1)}, bf16[4,128,2560]{2,1,0:T(8,128)(2,1)}, u32[]{:S(2)}, u32[]{:S(2)}) collective-permute-start(bf16[4,128,2560]{2,1,0:T(8,128)(2,1)} %bitcast.21.refs_0_), channel_id=1, source_target_pairs={{0,1},{1,0},{2,3},{3,2},{4,5},{5,4},{6,7},{7,6},{8,9},{9,8},{10,11... | collective-permute-start | bytes 7864328 | tf_op jit(solution)/shard_map/ppermute | solution.py:22
  389.2 229.1 %reduce-scatter.8.cloned.1.call-start = ((), (), s32[]{:S(2)}) async-start(), calls=%async_computation.7 | async-start | bytes 2048000 | tf_op jit(solution)/shard_map/reduce_scatter | solution.py:884
  395.5 23.3 %collective-permute-start.58 = (bf16[128,2560]{1,0:T(8,128)(2,1)}, bf16[128,2560]{1,0:T(8,128)(2,1)}, u32[]{:S(2)}, u32[]{:S(2)}) collective-permute-start(bf16[128,2560]{1,0:T(8,128)(2,1)} %collective-permute-done.45.refs_1_), channel_id=1, source_target_pairs={{0,4},{4,0},{1,5},{5,1},{2,6},{6,2},{3,7},{7,3},{8,12},{12,8},{9,1... | collective-permute-start | bytes 1966088 | tf_op jit(solution)/shard_map/ppermute | solution.py:22
  397.2 22.6 %collective-permute-start.56 = (bf16[128,2560]{1,0:T(8,128)(2,1)}, bf16[128,2560]{1,0:T(8,128)(2,1)}, u32[]{:S(2)}, u32[]{:S(2)}) collective-permute-start(bf16[128,2560]{1,0:T(8,128)(2,1)} %bitcast.43.refs_0_), channel_id=1, source_target_pairs={{0,2},{2,0},{1,3},{3,1},{4,6},{6,4},{5,7},{7,5},{8,10},{10,8},{9,1... | collective-permute-start | bytes 1966088 | tf_op jit(solution)/shard_map/ppermute | solution.py:22
  398.2 28.8 %collective-permute-start.57 = (bf16[128,2560]{1,0:T(8,128)(2,1)}, bf16[128,2560]{1,0:T(8,128)(2,1)}, u32[]{:S(2)}, u32[]{:S(2)}) collective-permute-start(bf16[128,2560]{1,0:T(8,128)(2,1)} %bitcast.43.refs_0_), channel_id=1, source_target_pairs={{0,4},{4,0},{1,5},{5,1},{2,6},{6,2},{3,7},{7,3},{8,12},{12,8},{9,1... | collective-permute-start | bytes 1966088 | tf_op jit(solution)/shard_map/ppermute | solution.py:22
  402.2 61.1 %collective-permute-start.68 = (bf16[128,2560]{1,0:T(8,128)(2,1)S(1)}, bf16[128,2560]{1,0:T(8,128)(2,1)}, u32[]{:S(2)}, u32[]{:S(2)}) collective-permute-start(bf16[128,2560]{1,0:T(8,128)(2,1)S(1)} %bitcast.202), channel_id=1, source_target_pairs={{0,1},{1,0},{2,3},{3,2},{4,5},{5,4},{6,7},{7,6},{8,9},{9,8},{10,11... | collective-permute-start | bytes 1966088 | tf_op jit(solution)/shard_map/ppermute | solution.py:22
  402.2 61.1 %collective-permute-start.69 = (bf16[128,2560]{1,0:T(8,128)(2,1)}, bf16[128,2560]{1,0:T(8,128)(2,1)}, u32[]{:S(2)}, u32[]{:S(2)}) collective-permute-start(bf16[128,2560]{1,0:T(8,128)(2,1)} %collective-permute-done.45.refs_1_), channel_id=1, source_target_pairs={{0,1},{1,0},{2,3},{3,2},{4,5},{5,4},{6,7},{7,6},{8,9},{9,8},{10,11... | collective-permute-start | bytes 1966088 | tf_op jit(solution)/shard_map/ppermute | solution.py:22
  418.8 32.1 %collective-permute-start.63 = (bf16[4,2,80,640]{3,2,0,1:T(8,128)(2,1)S(1)}, bf16[4,2,80,640]{3,2,0,1:T(8,128)(2,1)S(1)}, u32[]{:S(2)}, u32[]{:S(2)}) collective-permute-start(bf16[4,2,80,640]{3,2,0,1:T(8,128)(2,1)S(1)} %get-tuple-element.564), channel_id=1, source_target_pairs={{0,2},{2,0},{1,3},{3,1},{4,6},{6,4},{5,7},{7,5},{8,10},{10,8},{9,1... | collective-permute-start | bytes 2457608 | tf_op jit(solution)/shard_map/ppermute | solution.py:22
  437.3 14.0 %collective-permute-start.61 = (bf16[2,128,640]{2,1,0:T(8,128)(2,1)}, bf16[2,128,640]{2,1,0:T(8,128)(2,1)}, u32[]{:S(2)}, u32[]{:S(2)}) collective-permute-start(bf16[2,128,640]{2,1,0:T(8,128)(2,1)} %fusion.45), channel_id=1, source_target_pairs={{0,2},{2,0},{1,3},{3,1},{4,6},{6,4},{5,7},{7,5},{8,10},{10,8},{9,1... | collective-permute-start | bytes 983048 | tf_op jit(solution)/shard_map/ppermute | solution.py:22
  438.3 22.7 %collective-permute-start.62 = (bf16[128,2560]{1,0:T(8,128)(2,1)}, bf16[128,2560]{1,0:T(8,128)(2,1)}, u32[]{:S(2)}, u32[]{:S(2)}) collective-permute-start(bf16[128,2560]{1,0:T(8,128)(2,1)} %collective-permute-done.57.refs_2_), channel_id=1, source_target_pairs={{0,2},{2,0},{1,3},{3,1},{4,6},{6,4},{5,7},{7,5},{8,10},{10,8},{9,1... | collective-permute-start | bytes 1966088 | tf_op jit(solution)/shard_map/ppermute | solution.py:22
  470.0 150.3 %reduce-scatter.6.cloned.1.call-start = ((), (), s32[]{:S(2)}) async-start(), calls=%async_computation.6 | async-start | bytes 2560000 | tf_op jit(solution)/shard_map/reduce_scatter | solution.py:884
  472.8 32.0 %collective-permute-start.60 = (bf16[2,320,1024]{2,1,0:T(8,128)(2,1)}, bf16[2,320,1024]{2,1,0:T(8,128)(2,1)}, u32[]{:S(2)}, u32[]{:S(2)}) collective-permute-start(bf16[2,320,1024]{2,1,0:T(8,128)(2,1)} %get-tuple-element.418), channel_id=1, source_target_pairs={{0,4},{4,0},{1,5},{5,1},{2,6},{6,2},{3,7},{7,3},{8,12},{12,8},{9,1... | collective-permute-start | bytes 3932168 | tf_op jit(solution)/shard_map/ppermute | solution.py:22
  475.6 17.6 %collective-permute-start.64 = (bf16[128,2560]{1,0:T(8,128)(2,1)}, bf16[128,2560]{1,0:T(8,128)(2,1)}, u32[]{:S(2)}, u32[]{:S(2)}) collective-permute-start(bf16[128,2560]{1,0:T(8,128)(2,1)} %bitcast.43.refs_0_), channel_id=1, source_target_pairs={{0,1},{1,0},{2,3},{3,2},{4,5},{5,4},{6,7},{7,6},{8,9},{9,8},{10,11... | collective-permute-start | bytes 1966088 | tf_op jit(solution)/shard_map/ppermute | solution.py:22
  475.6 17.6 %collective-permute-start.65 = (bf16[128,2560]{1,0:T(8,128)(2,1)}, bf16[128,2560]{1,0:T(8,128)(2,1)}, u32[]{:S(2)}, u32[]{:S(2)}) collective-permute-start(bf16[128,2560]{1,0:T(8,128)(2,1)} %collective-permute-done.56.refs_1_), channel_id=1, source_target_pairs={{0,1},{1,0},{2,3},{3,2},{4,5},{5,4},{6,7},{7,6},{8,9},{9,8},{10,11... | collective-permute-start | bytes 1966088 | tf_op jit(solution)/shard_map/ppermute | solution.py:22
  476.2 17.6 %collective-permute-start.66 = (bf16[128,2560]{1,0:T(8,128)(2,1)}, bf16[128,2560]{1,0:T(8,128)(2,1)}, u32[]{:S(2)}, u32[]{:S(2)}) collective-permute-start(bf16[128,2560]{1,0:T(8,128)(2,1)} %collective-permute-done.57.refs_2_), channel_id=1, source_target_pairs={{0,1},{1,0},{2,3},{3,2},{4,5},{5,4},{6,7},{7,6},{8,9},{9,8},{10,11... | collective-permute-start | bytes 1966088 | tf_op jit(solution)/shard_map/ppermute | solution.py:22
  493.2 77.2 %collective-permute-start.39 = (bf16[128,2560]{1,0:T(8,128)(2,1)}, bf16[128,2560]{1,0:T(8,128)(2,1)}, u32[]{:S(2)}, u32[]{:S(2)}) collective-permute-start(bf16[128,2560]{1,0:T(8,128)(2,1)} %get-tuple-element.555), channel_id=1, source_target_pairs={{0,1},{1,0},{2,3},{3,2},{4,5},{5,4},{6,7},{7,6},{8,9},{9,8},{10,11... | collective-permute-start | bytes 1966088 | tf_op jit(solution)/shard_map/ppermute | solution.py:22
  493.2 97.9 %collective-permute-start.38 = (bf16[128,2560]{1,0:T(8,128)(2,1)}, bf16[128,2560]{1,0:T(8,128)(2,1)}, u32[]{:S(2)}, u32[]{:S(2)}) collective-permute-start(bf16[128,2560]{1,0:T(8,128)(2,1)} %get-tuple-element.556), channel_id=1, source_target_pairs={{0,1},{1,0},{2,3},{3,2},{4,5},{5,4},{6,7},{7,6},{8,9},{9,8},{10,11... | collective-permute-start | bytes 1966088 | tf_op jit(solution)/shard_map/ppermute | solution.py:22
  493.7 27.5 %collective-permute-start.74 = (bf16[4,80,640]{2,1,0:T(8,128)(2,1)}, bf16[4,80,640]{2,1,0:T(8,128)(2,1)S(1)}, u32[]{:S(2)}, u32[]{:S(2)}) collective-permute-start(bf16[4,80,640]{2,1,0:T(8,128)(2,1)} %get-tuple-element.586), channel_id=1, source_target_pairs={{0,4},{4,0},{1,5},{5,1},{2,6},{6,2},{3,7},{7,3},{8,12},{12,8},{9,1... | collective-permute-start | bytes 1228808 | tf_op jit(solution)/shard_map/ppermute | solution.py:22
  494.1 47.6 %collective-permute-start.73 = (bf16[2,320,1024]{2,1,0:T(8,128)(2,1)}, bf16[2,320,1024]{2,1,0:T(8,128)(2,1)}, u32[]{:S(2)}, u32[]{:S(2)}) collective-permute-start(bf16[2,320,1024]{2,1,0:T(8,128)(2,1)} %get-tuple-element.466), channel_id=1, source_target_pairs={{0,4},{4,0},{1,5},{5,1},{2,6},{6,2},{3,7},{7,3},{8,12},{12,8},{9,1... | collective-permute-start | bytes 3932168 | tf_op jit(solution)/shard_map/ppermute | solution.py:22
  507.5 64.5 %collective-permute-start.76 = (bf16[320,1024]{1,0:T(8,128)(2,1)}, bf16[320,1024]{1,0:T(8,128)(2,1)}, u32[]{:S(2)}, u32[]{:S(2)}) collective-permute-start(bf16[320,1024]{1,0:T(8,128)(2,1)} %get-tuple-element.570), channel_id=1, source_target_pairs={{0,8},{8,0},{16,24},{24,16},{1,9},{9,1},{17,25},{25,17},{2,10},{10... | collective-permute-start | bytes 1966088 | tf_op jit(solution)/shard_map/ppermute | solution.py:38
  521.3 46.3 %collective-permute-start.72 = (bf16[2,320,1024]{2,1,0:T(8,128)(2,1)}, bf16[2,320,1024]{2,1,0:T(8,128)(2,1)}, u32[]{:S(2)}, u32[]{:S(2)}) collective-permute-start(bf16[2,320,1024]{2,1,0:T(8,128)(2,1)} %get-tuple-element.465), channel_id=1, source_target_pairs={{0,4},{4,0},{1,5},{5,1},{2,6},{6,2},{3,7},{7,3},{8,12},{12,8},{9,1... | collective-permute-start | bytes 3932168 | tf_op jit(solution)/shard_map/ppermute | solution.py:22
  578.6 15.8 %collective-permute-start.75 = (bf16[128,2560]{1,0:T(8,128)(2,1)S(1)}, bf16[128,2560]{1,0:T(8,128)(2,1)S(1)}, u32[]{:S(2)}, u32[]{:S(2)}) collective-permute-start(bf16[128,2560]{1,0:T(8,128)(2,1)S(1)} %add_convert_fusion.6), channel_id=1, source_target_pairs={{0,2},{2,0},{1,3},{3,1},{4,6},{6,4},{5,7},{7,5},{8,10},{10,8},{9,1... | collective-permute-start | bytes 1966088 | tf_op jit(solution)/shard_map/ppermute | solution.py:22
  587.6 18.3 %collective-permute-start.83 = (bf16[320,1024]{1,0:T(8,128)(2,1)S(1)}, bf16[320,1024]{1,0:T(8,128)(2,1)S(1)}, u32[]{:S(2)}, u32[]{:S(2)}) collective-permute-start(bf16[320,1024]{1,0:T(8,128)(2,1)S(1)} %copy-done.39), channel_id=1, source_target_pairs={{0,8},{8,0},{16,24},{24,16},{1,9},{9,1},{17,25},{25,17},{2,10},{10... | collective-permute-start | bytes 1966088 | tf_op jit(solution)/shard_map/ppermute | solution.py:38
  590.3 26.3 %collective-permute-start.84 = (bf16[320,1024]{1,0:T(8,128)(2,1)S(1)}, bf16[320,1024]{1,0:T(8,128)(2,1)S(1)}, u32[]{:S(2)}, u32[]{:S(2)}) collective-permute-start(bf16[320,1024]{1,0:T(8,128)(2,1)S(1)} %copy-done.38), channel_id=1, source_target_pairs={{0,8},{8,0},{16,24},{24,16},{1,9},{9,1},{17,25},{25,17},{2,10},{10... | collective-permute-start | bytes 1966088 | tf_op jit(solution)/shard_map/ppermute | solution.py:38
  (93 other events, 738.7 us)
Sparse Core Ops, SparseCore 0:
  10.2 36.0 all-gather.4
  55.1 55.0 all-gather.6
  144.4 70.4 all-gather.8
  389.3 40.2 reduce-scatter.3
  470.1 38.1 reduce-scatter.7
  524.7 43.1 reduce-scatter.5

commit v3 on v2

--- a/solution.py
+++ b/solution.py
@@ -61,11 +61,15 @@
 class Line:
     def __init__(self):
         self.last = None
+        self.held = []
 
     def __call__(self, *values):
-        if self.last is None:
-            return values
-        return lax.optimization_barrier((*values, self.last))[:-1]
+        others = self.held + ([] if self.last is None else [self.last])
+        self.held = []
+        return lax.optimization_barrier((*values, *others))[: len(values)]
+
+    def hold(self, *values):
+        self.held += values
 
     def mark(self, value):
         self.last = value
@@ -130,19 +134,17 @@
     )
 
 
-def project(recv, keep, w_own, w_oth):
+def project(recv, keep, weight):
     rows = recv.shape[0]
-    left = jnp.concatenate([recv, keep], axis=0)
-    total = dot(left, jnp.concatenate([w_own, w_oth], axis=0))
+    total = dot(jnp.concatenate([recv, keep], axis=0), weight)
     return total[:rows].astype(BF16), total[rows:]
 
 
 def project_back(terms):
     rows = terms[0][0].shape[0]
     total = 0.0
-    for recv, own, w_own, w_oth in terms:
-        left = jnp.concatenate([recv, own], axis=0)
-        total = total + dot_nt(left, jnp.concatenate([w_own, w_oth], axis=0))
+    for recv, own, weight in terms:
+        total = total + dot_nt(jnp.concatenate([recv, own], axis=0), weight)
     half = total.shape[1] // 2
     total = jnp.stack([total[:, :half], total[:, half:]])
     return total[:, :rows].astype(BF16), total[:, rows:]
@@ -535,8 +537,14 @@
     )(*pieces, w_down)
 
 
-def units_back_kernel(gate, up, w_gate, w_up, out):
-    out[...] = (dot_nt(gate[...], w_gate[...]) + dot_nt(up[...], w_up[...])).astype(BF16)
+def spill(total, outs):
+    rows = outs[0].shape[0]
+    for i, out in enumerate(outs):
+        out[...] = total[i * rows : (i + 1) * rows].astype(BF16)
+
+
+def units_back_kernel(gate, up, w_gate, w_up, *outs):
+    spill(dot_nt(gate[...], w_gate[...]) + dot_nt(up[...], w_up[...]), outs)
 
 
 def units_back(gate, up, w_gate, w_up):
@@ -549,16 +557,16 @@
         units_back_kernel,
         grid=(width // tile,),
         in_specs=[whole, whole, row, row],
-        out_specs=pl.BlockSpec((rows, tile), lambda j: (0, j)),
-        out_shape=jax.ShapeDtypeStruct((rows, width), BF16),
+        out_specs=[pl.BlockSpec((rows // 4, tile), lambda j: (0, j))] * 4,
+        out_shape=[jax.ShapeDtypeStruct((rows // 4, width), BF16)] * 4,
         compiler_params=params(),
         cost_estimate=cost(4 * rows * width * held, 4 * width * held),
         name="units_back",
     )(gate, up, w_gate, w_up)
 
 
-def units_made_kernel(hidden, w_down, out):
-    out[...] = dot(hidden[...], w_down[...]).astype(BF16)
+def units_made_kernel(hidden, w_down, *outs):
+    spill(dot(hidden[...], w_down[...]), outs)
 
 
 def units_made(hidden, w_down):
@@ -572,8 +580,8 @@
             pl.BlockSpec((rows, held), lambda j: (0, 0), pipeline_mode=pl.Buffered(1)),
             pl.BlockSpec((held, tile), lambda j: (0, j)),
         ],
-        out_specs=pl.BlockSpec((rows, tile), lambda j: (0, j)),
-        out_shape=jax.ShapeDtypeStruct((rows, width), BF16),
+        out_specs=[pl.BlockSpec((rows // 4, tile), lambda j: (0, j))] * 4,
+        out_shape=[jax.ShapeDtypeStruct((rows // 4, width), BF16)] * 4,
         compiler_params=params(),
         cost_estimate=cost(2 * rows * width * held, 2 * width * held),
         name="units_made",
@@ -585,42 +593,44 @@
     return width, held - width
 
 
-def others(places, gathered, pieces):
-    count = len(pieces)
-    return [gathered[(places[0] + j) % (count + 1)] for j in range(1, count + 1)] + [
-        p[...] for p in pieces
-    ]
+def at_distance(places, gathered, steps):
+    count = gathered[0].shape[0]
+    return [gathered[0][(places[0] + steps) % count], *[part[steps] for part in gathered[1:]]]
+
+
+def others(places, gathered):
+    count = gathered[0].shape[0]
+    return [v for steps in range(1, count) for v in at_distance(places, gathered, steps)]
 
 
 def share_pull_kernel(count, places, *refs):
-    gathered, pieces, (w_down, out, tokens) = refs[0], refs[1 : 1 + count], refs[1 + count :]
+    gathered, (w_down, out, tokens) = refs[:count], refs[count:]
 
     @pl.when(pl.program_id(0) == 0)
     def _():
-        fill(tokens, others(places, gathered, pieces))
+        fill(tokens, others(places, gathered))
 
     out[...] = dot_nt(tokens[...], w_down[...]).astype(BF16)
 
 
 def share_kernel(count, places, *refs):
-    gathered, pieces = refs[0], refs[1 : 1 + count]
-    w_gate, w_up, pulled, hidden_out, gate_out, up_out, tokens = refs[1 + count :]
+    gathered, refs = refs[:count], refs[count:]
+    w_gate, w_up, pulled, hidden_out, gate_out, up_out, tokens = refs
 
     @pl.when(pl.program_id(0) == 0)
     def _():
-        fill(tokens, others(places, gathered, pieces))
+        fill(tokens, others(places, gathered))
 
     gate_pre, up_pre = dot(tokens[...], w_gate[...]), dot(tokens[...], w_up[...])
     unit_step(gate_pre, up_pre, pulled[...].astype(F32), hidden_out, gate_out, up_out)
 
 
-def share_call(kernel, places, gathered, pieces, weights, more, outs, name):
-    count = len(pieces)
-    rows, width = pieces[0].shape
+def share_call(kernel, places, gathered, weights, more, outs, name):
+    count, rows, width = gathered[0].shape
     tile = 512
     held = weights[0].shape[0] if weights[0].shape[1] == width else weights[0].shape[1]
     window, offset = window_of(held)
-    total = 2 * count * rows
+    total = len(gathered) * (count - 1) * rows
     specs = []
     for weight in weights:
         if weight.shape[1] == width:
@@ -638,22 +648,15 @@
                 )
             )
     out = pl.BlockSpec((total, tile), lambda j, places: (0, j))
-    result = pl.pallas_call(
-        partial(kernel, count),
+    whole = pl.BlockSpec(
+        gathered[0].shape, lambda j, places: (0, 0, 0), pipeline_mode=pl.Buffered(1)
+    )
+    return pl.pallas_call(
+        partial(kernel, len(gathered)),
         grid_spec=pltpu.PrefetchScalarGridSpec(
             num_scalar_prefetch=1,
             grid=(window // tile,),
-            in_specs=[
-                pl.BlockSpec(
-                    gathered.shape, lambda j, places: (0, 0, 0), pipeline_mode=pl.Buffered(1)
-                )
-            ]
-            + [
-                pl.BlockSpec((rows, width), lambda j, places: (0, 0), pipeline_mode=pl.Buffered(1))
-            ]
-            * count
-            + specs
-            + [out] * len(more),
+            in_specs=[whole] * len(gathered) + specs + [out] * len(more),
             out_specs=[out] * outs,
             scratch_shapes=[pltpu.VMEM((total, width), BF16)],
         ),
@@ -663,32 +666,28 @@
             2 * len(weights) * total * width * window, 2 * len(weights) * width * window
         ),
         name=name,
-    )(places, gathered, *pieces, *weights, *more)
-    return result
-
-
-def share_pull(places, gathered, pieces, w_down):
-    return share_call(share_pull_kernel, places, gathered, pieces, [w_down], [], 1, "share_pull")[0]
-
-
-def share(places, gathered, pieces, w_gate, w_up, pulled):
-    return share_call(
-        share_kernel, places, gathered, pieces, [w_gate, w_up], [pulled], 3, "share"
-    )
+    )(places, *gathered, *weights, *more)
+
+
+def share_pull(places, gathered, w_down):
+    return share_call(share_pull_kernel, places, gathered, [w_down], [], 1, "share_pull")[0]
+
+
+def share(places, gathered, w_gate, w_up, pulled):
+    return share_call(share_kernel, places, gathered, [w_gate, w_up], [pulled], 3, "share")
 
 
 def unit_grad_kernel(count, kinds, places, *refs):
-    token_refs, refs = refs[: 2 * (1 + count)], refs[2 * (1 + count) :]
-    own_x, acts, outs = refs[:2], refs[2 : 2 + 3 * kinds], refs[2 + 3 * kinds : 2 + 5 * kinds]
-    left, whole = refs[2 + 5 * kinds :]
+    here, there, refs = refs[:count], refs[count : 2 * count], refs[2 * count :]
+    acts, outs = refs[: 3 * kinds], refs[3 * kinds : 5 * kinds]
+    left, whole = refs[5 * kinds :]
     block = whole.shape[0] // 2
-    here, there = token_refs[: 1 + count], token_refs[1 + count :]
-    me = places[0]
     fill(
         left,
-        [here[0][me], there[0][me], own_x[0][...], own_x[1][...]]
-        + others(places, here[0], here[1:])
-        + others(places, there[0], there[1:]),
+        at_distance(places, here, 0)
+        + at_distance(places, there, 0)
+        + others(places, here)
+        + others(places, there),
     )
     own = pl.multiple_of(places[2] * block, block)
     other = pl.multiple_of((1 - places[2]) * block, block)
@@ -705,29 +704,28 @@
         outs[2 * kind + 1][0] = whole[pl.ds(other, block)].astype(BF16)
 
 
-def unit_grad(places, here, there, own_x, acts):
-    count, kinds = len(here[1]), len(acts)
-    rows, features = own_x[0].shape
+def unit_grad(places, here, there, acts):
+    kinds = len(acts)
+    count, rows, features = here[0].shape
     window, offset = window_of(acts[0][0].shape[1])
-    width = features // (count + 1)
-    total = 4 * (count + 1) * rows
+    width = features // count
+    total = 2 * len(here) * count * rows
     once = pl.Buffered(1)
-    gathered = pl.BlockSpec((count + 1, rows, width), lambda i, p: (0, 0, 2 * (p[0] // 2) + i))
-    piece = pl.BlockSpec((rows, width), lambda i, p: (0, 2 * (p[0] // 2) + i))
+    gathered = pl.BlockSpec((count, rows, width), lambda i, p: (0, 0, 2 * (p[0] // 2) + i))
     mine = pl.BlockSpec(
-        (pl.Element(4 * rows), pl.Element(window)),
+        (pl.Element(2 * len(here) * rows), pl.Element(window)),
         lambda i, p: (0, pl.multiple_of(p[1] * offset, 128)),
         pipeline_mode=once,
     )
-    act = pl.BlockSpec((2 * count * rows, window), lambda i, p: (0, 0), pipeline_mode=once)
+    act = pl.BlockSpec(acts[0][1].shape, lambda i, p: (0, 0), pipeline_mode=once)
     out = pl.BlockSpec((1, width // 2, window), lambda i, p: (i, 0, 0))
     shape = (2, width // 2, window)
     return pl.pallas_call(
-        partial(unit_grad_kernel, count, kinds),
+        partial(unit_grad_kernel, len(here), kinds),
         grid_spec=pltpu.PrefetchScalarGridSpec(
             num_scalar_prefetch=1,
             grid=(2,),
-            in_specs=([gathered] + [piece] * count) * 2 + [piece] * 2 + [mine, act, act] * kinds,
+            in_specs=[gathered] * (2 * len(here)) + [mine, act, act] * kinds,
             out_specs=[out] * (2 * kinds),
             scratch_shapes=[
                 pltpu.VMEM((total, width), BF16),
@@ -738,7 +736,7 @@
         compiler_params=params(),
         cost_estimate=cost(4 * kinds * total * width * window, 2 * kinds * total * window),
         name="unit_grad",
-    )(places, here[0], *here[1], there[0], *there[1], *own_x, *[a for v in acts for a in v])
+    )(places, *here, *there, *[a for v in acts for a in v])
 
 
 def window_part(value, places, axis):
@@ -746,32 +744,32 @@
     return lax.dynamic_slice_in_dim(value, places[1] * offset, window, axis=axis)
 
 
-def others_plain(places, gathered, pieces):
-    count = len(pieces)
-    rolled = jnp.roll(gathered, -places[0], axis=0)[1:].reshape(-1, gathered.shape[2])
-    return jnp.concatenate([rolled, *pieces], axis=0)
-
-
-def share_pull_plain(places, gathered, pieces, w_down):
-    tokens = others_plain(places, gathered, pieces)
+def others_plain(places, gathered):
+    features = gathered[0].shape[2]
+    rolled = [jnp.roll(gathered[0], -places[0], axis=0), *gathered[1:]]
+    return jnp.concatenate([v[1:] for v in rolled], axis=1).reshape(-1, features)
+
+
+def share_pull_plain(places, gathered, w_down):
+    tokens = others_plain(places, gathered)
     return dot_nt(tokens, window_part(w_down, places, 0)).astype(BF16)
 
 
-def share_plain(places, gathered, pieces, w_gate, w_up, pulled):
-    tokens = others_plain(places, gathered, pieces)
+def share_plain(places, gathered, w_gate, w_up, pulled):
+    tokens = others_plain(places, gathered)
     act, slope = gelu_pair(dot(tokens, window_part(w_gate, places, 1)))
     up_pre = dot(tokens, window_part(w_up, places, 1))
     pulled = pulled.astype(F32)
     return [v.astype(BF16) for v in (act * up_pre, pulled * up_pre * slope, pulled * act)]
 
 
-def unit_grad_plain(places, here, there, own_x, acts):
-    features = own_x[0].shape[1]
-    block = features // (2 * (len(here[1]) + 1))
+def unit_grad_plain(places, here, there, acts):
+    count, _, features = here[0].shape
+    block = features // (2 * count)
     at = lambda v: lax.dynamic_index_in_dim(v, places[0], 0, keepdims=False)
-    tokens = [at(here[0]), at(there[0]), *own_x]
+    own = [v for part in (here, there) for v in (at(part[0]), *[w[0] for w in part[1:]])]
     tokens = jnp.concatenate(
-        tokens + [others_plain(places, *here), others_plain(places, *there)], axis=0
+        own + [others_plain(places, here), others_plain(places, there)], axis=0
     )
     tokens = lax.dynamic_slice_in_dim(tokens, places[0] // 2 * 4 * block, 4 * block, axis=1)
     outs = []
@@ -800,7 +798,8 @@
 
 def line_tree(line, *values):
     leaves, tree = jax.tree.flatten(values)
-    return jax.tree.unflatten(tree, line(*leaves))
+    arrays = iter(line(*[v for v in leaves if not isinstance(v, int)]))
+    return jax.tree.unflatten(tree, [v if isinstance(v, int) else next(arrays) for v in leaves])
 
 
 def tied_carry(line, other, arrived):
@@ -856,28 +855,25 @@
     )(*pieces, near, away)
 
 
-def total_of_all(value):
+def total_of_all(value, line):
     far = lax.axis_size(SZ)
     held = value.reshape(far, 2, 2, 2, -1)
     for place, axis in ((3, WC), (2, WX), (1, SY)):
-        bit = lax.axis_index(axis)
-        low, high = (lax.index_in_dim(held, i, place, keepdims=False) for i in (0, 1))
-        held = pick(bit, low, high) + swap(pick(bit, high, low), axis)
+        mine, send = rows_for(axis, place, held)
+        got = swap(line.mark(send), axis)
+        yield
+        mine, got = line(mine, got)
+        held = mine + got
     here = lax.axis_index(SZ)
     mine = lax.dynamic_index_in_dim(held, here, 0, keepdims=False)
-    for steps in range(1, far):
-        block = lax.dynamic_index_in_dim(held, (here - steps) % far, 0, keepdims=False)
-        mine = mine + around(block, steps)
-    return mine
-
-
-def join_gates(own, core, x_part, both, wx, wc):
-    parts = [[pick(wc, p, q), pick(wc, q, p)] for p, q in ((own, core), (x_part, both))]
-    return jnp.concatenate(
-        [pick(wx, parts[0][i], parts[1][i]) for i in (0, 1)]
-        + [pick(wx, parts[1][i], parts[0][i]) for i in (0, 1)],
-        axis=0,
-    )
+    blocks = [
+        lax.dynamic_index_in_dim(held, (here - steps) % far, 0, keepdims=False)
+        for steps in range(1, far)
+    ]
+    line.mark(mine)
+    blocks = [around(block, steps) for steps, block in enumerate(blocks, 1)]
+    yield
+    yield sum(line(*blocks), mine)
 
 
 def scatter_far(value):
@@ -929,12 +925,13 @@
         (share_pull_plain, share_plain, unit_grad_plain) if plain else (share_pull, share, unit_grad)
     )
 
-    oth_x, oth_y, oth_out = swap(w_x, WC), swap(w_y, WC), swap(w_out, WC)
+    joined_rows = lambda own, other: jnp.concatenate([own, other], axis=0)
+    core = lambda value: swap(value, WC)
+    oth_x, oth_y, oth_out = core(w_x), core(w_y), core(w_out)
     own_gates = jnp.concatenate([gate_a, gate_i], axis=1)
     gates = lax.all_gather(own_gates, (WX, WC), axis=0, tiled=True)
     cot = flat(cotangent)
     cot_all = lax.all_gather(cot, SZ)
-    cot_core = swap(cot, WC)
     source = wide(flat(inputs))
     norm_scale = lax.rsqrt(jnp.mean(source * source, axis=-1, keepdims=True) + 1e-06)
     normed = low(source * norm_scale * gain)
@@ -943,13 +940,18 @@
     recv = swap(send, WX)
     normed_turned = line.mark(line(normed)[0].T)
 
-    sent, own_x = project(*line(recv, keep, w_x, oth_x))
+    line.hold(oth_y, oth_out)
+    recv, keep, this, other = line(recv, keep, w_x, oth_x)
+    sent, own_x = project(recv, keep, joined_rows(this, other))
     line.mark(sent)
     recv_x = swap(sent, WX)
-    sent, own_y = project(*line(recv, keep, w_y, oth_y))
+    recv, keep, this, other = line(recv, keep, w_y, oth_y)
+    sent, own_y = project(recv, keep, joined_rows(this, other))
     line.mark(sent)
-    recv_y, cot_x = swap(after(sent, recv_x), WX), swap(after(cot, recv_x), WX)
-    own_x, recv_x, own_y, recv_y = cube(own_x), cube(recv_x), cube(own_y), cube(recv_y)
+    sent = line.mark(joined_rows(*line(sent, cot)))
+    w_out = line.mark(joined_rows(*line(w_out, oth_out)))
+    received = swap(after(sent, recv_x), WX)
+    own_x, recv_x, own_y = cube(own_x), cube(recv_x), cube(own_y)
     tail_own, tail_recv = line(own_x[:, edge:], recv_x[:, edge:])
     tail = along_seq(line.mark(low(tail_own + wide(tail_recv))), 1)
     own_x, recv_x, tail, gates = line(own_x, recv_x, tail, gates)
@@ -971,62 +973,62 @@
     ends, other_ends = line(ends, other_ends)
     joined = line.mark(carry_join(ends, other_ends, sy, 1))
     arrived = carry_shifts(joined, 1)
-    own_y, recv_y = line(own_y, recv_y)
+    own_y, received = line(own_y, received)
+    recv_y, cot_x = cube(received[:rows]), received[rows:]
     branch_y = line.mark(gelu_pair(own_y + wide(recv_y))[0])
     carry = carry_finish(*tied_carry(line, other_ends, arrived), sy, 1)
     mixed = flat(low((local_state + running * carry) * branch_y))
     keep, send = split_columns(mixed, wx, wc)
     line.mark(send)
     recv = swap(send, WX)
-    cot_x, mixed = line(cot_x, mixed)
-    cot_both = swap(cot_x, WC)
-    cot_x_far = [None if 2 * j == far else around(cot_x, j) for j in range(1, far)]
-    both_turned = line.mark(jnp.concatenate([normed_turned, mixed.T], axis=1))
-    recv, keep, oth_out, cot_all = line(recv, keep, oth_out, cot_all)
-    sent, own = project(recv, keep, w_out, oth_out)
+    cot_core, cot_both = core(cot), core(cot_x)
+    both_turned = line.mark(jnp.concatenate([normed_turned, line(mixed)[0].T], axis=1))
+    line.hold(cot_core, cot_both)
+    sent, own = project(*line(recv, keep, w_out))
     line.mark(sent)
     recv = swap(sent, WX)
-    pulled_units = line.mark(pull_units(line(cot, cot_core, cot_x, cot_both), w_down))
+    pulled_units = line.mark(pull_units(line(cot, cot_x, cot_core, cot_both), w_down))
     own, recv = line(own, recv)
     stream = source + own + wide(recv)
     second_scale = lax.rsqrt(jnp.mean(stream * stream, axis=-1, keepdims=True) + 1e-06)
     normed_two = line.mark(low(stream * second_scale * gain2))
 
-    normed_x, normed_core = swap(normed_two, WX), swap(normed_two, WC)
-    normed_all = lax.all_gather(normed_two, SZ)
-    core_of = lambda values: [swap(v, WC) for v in values]
+    normed_x, normed_core = swap(normed_two, WX), core(normed_two)
     turned = both_turned.reshape(far, 2, 2, 2, features // (8 * far), half)
-    turned, cot_x_far = line_tree(line, turned, cot_x_far)
-    mine_x, send_x = rows_for(WX, 2, turned)
+    cot_others = line.mark(jnp.roll(*line(cot_all), -sz, axis=0)[1:])
+    normed_x, cot_others = line(normed_x, cot_others)
+    cot_x_far = swap(cot_others, WX)
+    normed_both = core(normed_x)
+    pair = line.mark(joined_rows(*line(normed_two, normed_x)))
+    normed_here = (lax.all_gather(pair, SZ),)
+    mine_x, send_x = rows_for(WX, 2, *line(turned))
     got_x = swap(line.mark(send_x), WX)
-    normed_both = swap(normed_x, WC)
-    opposite = lambda v: lax.dynamic_index_in_dim(v, (sz + far // 2) % far, 0, keepdims=False)
-    across = lambda pieces, gathered: [
-        swap(opposite(gathered), WX) if v is None else v for v in pieces
-    ]
-    tied = line(normed_two, normed_core, normed_x, normed_both)
-    normed_x_far = [None if 2 * j == far else around(tied[2], j) for j in range(1, far)]
-    cot_x_far = across(cot_x_far, after(cot_all, tied[2]))
-    acted = units(tied, w_gate, w_up, pulled_units)
-    hidden, gate_grad, up_grad = acted
+    hidden, gate_grad, up_grad = acted = units(
+        line(normed_two, normed_x, normed_core, normed_both), w_gate, w_up, pulled_units
+    )
     line.mark(hidden)
     mine_y, send_y = rows_for(SY, 2, jnp.stack(line(mine_x, got_x)))
     got_y = swap(line.mark(send_y), SY)
-    pulled = line.mark(units_back(*line(gate_grad, up_grad), w_gate, w_up))
-    pulled_both, pulled_core = swap(pulled[half + rows :], WC), swap(pulled[rows:half], WC)
-    pulled_there, pulled_both, got_y, normed_all, cot_x_far = line_tree(
-        line, pulled[half : half + rows], pulled_both, got_y, normed_all, cot_x_far
-    )
+    pulled = units_back(*line(gate_grad, up_grad), w_gate, w_up)
+    line.mark(pulled[0])
+    pulled_both, pulled_core = core(pulled[3]), core(pulled[2])
+    line.hold(pulled_core)
+    pulled_there, pulled_both = line(pulled[1], pulled_both)
     for_x = line.mark(low(wide(pulled_there) + wide(pulled_both)))
     from_x = swap(for_x, WX)
-    made = line.mark(units_made(*line(hidden), w_down))
+    cot_core_all = core(cot_all)
+    made = units_made(*line(hidden), w_down)
+    line.mark(made[0])
+    line.hold(cot_core_all)
     mine_y, got_y = line(mine_y, got_y)
     near, send = rows_for(WC, 2, jnp.concatenate([mine_y, got_y], axis=0))
     near, send = (v.reshape(4, features // 8, half) for v in (near, send))
-    away = swap(line.mark(send), WC)
-    pulled_here, pulled_core, from_x, normed_x_far = line_tree(
-        line, pulled[:rows], pulled_core, from_x, normed_x_far
-    )
+    away = core(line.mark(send))
+    cot_x, cot_x_far = line(cot_x, cot_x_far)
+    cot_x_all = line.mark(jnp.concatenate([cot_x[None], cot_x_far], axis=0))
+    cot_here, cot_there = (cot_all, cot_x_all), (cot_core_all, core(cot_x_all))
+    line.hold(away, cot_there[1])
+    pulled_here, pulled_core, from_x = line(pulled[0], pulled_core, from_x)
     grad_normed_two = wide(pulled_here) + wide(pulled_core) + wide(from_x)
     weighted_two = grad_normed_two * gain2
     grad_stream = (
@@ -1037,23 +1039,18 @@
     grad_gain2 = jnp.sum(grad_normed_two * stream * second_scale, axis=0)
     grad_proj = line.mark(low(grad_stream))
     proj_x, proj_y = swap(grad_proj, WX), swap(grad_proj, SY)
-    normed_x_far = across(normed_x_far, normed_all)
-    tied = line(cot_all, *cot_x_far)
-    pull_here = line.mark(pull_of(spots, tied[0], tied[1:], w_down))
-
-    cot_core_all, cot_both_far = swap(cot_all, WC), core_of(cot_x_far)
-    normed_core_all = swap(normed_all, WC)
-    cot_here, cot_there = (cot_all, cot_x_far), (cot_core_all, cot_both_far)
-
-    def shared(gathered, pieces, pulled):
-        gathered, pulled, *pieces = line(gathered, pulled, *pieces)
-        acts = share_of(spots, gathered, pieces, w_gate, w_up, pulled)
+    proj_core = core(grad_proj)
+    pull_here = line.mark(pull_of(spots, line(*cot_here), w_down))
+
+    def shared(gathered, pulled):
+        *gathered, pulled = line(*gathered, pulled)
+        acts = share_of(spots, gathered, w_gate, w_up, pulled)
         line.mark(acts[0])
         return acts
 
-    def unit_sums(here, there, own_x, kinds):
+    def unit_sums(here, there, kinds):
         acts = [line(acted[k], acts_here[k], acts_there[k]) for k in kinds]
-        outs = grad_of(spots, here, there, line(*own_x), acts)
+        outs = grad_of(spots, line(*here), line(*there), acts)
         line.mark(outs[0])
         return [(outs[2 * i], swap(outs[2 * i + 1], SY)) for i in range(len(kinds))]
 
@@ -1071,19 +1068,19 @@
         parts = pick(parity, own, other), pick(parity, other, own)
         return wide(jnp.concatenate([parts[0], parts[1][:, window - offset :]], axis=1))
 
-    def token_grad_of(second, *pieces):
-        pieces = [*pieces, *core_of(pieces)]
-        return line.mark(token_grad(*line(near, away), second, line(*pieces)))
-
-    proj_x, proj_y, grad_proj = line(proj_x, proj_y, grad_proj)
-    sent, own = project_back([(proj_x, grad_proj, w_out, oth_out)])
+    def token_sums(second, *pieces):
+        grad = token_grad(*line(near, away), second, line(*pieces))
+        return scatter_far(line.mark(grad))
+
+    line.hold(proj_y, proj_core, *normed_here)
+    proj_x, grad_proj = line(proj_x, grad_proj)
+    sent, own = project_back([(proj_x, grad_proj, w_out)])
     line.mark(sent)
     sent, proj_xy = swap(sent, WX), swap(proj_x, SY)
-    tied = line(cot_core_all, *cot_both_far)
-    pull_there = line.mark(pull_of(spots, tied[0], tied[1:], w_down))
-    sent, own, proj_xy, normed_x_far = line_tree(line, sent, own, proj_xy, normed_x_far)
-    normed_both_far = core_of(normed_x_far)
-    normed_here, normed_there = (normed_all, normed_x_far), (normed_core_all, normed_both_far)
+    proj_x_core, proj_y_core = core(proj_x), core(proj_y)
+    pull_there = line.mark(pull_of(spots, line(*cot_there), w_down))
+    line.hold(proj_xy, proj_x_core, proj_y_core)
+    sent, own = line(sent, own)
     grad_mixed = cube(join_columns(own, wide(sent), wx, wc))
     line.mark(grad_mixed)
     grad_pre, behind, local_grad, back_ends = unroll(
@@ -1096,13 +1093,17 @@
     grad_pre = flat(grad_pre)
     other_ends = swap(back_ends, SY)
     pre_x, pre_y = swap(grad_pre, WX), swap(grad_pre, SY)
+    proj_xy_core, pre_core = core(proj_xy), core(grad_pre)
+    line.hold(proj_xy_core, pre_core)
     back_ends, other_ends = line(back_ends, other_ends)
     joined = line.mark(carry_join(back_ends, other_ends, sy, -1))
     arrived = carry_shifts(joined, -1)
-    acts_here = shared(*normed_here, pull_here)
-    other_ends, pre_x, pre_y, *arrived = line(other_ends, pre_x, pre_y, *arrived)
+    acts_here = shared(normed_here, pull_here)
+    other_ends, arrived, pre_x, pre_y = line_tree(line, other_ends, arrived, pre_x, pre_y)
     carry_back = carry_finish(other_ends, arrived, sy, -1)
     line.mark(carry_back)
+    pre_xy, pre_x_core, pre_y_core = swap(pre_y, WX), core(pre_x), core(pre_y)
+    normed_there = (core(after(normed_here[0], carry_back)),)
     spread, earlier, grad_wa, grad_wi, sums = recur_back(
         *line(behind, local_grad, carry_back, running, local_state, carry),
         gate_rec,
@@ -1116,9 +1117,16 @@
         as_row(decay_log),
     )
     line.mark(earlier)
-    pre_xy = swap(pre_x, SY)
     later = along_seq(low(earlier[:, HALO - (taps - 1) :]), -1)
-    out_sums = scatter_far(token_grad_of(1, grad_proj, proj_x, proj_y, proj_xy))
+    out_sums = token_sums(
+        1, grad_proj, proj_x, proj_y, proj_xy, proj_core, proj_x_core, proj_y_core, proj_xy_core
+    )
+    line.hold(pre_x_core, pre_y_core, pre_xy)
+    spread, later = line(spread, later)
+    grad_branch = flat(low(spread + jnp.pad(wide(later), ((0, 0), (edge, 0), (0, 0)))))
+    line.mark(grad_branch)
+    grad_x, grad_y = swap(grad_branch, WX), swap(grad_branch, SY)
+    grad_core = core(grad_branch)
     grad_wa, grad_wi, sums, grad_gain2 = line(grad_wa, grad_wi, sums, grad_gain2)
     small = jnp.concatenate([grad_gain2[None], sums], axis=0)
     small = low(jnp.pad(small.T, ((0, 0), (0, 128 - small.shape[0]))))
@@ -1134,26 +1142,42 @@
         mine, got = line(mine, got)
         return low(wide(mine) + wide(got))
 
-    rest = rest_step(WC, 3, rest)
-    spread, later = line(spread, later)
-    grad_branch = flat(low(spread + jnp.pad(wide(later), ((0, 0), (edge, 0), (0, 0)))))
-    line.mark(grad_branch)
-    branch_x_part, branch_y_part = swap(grad_branch, WX), swap(grad_branch, SY)
+    rest = rest_step(WC, 3, *line(rest))
+    line.hold(grad_core, rest[1])
+    acts_there = shared(normed_there, pull_there)
+    grad_x, grad_branch, grad_y, pre_xy = line(grad_x, grad_branch, grad_y, pre_xy)
+    grad_xy, grad_x_core, grad_y_core = swap(grad_y, WX), core(grad_x), core(grad_y)
+    pre_xy_core = core(pre_xy)
     rest = rest_step(WX, 2, rest_join(*rest))
-    acts_there = shared(*normed_there, pull_there)
-    branch_x_part, branch_y_part, pre_xy = line(branch_x_part, branch_y_part, pre_xy)
     sent, own = project_back(
         [
-            line(branch_x_part, grad_branch, w_x, oth_x),
-            line(pre_x, grad_pre, w_y, oth_y),
+            (grad_x, grad_branch, joined_rows(w_x, oth_x)),
+            (*line(pre_x, grad_pre), joined_rows(w_y, oth_y)),
         ]
     )
     line.mark(sent)
+    line.hold(grad_x_core, grad_y_core, pre_xy_core, grad_xy)
     sent = swap(sent, WX)
-    branch_xy_part = swap(branch_y_part, WX)
-    (down,) = unit_sums(cot_here, cot_there, (cot_x, cot_both), [0])
     rest = rest_step(SY, 1, rest_join(*rest))
-    sent, own, branch_xy_part, out_sums = line(sent, own, branch_xy_part, out_sums)
+    (down,) = unit_sums(cot_here, cot_there, [0])
+    y_sums = token_sums(
+        0, grad_pre, pre_x, pre_y, pre_xy, pre_core, pre_x_core, pre_y_core, pre_xy_core
+    )
+    line.hold(out_sums)
+    rest = scatter_far(line.mark(rest_join(*rest).reshape(features // 8, -1)))
+    grad_xy_core = core(after(grad_xy, down[0]))
+    line.hold(grad_xy_core)
+    (gate,) = unit_sums(normed_here, normed_there, [1])
+    x_sums = token_sums(
+        0, grad_branch, grad_x, grad_y, grad_xy, grad_core, grad_x_core, grad_y_core, grad_xy_core
+    )
+    line.hold(sent)
+    down = unit_join(*down)
+    (up,) = unit_sums(normed_here, normed_there, [2])
+    gate = unit_join(*gate)
+    made_both, made_core = core(made[3]), core(made[2])
+    line.hold(made_both, made_core)
+    sent, own = line(sent, own)
     grad_normed = join_columns(own, wide(sent), wx, wc)
     weighted = grad_normed * gain
     input_grad = (
@@ -1162,36 +1186,32 @@
         - source * norm_scale**3 * jnp.mean(weighted * source, axis=-1, keepdims=True)
     )
     grad_gain = jnp.sum(grad_normed * source * norm_scale, axis=0)
+    grad_gain, input_grad = tie(grad_gain, input_grad)
     line.mark(grad_gain)
-
-    y_sums = scatter_far(token_grad_of(0, grad_pre, pre_x, pre_y, pre_xy))
-    (gate,) = unit_sums(normed_here, normed_there, (normed_x, normed_both), [1])
-    x_grad = token_grad_of(0, grad_branch, branch_x_part, branch_y_part, branch_xy_part)
-
-    down = unit_join(*down)
-    (up,) = unit_sums(normed_here, normed_there, (normed_x, normed_both), [2])
-    rest = rest_join(*rest).reshape(features // 8, -1)
-    late_sums = scatter_far(line.mark(jnp.concatenate([x_grad, rest], axis=1)))
-    gate = unit_join(*gate)
-    (y_sums,) = line(y_sums)
+    gain_total = total_of_all(grad_gain, line)
+    next(gain_total)
+    made_there, made_both = line(made[1], made_both)
+    made_x = swap(line.mark(low(wide(made_there) + wide(made_both))), WX)
     up = unit_join(*up)
-    grad_gain = total_of_all(*line(grad_gain))
-    made_there, made_both = line(made[half : half + rows], swap(after(made, grad_mixed)[half + rows :], WC))
-    made_x = swap(line.mark(low(wide(made_there) + wide(made_both))), WX)
-    made_core = swap(after(made, grad_mixed)[rows:half], WC)
+    next(gain_total)
     down_grad = line.mark(unit_final(*down).T)
-    made_here, made_core, made_x = line(made[:rows], made_core, made_x)
+    next(gain_total)
+    made_here, made_core, made_x = line(made[0], made_core, made_x)
     output = line.mark(low(stream + wide(made_here) + wide(made_core) + wide(made_x)))
+    next(gain_total)
     gate_grad = line.mark(unit_final(*gate))
     up_grad = line.mark(unit_final(*up))
-    x_sums, rest = late_sums[:, :features], wide(late_sums[:, features:])
+    grad_gain = line.mark(next(gain_total))
+    out_sums, y_sums, rest, x_sums = (
+        line.mark(wide(*line(v))) for v in (out_sums, y_sums, rest, x_sums)
+    )
     grads = rest[:, 2 * head :]
     return (
         cube(output),
         cube(input_grad),
         grad_gain,
-        wide(x_sums),
-        wide(y_sums),
+        x_sums,
+        y_sums,
         grads[:, 1 : 1 + taps].T,
         grads[:, 1 + taps],
         rest[:, :head],
@@ -1199,7 +1219,7 @@
         rest[:, head : 2 * head],
         grads[:, 3 + taps],
         grads[:, 4 + taps],
-        wide(out_sums),
+        out_sums,
         grads[:, 0],
         gate_grad,
         up_grad,

time: 642 us -> 558 us (0.87)
  waiting for transfers between devices: 203 us -> 135 us
  starting transfers between devices: 91.3 us -> 77.4 us
  local copies, waits for them, and re-layouts: 40 us -> 29.3 us
  Pallas kernels: 191 us -> 200 us
    ppermute x7 -> x3, waiting for transfers between devices: 50.7 us -> 1.08 us  [around(): lax.ppermute(value, SZ, [((to + steps) % count, to) for to in range(count)])]
    ppermute x7 -> x3, starting transfers between devices: 15.9 us -> 5.18 us  [around(): lax.ppermute(value, SZ, [((to + steps) % count, to) for to in range(count)])]
    ppermute x3, waiting for transfers between devices: 18.2 us -> 8.59 us  [partner_far(): lax.ppermute(value, SZ, [(source, source ^ 1) for source in range(count)])]
    pallas_call x7, Pallas kernels: 86 us -> 95.4 us  [the longest x4 61.1 us: share_call(): pl.pallas_call(partial(kernel, len(gathered)), grid_spec=pltpu.PrefetchSc...]
    slice x4 -> x1, local copies, waits for them, and re-layouts: 7.04 us -> 0.09 us  [local(): recv_y, cot_x = (cube(received[:rows]), received[rows:])]
    ppermute x67 -> x60, waiting for transfers between devices: 130 us -> 125 us  [swap(): return lax.ppermute(value, axis, [(0, 1), (1, 0)])]
    ppermute x67 -> x60, starting transfers between devices: 49.9 us -> 44.4 us  [swap(): return lax.ppermute(value, axis, [(0, 1), (1, 0)])]
    unnamed x134 -> x112, local copies, waits for them, and re-layouts: 13.2 us -> 10.2 us
  transfers between devices with their start and end apart: 91 -> 81, of which waited for: 25 -> 24; matrix products, arithmetic and copies ran while one was open for 18% -> 20% of each run, Pallas kernels for 28% -> 35%
where the time goes in v3:
time: 558 us; the launch traced here: 551 us
  Pallas kernels  200 us (36%)
  waiting for transfers between devices  135 us (24%)
  starting transfers between devices  77.4 us (14%)
  other arithmetic  66.5 us (12%)
  local copies, waits for them, and re-layouts  29.3 us (5%)
  matrix products  25.5 us (5%)
  between operations  17.5 us (3%)
    ppermute x60, waiting for transfers between devices, swap(): return lax.ppermute(value, axis, [(0, 1), (1, 0)])  125 us
    pallas_call x4, Pallas kernels, share_call(): pl.pallas_call(partial(kernel, len(gathered)), grid_spec=pltpu.PrefetchSc...  61.1 us
    ppermute x60, starting transfers between devices, swap(): return lax.ppermute(value, axis, [(0, 1), (1, 0)])  44.4 us
    pallas_call x3, Pallas kernels, unit_grad(): pl.pallas_call(partial(unit_grad_kernel, len(here), kinds), grid_spec=plt...  34.3 us
    convert_element_type x15, other arithmetic, local(): low = lambda v: v.astype(BF16)  20.9 us
    pallas_call x3, Pallas kernels, token_grad(): pl.pallas_call(partial(token_grad_kernel, second * rows), grid=(width //...  19.9 us
    pallas_call x1, Pallas kernels, units(): pl.pallas_call(partial(units_kernel, count), grid=(held // tile,), in_spe...  19.7 us
    pallas_call x1, Pallas kernels, units_back(): pl.pallas_call(units_back_kernel, grid=(width // tile,), in_specs=[whole,...  18.1 us
  transfers between devices with their start and end apart: 81, of which 24 were waited for; matrix products, arithmetic and copies ran while one was open for 20% of the time, Pallas kernels for 35%

profile of v3, /device:TPU:0, one launch (start us, length us, event | category | flops | bytes accessed | tf_op | source)
XLA Modules:
  0.0 551.4 jit_solution(9121988898098858941)
XLA Ops:
  9.1 2.0 pad_maximum_fusion.7
  11.9 2.6 collective-permute-start
  14.5 8.4 %collective-permute-done = bf16[128,1280]{1,0:T(8,128)(2,1)S(1)} collective-permute-done((bf16[128,1280]{1,0:T(8,128)(2,1)S(1)}, bf16[128,1280]{1,0:T(8,128)(2,1)S(1)}, u32[]{:S(2)}, u32[]{:S(2)}) %collective-permute-start) | collective-permute-done | bytes 327712 | tf_op jit(solution)/shard_map/ppermute | solution.py:22
  23.8 4.0 fusion
  28.0 3.0 collective-permute-start.4
  31.0 3.5 fusion.4
  39.6 4.0 constant_dynamic-update-slice_fusion.2
  43.5 8.3 %collective-permute-done.4 = bf16[128,2560]{1,0:T(8,128)(2,1)S(1)} collective-permute-done((bf16[128,2560]{1,0:T(8,128)(2,1)S(1)}, bf16[128,2560]{1,0:T(8,128)(2,1)S(1)}, u32[]{:S(2)}, u32[]{:S(2)}) %collective-permute-start.4) | collective-permute-done | bytes 655392 | tf_op jit(solution)/shard_map/ppermute | solution.py:22
  52.7 3.4 collective-permute-start.5
  60.8 9.1 %recur.1 = (bf16[2,64,2560]{2,1,0:T(8,128)(2,1)}, bf16[2,64,2560]{2,1,0:T(8,128)(2,1)}, f32[2,64,2560]{2,1,0:T(8,128)}, f32[2,64,2560]{2,1,0:T(8,128)}, f32[2,64...) custom-call(f32[2,64,2560]{2,1,0:T(8,128)} %bitcast.208, bf16[2,64,2560]{2,1,0:T(8,128)(2,1)} %bitcast.231, ...), custom_call_target="tpu_custom_call" | custom-call | flops 1310720 | bytes 262144 | tf_op jit(solution)/shard_map/recur/pallas_call | solution.py:263
  74.3 5.5 collective-permute-start.9
  81.1 2.7 collective-permute-start.7
  83.8 5.7 %collective-permute-done.10 = bf16[256,2560]{1,0:T(8,128)(2,1)S(1)} collective-permute-done((bf16[256,2560]{1,0:T(8,128)(2,1)S(1)}, bf16[256,2560]{1,0:T(8,128)(2,1)S(1)}, u32[]{:S(2)}, u32[]{:S(2)}) %collective-permute-start.10) | collective-permute-done | bytes 1310752 | tf_op jit(solution)/shard_map/ppermute | solution.py:22
  94.4 7.7 %collective-permute-done.11 = bf16[128,1280]{1,0:T(8,128)(2,1)S(1)} collective-permute-done((bf16[128,1280]{1,0:T(8,128)(2,1)S(1)}, bf16[128,1280]{1,0:T(8,128)(2,1)S(1)}, u32[]{:S(2)}, u32[]{:S(2)}) %collective-permute-start.11) | collective-permute-done | bytes 327712 | tf_op jit(solution)/shard_map/ppermute | solution.py:22
  102.1 5.0 fusion.60
  108.2 10.5 %pull_units.1.refs_6_ = bf16[512,1920]{1,0:T(8,128)(2,1)} custom-call(bf16[128,2560]{1,0:T(8,128)(2,1)} %bitcast.4.refs_0_, bf16[128,2560]{1,0:T(8,128)(2,1)} %copy-done.6, bf16[128,2560]{1,0:T(8,128)(2,1)} %collective-permute-done.12.refs_2_, bf16[128,2560]{1,0:T(8,128)(2,1)} %copy-done.27, bf16[1920,2560]{1,0:T(8,128)(2,1)} %refs_2_.5), custom_call_target="tpu_custom_call" | custom-call | flops 100663296 | bytes 196608 | tf_op jit(solution)/shard_map/pull_units/pallas_call | solution.py:527
  118.7 4.6 collective-permute-done.14
  128.2 3.5 fusion.21
  131.8 8.4 %collective-permute-done.15.refs_1_ = bf16[128,2560]{1,0:T(8,128)(2,1)} collective-permute-done((bf16[128,2560]{1,0:T(8,128)(2,1)}, bf16[128,2560]{1,0:T(8,128)(2,1)}, u32[]{:S(2)}, u32[]{:S(2)}) %collective-permute-start.15) | collective-permute-done | bytes 655392 | tf_op jit(solution)/shard_map/ppermute | solution.py:22
  140.2 2.0 constant_dynamic-update-slice_fusion.5
  142.2 2.0 constant_dynamic-update-slice_fusion.4
  147.0 19.7 %units.1 = (bf16[512,1920]{1,0:T(8,128)(2,1)}, bf16[512,1920]{1,0:T(8,128)(2,1)}, bf16[512,1920]{1,0:T(8,128)(2,1)}) custom-call(bf16[128,2560]{1,0:T(8,128)(2,1)} %multiply_convert_fusion.refs_0_, bf16[128,2560]{1,0:T(8,128)(2,1)} %collective-permute-done.15.refs_1_, bf16[128,2560]{1,0:T(8,128)(2,1)} %collective-permute-done.16.refs_2_, ...), custom_call_target="tpu_custom_call" | custom-call | flops 201326592 | bytes 393216 | tf_op jit(solution)/shard_map/units/pallas_call | solution.py:498
  166.8 18.1 %units_back.1 = (bf16[128,2560]{1,0:T(8,128)(2,1)}, bf16[128,2560]{1,0:T(8,128)(2,1)}, bf16[128,2560]{1,0:T(8,128)(2,1)}, bf16[128,2560]{1,0:T(8,128)(2,1)}) custom-call(bf16[512,1920]{1,0:T(8,128)(2,1)} %get-tuple-element.430.gate.refs_2_, bf16[512,1920]{1,0:T(8,128)(2,1)} %get-tuple-element.452.up.refs_2_, bf16[2560,1920]{1,0:T(8,128)(2,1)} %refs_1_.3, ...), custom_call_target="tpu_custom_call" | custom-call | flops 201326592 | bytes 393216 | tf_op jit(solution)/shard_map/units_back/pallas_call | solution.py:556
  188.4 9.8 %units_made.1 = (bf16[128,2560]{1,0:T(8,128)(2,1)}, bf16[128,2560]{1,0:T(8,128)(2,1)}, bf16[128,2560]{1,0:T(8,128)(2,1)}, bf16[128,2560]{1,0:T(8,128)(2,1)}) custom-call(bf16[512,1920]{1,0:T(8,128)(2,1)} %get-tuple-element.409.hidden.refs_4_, bf16[1920,2560]{1,0:T(8,128)(2,1)} %refs_2_.5), custom_call_target="tpu_custom_call" | custom-call | flops 100663296 | bytes 196608 | tf_op jit(solution)/shard_map/units_made/pallas_call | solution.py:576
  198.2 4.0 collective-permute-done.24
  207.2 16.1 %collective-permute-done.23 = bf16[128,2560]{1,0:T(8,128)(2,1)S(1)} collective-permute-done((bf16[128,2560]{1,0:T(8,128)(2,1)S(1)}, bf16[128,2560]{1,0:T(8,128)(2,1)S(1)}, u32[]{:S(2)}, u32[]{:S(2)}) %collective-permute-start.23) | collective-permute-done | bytes 655392 | tf_op jit(solution)/shard_map/ppermute | solution.py:22
  224.1 2.8 fusion.78
  229.8 18.4 %share_pull.2.refs_3_ = bf16[768,1024]{1,0:T(8,128)(2,1)} custom-call(s32[3]{0:T(128)} %pad_add_fusion.places, bf16[4,128,2560]{2,1,0:T(8,128)(2,1)} %all-gather.7.cloned.1.call-done.refs_0_, bf16[4,128,2560]{2,1,0:T(8,128)(2,1)} %copy-done.1, bf16[1920,2560]{1,0:T(8,128)(2,1)} %refs_2_.5), custom_call_target="tpu_custom_call" | custom-call | flops 80530640 | bytes 104857 | tf_op jit(solution)/shard_map/share_pull/pallas_call | solution.py:654
  249.4 5.0 fusion.24
  256.5 9.7 %share_pull.3.refs_3_ = bf16[768,1024]{1,0:T(8,128)(2,1)} custom-call(s32[3]{0:T(128)} %pad_add_fusion.places, bf16[4,128,2560]{2,1,0:T(8,128)(2,1)} %collective-permute-done.25.refs_0_.refs_2_, bf16[4,128,2560]{2,1,0:T(8,128)(2,1)} %collective-permute-done.28.refs_1_.refs_3_, bf16[1920,2560]{1,0:T(8,128)(2,1)} %refs_2_.5), custom_call_target="tpu_custom_call" | custom-call | flops 80530640 | bytes 104857 | tf_op jit(solution)/shard_map/share_pull/pallas_call | solution.py:654
  267.6 7.8 %unroll.1 = (bf16[2,64,2560]{2,1,0:T(8,128)(2,1)}, f32[2,64,2560]{2,1,0:T(8,128)}, f32[2,64,2560]{2,1,0:T(8,128)}, f32[4,2560]{1,0:T(4,128)}) custom-call(f32[2,64,2560]{2,1,0:T(8,128)} %pad_maximum_fusion.2.mixed_grad, f32[2,64,2560]{2,1,0:T(8,128)} %bitcast.193, bf16[2,64,2560]{2,1,0:T(8,128)(2,1)} %bitcast.201, ...), custom_call_target="tpu_custom_call" | custom-call | flops 1310720 | bytes 262144 | tf_op jit(solution)/shard_map/unroll/pallas_call | solution.py:312
  285.2 16.4 %share.2 = (bf16[768,1024]{1,0:T(8,128)(2,1)}, bf16[768,1024]{1,0:T(8,128)(2,1)}, bf16[768,1024]{1,0:T(8,128)(2,1)}) custom-call(s32[3]{0:T(128)} %pad_add_fusion.places, bf16[4,256,2560]{2,1,0:T(8,128)(2,1)} %bitcast.26.refs_0_, bf16[2560,1920]{1,0:T(8,128)(2,1)} %refs_1_.3, bf16[2560,1920]{1,0:T(8,128)(2,1)} %refs_2_.7, bf16[768,1024]{1,0:T(8,128)(2,1)} %share_pull.2.refs_3_), custom_call_target="tpu_custom_call" | custom-call | flops 161061280 | bytes 209715 | tf_op jit(solution)/shard_map/share/pallas_call | solution.py:654
  304.3 9.9 %recur_back.1 = (f32[2,64,2560]{2,1,0:T(8,128)}, f32[2,8,2560]{2,1,0:T(8,128)}, bf16[2560,256]{1,0:T(8,128)(2,1)}, bf16[2560,256]{1,0:T(8,128)(2,1)}, f32[8,2560]{1,0:T(8,128)}) custom-call(f32[2,64,2560]{2,1,0:T(8,128)} %get-tuple-element.358.behind, f32[2,64,2560]{2,1,0:T(8,128)} %get-tuple-element.359.local_grad, f32[2,1,2560]{2,1,0:T(1,128)} %copy.106.carry_back, ...), custom_call_target="tpu_custom_call" | custom-call | flops 1966080 | bytes 327680 | tf_op jit(solution)/shard_map/recur_back/pallas_call | solution.py:422
  316.4 6.7 %token_grad.3 = bf16[320,2560]{1,0:T(8,128)(2,1)} custom-call(bf16[128,2560]{1,0:T(8,128)(2,1)} %copy-done.22, bf16[128,2560]{1,0:T(8,128)(2,1)} %collective-permute-done.29.refs_1_, bf16[128,2560]{1,0:T(8,128)(2,1)} %copy-done.36, bf16[128,2560]{1,0:T(8,128)(2,1)} %collective-permute-done.33.refs_3_, bf16[128,2560]{1,0:T(8,128)(2,1)} %collective-permute-done.31.refs_4_, ...), custom_call_target="tpu_custom_call" | custom-call | flops 33554432 | bytes 131072 | tf_op jit(solution)/shard_map/token_grad/pallas_call | solution.py:845
  329.8 2.6 collective-permute-start.49
  333.2 2.3 fusion.22
  335.6 16.5 %share.3 = (bf16[768,1024]{1,0:T(8,128)(2,1)}, bf16[768,1024]{1,0:T(8,128)(2,1)}, bf16[768,1024]{1,0:T(8,128)(2,1)}) custom-call(s32[3]{0:T(128)} %pad_add_fusion.places, bf16[4,256,2560]{2,1,0:T(8,128)(2,1)} %collective-permute-done.50.refs_0_.refs_1_, bf16[2560,1920]{1,0:T(8,128)(2,1)} %refs_1_.3, bf16[2560,1920]{1,0:T(8,128)(2,1)} %refs_2_.7, ...), custom_call_target="tpu_custom_call" | custom-call | flops 161061280 | bytes 209715 | tf_op jit(solution)/shard_map/share/pallas_call | solution.py:654
  353.5 2.0 add_convert_fusion
  356.9 4.0 fusion.12
  361.0 4.0 fusion.18
  366.1 4.0 collective-permute-done.58.refs_3_
  370.1 16.2 %collective-permute-done.54 = bf16[4,2,80,640]{3,2,1,0:T(8,128)(2,1)S(1)} collective-permute-done((bf16[4,2,80,640]{3,2,1,0:T(8,128)(2,1)S(1)}, bf16[4,2,80,640]{3,2,1,0:T(8,128)(2,1)S(1)}, u32[]{:S(2)}, u32[]{:S(2)}) %collective-permute-start.54) | collective-permute-done | bytes 819232 | tf_op jit(solution)/shard_map/ppermute | solution.py:22
  387.3 11.4 %unit_grad.3 = (f32[2,320,1024]{2,1,0:T(8,128)}, bf16[2,320,1024]{2,1,0:T(8,128)(2,1)}) custom-call(s32[3]{0:T(128)} %pad_add_fusion.places, bf16[4,128,2560]{2,1,0:T(8,128)(2,1)} %all-gather.7.cloned.1.call-done.refs_0_, bf16[4,128,2560]{2,1,0:T(8,128)(2,1)} %copy-done.1, bf16[4,128,2560]{2,1,0:T(8,128)(2,1)} %collective-permute-done.25.refs_0_.refs_2_, ...), custom_call_target="tpu_custom_call" | custom-call | flops 107374184 | bytes 83886 | tf_op jit(solution)/shard_map/unit_grad/pallas_call | solution.py:723
  398.8 6.6 %token_grad.4 = bf16[320,2560]{1,0:T(8,128)(2,1)} custom-call(bf16[128,2560]{1,0:T(8,128)(2,1)} %bitcast.236, bf16[128,2560]{1,0:T(8,128)(2,1)} %collective-permute-done.42.refs_1_, bf16[128,2560]{1,0:T(8,128)(2,1)} %copy-done.33, bf16[128,2560]{1,0:T(8,128)(2,1)} %collective-permute-done.47.refs_3_, bf16[128,2560]{1,0:T(8,128)(2,1)} %copy-done.32, ...), custom_call_target="tpu_custom_call" | custom-call | flops 33554432 | bytes 131072 | tf_op jit(solution)/shard_map/token_grad/pallas_call | solution.py:845
  408.3 9.9 %collective-permute-done.59 = bf16[4,80,640]{2,1,0:T(8,128)(2,1)} collective-permute-done((bf16[4,80,640]{2,1,0:T(8,128)(2,1)}, bf16[4,80,640]{2,1,0:T(8,128)(2,1)}, u32[]{:S(2)}, u32[]{:S(2)}) %collective-permute-start.59) | collective-permute-done | bytes 409632 | tf_op jit(solution)/shard_map/ppermute | solution.py:22
  418.2 2.0 add_convert_fusion.9
  420.3 11.6 %unit_grad.4 = (f32[2,320,1024]{2,1,0:T(8,128)}, bf16[2,320,1024]{2,1,0:T(8,128)(2,1)}) custom-call(s32[3]{0:T(128)} %pad_add_fusion.places, bf16[4,256,2560]{2,1,0:T(8,128)(2,1)} %bitcast.26.refs_0_, bf16[4,256,2560]{2,1,0:T(8,128)(2,1)} %collective-permute-done.50.refs_0_.refs_1_, bf16[512,1920]{1,0:T(8,128)(2,1)} %get-tuple-element.430.gate.refs_2_, ...), custom_call_target="tpu_custom_call" | custom-call | flops 107374184 | bytes 83886 | tf_op jit(solution)/shard_map/unit_grad/pallas_call | solution.py:723
  435.3 6.6 %token_grad.5 = bf16[320,2560]{1,0:T(8,128)(2,1)} custom-call(bf16[128,2560]{1,0:T(8,128)(2,1)} %bitcast.223, bf16[128,2560]{1,0:T(8,128)(2,1)} %collective-permute-done.48.refs_1_, bf16[128,2560]{1,0:T(8,128)(2,1)} %collective-permute-done.49.refs_2_, bf16[128,2560]{1,0:T(8,128)(2,1)} %copy-done.34, bf16[128,2560]{1,0:T(8,128)(2,1)} %copy-done.30, ...), custom_call_target="tpu_custom_call" | custom-call | flops 33554432 | bytes 131072 | tf_op jit(solution)/shard_map/token_grad/pallas_call | solution.py:845
  442.0 4.3 collective-permute-done.62
  446.3 2.6 add_convert_fusion.3
  449.8 2.8 collective-permute-start.67
  452.6 11.3 %unit_grad.5 = (f32[2,320,1024]{2,1,0:T(8,128)}, bf16[2,320,1024]{2,1,0:T(8,128)(2,1)}) custom-call(s32[3]{0:T(128)} %pad_add_fusion.places, bf16[4,256,2560]{2,1,0:T(8,128)(2,1)} %bitcast.26.refs_0_, bf16[4,256,2560]{2,1,0:T(8,128)(2,1)} %collective-permute-done.50.refs_0_.refs_1_, bf16[512,1920]{1,0:T(8,128)(2,1)} %get-tuple-element.452.up.refs_2_, ...), custom_call_target="tpu_custom_call" | custom-call | flops 107374184 | bytes 83886 | tf_op jit(solution)/shard_map/unit_grad/pallas_call | solution.py:723
  465.1 9.3 %collective-permute-done.61 = bf16[2,320,1024]{2,1,0:T(8,128)(2,1)} collective-permute-done((bf16[2,320,1024]{2,1,0:T(8,128)(2,1)}, bf16[2,320,1024]{2,1,0:T(8,128)(2,1)}, u32[]{:S(2)}, u32[]{:S(2)}) %collective-permute-start.61) | collective-permute-done | bytes 1310752 | tf_op jit(solution)/shard_map/ppermute | solution.py:22
  477.1 2.8 collective-permute-start.73
  482.4 3.1 fusion.36
  488.3 12.1 %collective-permute-done.65 = bf16[2,320,1024]{2,1,0:T(8,128)(2,1)} collective-permute-done((bf16[2,320,1024]{2,1,0:T(8,128)(2,1)}, bf16[2,320,1024]{2,1,0:T(8,128)(2,1)}, u32[]{:S(2)}, u32[]{:S(2)}) %collective-permute-start.65) | collective-permute-done | bytes 1310752 | tf_op jit(solution)/shard_map/ppermute | solution.py:22
  500.4 2.6 add_convert_fusion.1
  505.5 3.6 collective-permute-start.72
  512.5 2.2 add_convert_fusion.5
  514.8 2.6 collective-permute-done.73
  517.3 4.7 collective-permute-start.70
  525.3 6.0 %collective-permute-done.72 = bf16[320,1024]{1,0:T(8,128)(2,1)S(1)} collective-permute-done((bf16[320,1024]{1,0:T(8,128)(2,1)S(1)}, bf16[320,1024]{1,0:T(8,128)(2,1)S(1)}, u32[]{:S(2)}, u32[]{:S(2)}) %collective-permute-start.72) | collective-permute-done | bytes 655392 | tf_op jit(solution)/shard_map/ppermute | solution.py:38
  535.7 2.0 convert_element_type.211
  541.5 2.0 convert_element_type.213
  (365 shorter events, 110.0 us)
Async XLA Ops:
  8.0 52.1 %all-gather.5.cloned.1.call-start = ((), (), s32[]{:S(2)}) async-start(), calls=%async_computation.4 | async-start | bytes 3276800 | tf_op jit(solution)/shard_map/all_gather | solution.py:932
  8.1 14.9 %collective-permute-start.3 = (bf16[640,2560]{1,0:T(8,128)(2,1)}, bf16[640,2560]{1,0:T(8,128)(2,1)}, u32[]{:S(2)}, u32[]{:S(2)}) collective-permute-start(bf16[640,2560]{1,0:T(8,128)(2,1)} %param.31), channel_id=1, source_target_pairs={{0,1},{1,0},{2,3},{3,2},{4,5},{5,4},{6,7},{7,6},{8,9},{9,8},{10,11... | collective-permute-start | bytes 9830408 | tf_op jit(solution)/shard_map/ppermute | solution.py:22
  8.6 14.3 %collective-permute-start.1 = (bf16[640,2560]{1,0:T(8,128)(2,1)}, bf16[640,2560]{1,0:T(8,128)(2,1)}, u32[]{:S(2)}, u32[]{:S(2)}) collective-permute-start(bf16[640,2560]{1,0:T(8,128)(2,1)} %param.22), channel_id=1, source_target_pairs={{0,1},{1,0},{2,3},{3,2},{4,5},{5,4},{6,7},{7,6},{8,9},{9,8},{10,11... | collective-permute-start | bytes 9830408 | tf_op jit(solution)/shard_map/ppermute | solution.py:22
  8.7 15.1 %collective-permute-start.2 = (bf16[640,2560]{1,0:T(8,128)(2,1)}, bf16[640,2560]{1,0:T(8,128)(2,1)}, u32[]{:S(2)}, u32[]{:S(2)}) collective-permute-start(bf16[640,2560]{1,0:T(8,128)(2,1)} %param.23), channel_id=1, source_target_pairs={{0,1},{1,0},{2,3},{3,2},{4,5},{5,4},{6,7},{7,6},{8,9},{9,8},{10,11... | collective-permute-start | bytes 9830408 | tf_op jit(solution)/shard_map/ppermute | solution.py:22
  11.1 115.0 %all-gather.7.cloned.1.call-start = ((), (), s32[]{:S(2)}) async-start(), calls=%async_computation.5 | async-start | bytes 3276800 | tf_op jit(solution)/shard_map/all_gather | solution.py:934
  11.9 11.1 %collective-permute-start = (bf16[128,1280]{1,0:T(8,128)(2,1)S(1)}, bf16[128,1280]{1,0:T(8,128)(2,1)S(1)}, u32[]{:S(2)}, u32[]{:S(2)}) collective-permute-start(bf16[128,1280]{1,0:T(8,128)(2,1)S(1)} %pad_maximum_fusion.8), channel_id=1, source_target_pairs={{0,2},{2,0},{1,3},{3,1},{4,6},{6,4},{5,7},{7,5},{8,10},{10,8},{9,1... | collective-permute-start | bytes 983048 | tf_op jit(solution)/shard_map/ppermute | solution.py:22
  28.0 23.8 %collective-permute-start.4 = (bf16[128,2560]{1,0:T(8,128)(2,1)S(1)}, bf16[128,2560]{1,0:T(8,128)(2,1)S(1)}, u32[]{:S(2)}, u32[]{:S(2)}) collective-permute-start(bf16[128,2560]{1,0:T(8,128)(2,1)S(1)} %slice.758), channel_id=1, source_target_pairs={{0,2},{2,0},{1,3},{3,1},{4,6},{6,4},{5,7},{7,5},{8,10},{10,8},{9,1... | collective-permute-start | bytes 1966088 | tf_op jit(solution)/shard_map/ppermute | solution.py:22
  59.3 30.2 %collective-permute-start.10 = (bf16[256,2560]{1,0:T(8,128)(2,1)S(1)}, bf16[256,2560]{1,0:T(8,128)(2,1)S(1)}, u32[]{:S(2)}, u32[]{:S(2)}) collective-permute-start(bf16[256,2560]{1,0:T(8,128)(2,1)S(1)} %constant_dynamic-update-slice_fusion), channel_id=1, source_target_pairs={{0,2},{2,0},{1,3},{3,1},{4,6},{6,4},{5,7},{7,5},{8,10},{10,8},{9,1... | collective-permute-start | bytes 3932168 | tf_op jit(solution)/shard_map/ppermute | solution.py:22
  71.6 22.8 %collective-permute-start.12 = (bf16[128,2560]{1,0:T(8,128)(2,1)}, bf16[128,2560]{1,0:T(8,128)(2,1)}, u32[]{:S(2)}, u32[]{:S(2)}) collective-permute-start(bf16[128,2560]{1,0:T(8,128)(2,1)} %bitcast.4.refs_0_), channel_id=1, source_target_pairs={{0,1},{1,0},{2,3},{3,2},{4,5},{5,4},{6,7},{7,6},{8,9},{9,8},{10,11... | collective-permute-start | bytes 1966088 | tf_op jit(solution)/shard_map/ppermute | solution.py:22
  71.6 177.0 %all-gather.9.cloned.1.call-start = ((), (), s32[]{:S(2)}) async-start(), calls=%async_computation.10 | async-start | bytes 6553600 | tf_op jit(solution)/shard_map/all_gather | solution.py:1003
  74.3 16.3 %collective-permute-start.9 = (f32[4,2560]{1,0:T(4,128)S(1)}, f32[4,2560]{1,0:T(4,128)S(1)}, u32[]{:S(2)}, u32[]{:S(2)}) collective-permute-start(f32[4,2560]{1,0:T(4,128)S(1)} %pad_maximum_fusion.12), channel_id=1, source_target_pairs={{0,24},{1,25},{2,26},{3,27},{4,28},{5,29},{6,30},{7,31}} | collective-permute-start | bytes 122888 | tf_op jit(solution)/shard_map/ppermute | solution.py:28
  79.8 10.8 %collective-permute-start.8 = (f32[4,2560]{1,0:T(4,128)S(1)}, f32[4,2560]{1,0:T(4,128)S(1)}, u32[]{:S(2)}, u32[]{:S(2)}) collective-permute-start(f32[4,2560]{1,0:T(4,128)S(1)} %pad_maximum_fusion.12), channel_id=1, source_target_pairs={{0,16},{8,24},{1,17},{9,25},{2,18},{10,26},{3,19},{11,27},{4,20},{... | collective-permute-start | bytes 122888 | tf_op jit(solution)/shard_map/ppermute | solution.py:28
  89.6 12.5 %collective-permute-start.13 = (bf16[128,2560]{1,0:T(8,128)(2,1)S(1)}, bf16[128,2560]{1,0:T(8,128)(2,1)S(1)}, u32[]{:S(2)}, u32[]{:S(2)}) collective-permute-start(bf16[128,2560]{1,0:T(8,128)(2,1)S(1)} %get-tuple-element.324.refs_1_), channel_id=1, source_target_pairs={{0,1},{1,0},{2,3},{3,2},{4,5},{5,4},{6,7},{7,6},{8,9},{9,8},{10,11... | collective-permute-start | bytes 1966088 | tf_op jit(solution)/shard_map/ppermute | solution.py:22
  92.2 9.8 %collective-permute-start.11 = (bf16[128,1280]{1,0:T(8,128)(2,1)S(1)}, bf16[128,1280]{1,0:T(8,128)(2,1)S(1)}, u32[]{:S(2)}, u32[]{:S(2)}) collective-permute-start(bf16[128,1280]{1,0:T(8,128)(2,1)S(1)} %pad_maximum_fusion.10), channel_id=1, source_target_pairs={{0,2},{2,0},{1,3},{3,1},{4,6},{6,4},{5,7},{7,5},{8,10},{10,8},{9,1... | collective-permute-start | bytes 983048 | tf_op jit(solution)/shard_map/ppermute | solution.py:22
  107.2 16.1 %collective-permute-start.14 = (bf16[128,2560]{1,0:T(8,128)(2,1)S(1)}, bf16[128,2560]{1,0:T(8,128)(2,1)S(1)}, u32[]{:S(2)}, u32[]{:S(2)}) collective-permute-start(bf16[128,2560]{1,0:T(8,128)(2,1)S(1)} %slice.756), channel_id=1, source_target_pairs={{0,2},{2,0},{1,3},{3,1},{4,6},{6,4},{5,7},{7,5},{8,10},{10,8},{9,1... | collective-permute-start | bytes 1966088 | tf_op jit(solution)/shard_map/ppermute | solution.py:22
  124.7 15.5 %collective-permute-start.15 = (bf16[128,2560]{1,0:T(8,128)(2,1)}, bf16[128,2560]{1,0:T(8,128)(2,1)}, u32[]{:S(2)}, u32[]{:S(2)}) collective-permute-start(bf16[128,2560]{1,0:T(8,128)(2,1)} %multiply_convert_fusion.refs_0_), channel_id=1, source_target_pairs={{0,2},{2,0},{1,3},{3,1},{4,6},{6,4},{5,7},{7,5},{8,10},{10,8},{9,1... | collective-permute-start | bytes 1966088 | tf_op jit(solution)/shard_map/ppermute | solution.py:22
  126.1 72.1 %collective-permute-start.25 = (bf16[4,128,2560]{2,1,0:T(8,128)(2,1)}, bf16[4,128,2560]{2,1,0:T(8,128)(2,1)}, u32[]{:S(2)}, u32[]{:S(2)}) collective-permute-start(bf16[4,128,2560]{2,1,0:T(8,128)(2,1)} %all-gather.7.cloned.1.call-done.refs_0_), channel_id=1, source_target_pairs={{0,1},{1,0},{2,3},{3,2},{4,5},{5,4},{6,7},{7,6},{8,9},{9,8},{10,11... | collective-permute-start | bytes 7864328 | tf_op jit(solution)/shard_map/ppermute | solution.py:22
  127.7 19.3 %collective-permute-start.16 = (bf16[128,2560]{1,0:T(8,128)(2,1)}, bf16[128,2560]{1,0:T(8,128)(2,1)}, u32[]{:S(2)}, u32[]{:S(2)}) collective-permute-start(bf16[128,2560]{1,0:T(8,128)(2,1)} %multiply_convert_fusion.refs_0_), channel_id=1, source_target_pairs={{0,1},{1,0},{2,3},{3,2},{4,5},{5,4},{6,7},{7,6},{8,9},{9,8},{10,11... | collective-permute-start | bytes 1966088 | tf_op jit(solution)/shard_map/ppermute | solution.py:22
  144.2 264.1 %reduce-scatter.5.cloned.1.call-start = ((), (), s32[]{:S(2)}) async-start(), calls=%async_computation.6 | async-start | bytes 2048000 | tf_op jit(solution)/shard_map/reduce_scatter | solution.py:880
  144.7 22.0 %collective-permute-start.18 = (bf16[4,2,2,80,256]{4,3,2,1,0:T(8,128)(2,1)S(1)}, bf16[4,2,2,80,256]{4,3,2,1,0:T(8,128)(2,1)S(1)}, u32[]{:S(2)}, u32[]{:S(2)}) collective-permute-start(bf16[4,2,2,80,256]{4,3,2,1,0:T(8,128)(2,1)S(1)} %fusion.65), channel_id=1, source_target_pairs={{0,2},{2,0},{1,3},{3,1},{4,6},{6,4},{5,7},{7,5},{8,10},{10,8},{9,1... | collective-permute-start | bytes 1966088 | tf_op jit(solution)/shard_map/ppermute | solution.py:22
  145.6 58.6 %collective-permute-start.27 = (bf16[3,128,2560]{2,1,0:T(8,128)(2,1)}, bf16[3,128,2560]{2,1,0:T(8,128)(2,1)}, u32[]{:S(2)}, u32[]{:S(2)}) collective-permute-start(bf16[3,128,2560]{2,1,0:T(8,128)(2,1)} %fusion.21), channel_id=1, source_target_pairs={{0,2},{2,0},{1,3},{3,1},{4,6},{6,4},{5,7},{7,5},{8,10},{10,8},{9,1... | collective-permute-start | bytes 5898248 | tf_op jit(solution)/shard_map/ppermute | solution.py:22
  185.5 16.7 %collective-permute-start.24 = (bf16[2,4,2,80,256]{4,3,2,1,0:T(8,128)(2,1)S(1)}, bf16[2,4,2,80,256]{4,3,2,1,0:T(8,128)(2,1)S(1)}, u32[]{:S(2)}, u32[]{:S(2)}) collective-permute-start(bf16[2,4,2,80,256]{4,3,2,1,0:T(8,128)(2,1)S(1)} %fusion.64), channel_id=1, source_target_pairs={{0,4},{4,0},{1,5},{5,1},{2,6},{6,2},{3,7},{7,3},{8,12},{12,8},{9,1... | collective-permute-start | bytes 1966088 | tf_op jit(solution)/shard_map/ppermute | solution.py:22
  206.0 17.2 %collective-permute-start.28 = (bf16[4,128,2560]{2,1,0:T(8,128)(2,1)S(1)}, bf16[4,128,2560]{2,1,0:T(8,128)(2,1)}, u32[]{:S(2)}, u32[]{:S(2)}) collective-permute-start(bf16[4,128,2560]{2,1,0:T(8,128)(2,1)S(1)} %pad_maximum_fusion.refs_1_), channel_id=1, source_target_pairs={{0,1},{1,0},{2,3},{3,2},{4,5},{5,4},{6,7},{7,6},{8,9},{9,8},{10,11... | collective-permute-start | bytes 7864328 | tf_op jit(solution)/shard_map/ppermute | solution.py:22
  206.1 17.1 %collective-permute-start.23 = (bf16[128,2560]{1,0:T(8,128)(2,1)S(1)}, bf16[128,2560]{1,0:T(8,128)(2,1)S(1)}, u32[]{:S(2)}, u32[]{:S(2)}) collective-permute-start(bf16[128,2560]{1,0:T(8,128)(2,1)S(1)} %add_convert_fusion.8), channel_id=1, source_target_pairs={{0,2},{2,0},{1,3},{3,1},{4,6},{6,4},{5,7},{7,5},{8,10},{10,8},{9,1... | collective-permute-start | bytes 1966088 | tf_op jit(solution)/shard_map/ppermute | solution.py:22
  207.0 16.3 %collective-permute-start.26 = (bf16[4,320,256]{2,1,0:T(8,128)(2,1)S(1)}, bf16[4,320,256]{2,1,0:T(8,128)(2,1)S(1)}, u32[]{:S(2)}, u32[]{:S(2)}) collective-permute-start(bf16[4,320,256]{2,1,0:T(8,128)(2,1)S(1)} %bitcast.232), channel_id=1, source_target_pairs={{0,1},{1,0},{2,3},{3,2},{4,5},{5,4},{6,7},{7,6},{8,9},{9,8},{10,11... | collective-permute-start | bytes 1966088 | tf_op jit(solution)/shard_map/ppermute | solution.py:22
  226.9 21.4 %collective-permute-start.30 = (bf16[128,2560]{1,0:T(8,128)(2,1)S(1)}, bf16[128,2560]{1,0:T(8,128)(2,1)S(1)}, u32[]{:S(2)}, u32[]{:S(2)}) collective-permute-start(bf16[128,2560]{1,0:T(8,128)(2,1)S(1)} %get-tuple-element.371.refs_0_), channel_id=1, source_target_pairs={{0,4},{4,0},{1,5},{5,1},{2,6},{6,2},{3,7},{7,3},{8,12},{12,8},{9,1... | collective-permute-start | bytes 1966088 | tf_op jit(solution)/shard_map/ppermute | solution.py:22
  228.4 20.2 %collective-permute-start.31 = (bf16[128,2560]{1,0:T(8,128)(2,1)S(1)}, bf16[128,2560]{1,0:T(8,128)(2,1)}, u32[]{:S(2)}, u32[]{:S(2)}) collective-permute-start(bf16[128,2560]{1,0:T(8,128)(2,1)S(1)} %get-tuple-element.371.refs_0_), channel_id=1, source_target_pairs={{0,1},{1,0},{2,3},{3,2},{4,5},{5,4},{6,7},{7,6},{8,9},{9,8},{10,11... | collective-permute-start | bytes 1966088 | tf_op jit(solution)/shard_map/ppermute | solution.py:22
  228.4 20.2 %collective-permute-start.29 = (bf16[128,2560]{1,0:T(8,128)(2,1)S(1)}, bf16[128,2560]{1,0:T(8,128)(2,1)}, u32[]{:S(2)}, u32[]{:S(2)}) collective-permute-start(bf16[128,2560]{1,0:T(8,128)(2,1)S(1)} %get-tuple-element.371.refs_0_), channel_id=1, source_target_pairs={{0,2},{2,0},{1,3},{3,1},{4,6},{6,4},{5,7},{7,5},{8,10},{10,8},{9,1... | collective-permute-start | bytes 1966088 | tf_op jit(solution)/shard_map/ppermute | solution.py:22
  248.3 17.9 %collective-permute-start.35 = (bf16[128,2560]{1,0:T(8,128)(2,1)S(1)}, bf16[128,2560]{1,0:T(8,128)(2,1)}, u32[]{:S(2)}, u32[]{:S(2)}) collective-permute-start(bf16[128,2560]{1,0:T(8,128)(2,1)S(1)} %collective-permute-done.30.refs_2_), channel_id=1, source_target_pairs={{0,1},{1,0},{2,3},{3,2},{4,5},{5,4},{6,7},{7,6},{8,9},{9,8},{10,11... | collective-permute-start | bytes 1966088 | tf_op jit(solution)/shard_map/ppermute | solution.py:22
  248.6 17.6 %collective-permute-start.34 = (bf16[128,2560]{1,0:T(8,128)(2,1)}, bf16[128,2560]{1,0:T(8,128)(2,1)}, u32[]{:S(2)}, u32[]{:S(2)}) collective-permute-start(bf16[128,2560]{1,0:T(8,128)(2,1)} %collective-permute-done.29.refs_1_), channel_id=1, source_target_pairs={{0,1},{1,0},{2,3},{3,2},{4,5},{5,4},{6,7},{7,6},{8,9},{9,8},{10,11... | collective-permute-start | bytes 1966088 | tf_op jit(solution)/shard_map/ppermute | solution.py:22
  248.9 17.3 %collective-permute-start.33 = (bf16[128,2560]{1,0:T(8,128)(2,1)}, bf16[128,2560]{1,0:T(8,128)(2,1)}, u32[]{:S(2)}, u32[]{:S(2)}) collective-permute-start(bf16[128,2560]{1,0:T(8,128)(2,1)} %collective-permute-done.29.refs_1_), channel_id=1, source_target_pairs={{0,4},{4,0},{1,5},{5,1},{2,6},{6,2},{3,7},{7,3},{8,12},{12,8},{9,1... | collective-permute-start | bytes 1966088 | tf_op jit(solution)/shard_map/ppermute | solution.py:22
  254.6 11.6 %collective-permute-start.32 = (bf16[2,128,640]{2,1,0:T(8,128)(2,1)S(1)}, bf16[2,128,640]{2,1,0:T(8,128)(2,1)S(1)}, u32[]{:S(2)}, u32[]{:S(2)}) collective-permute-start(bf16[2,128,640]{2,1,0:T(8,128)(2,1)S(1)} %fusion.52), channel_id=1, source_target_pairs={{0,2},{2,0},{1,3},{3,1},{4,6},{6,4},{5,7},{7,5},{8,10},{10,8},{9,1... | collective-permute-start | bytes 983048 | tf_op jit(solution)/shard_map/ppermute | solution.py:22
  277.5 24.1 %collective-permute-start.43 = (bf16[128,2560]{1,0:T(8,128)(2,1)}, bf16[128,2560]{1,0:T(8,128)(2,1)S(1)}, u32[]{:S(2)}, u32[]{:S(2)}) collective-permute-start(bf16[128,2560]{1,0:T(8,128)(2,1)} %bitcast.234), channel_id=1, source_target_pairs={{0,4},{4,0},{1,5},{5,1},{2,6},{6,2},{3,7},{7,3},{8,12},{12,8},{9,1... | collective-permute-start | bytes 1966088 | tf_op jit(solution)/shard_map/ppermute | solution.py:22
  278.0 23.6 %collective-permute-start.42 = (bf16[128,2560]{1,0:T(8,128)(2,1)}, bf16[128,2560]{1,0:T(8,128)(2,1)}, u32[]{:S(2)}, u32[]{:S(2)}) collective-permute-start(bf16[128,2560]{1,0:T(8,128)(2,1)} %bitcast.235), channel_id=1, source_target_pairs={{0,2},{2,0},{1,3},{3,1},{4,6},{6,4},{5,7},{7,5},{8,10},{10,8},{9,1... | collective-permute-start | bytes 1966088 | tf_op jit(solution)/shard_map/ppermute | solution.py:22
  281.3 20.4 %collective-permute-start.41 = (f32[4,2560]{1,0:T(4,128)S(1)}, f32[4,2560]{1,0:T(4,128)S(1)}, u32[]{:S(2)}, u32[]{:S(2)}) collective-permute-start(f32[4,2560]{1,0:T(4,128)S(1)} %pad_maximum_fusion.13), channel_id=1, source_target_pairs={{24,0},{25,1},{26,2},{27,3},{28,4},{29,5},{30,6},{31,7}} | collective-permute-start | bytes 122888 | tf_op jit(solution)/shard_map/ppermute | solution.py:28
  282.6 19.1 %collective-permute-start.40 = (f32[4,2560]{1,0:T(4,128)S(1)}, f32[4,2560]{1,0:T(4,128)S(1)}, u32[]{:S(2)}, u32[]{:S(2)}) collective-permute-start(f32[4,2560]{1,0:T(4,128)S(1)} %pad_maximum_fusion.13), channel_id=1, source_target_pairs={{16,0},{24,8},{17,1},{25,9},{18,2},{26,10},{19,3},{27,11},{20,4},{... | collective-permute-start | bytes 122888 | tf_op jit(solution)/shard_map/ppermute | solution.py:28
  283.9 17.8 %collective-permute-start.39 = (f32[4,2560]{1,0:T(4,128)S(1)}, f32[4,2560]{1,0:T(4,128)S(1)}, u32[]{:S(2)}, u32[]{:S(2)}) collective-permute-start(f32[4,2560]{1,0:T(4,128)S(1)} %pad_maximum_fusion.13), channel_id=1, source_target_pairs={{8,0},{16,8},{24,16},{9,1},{17,9},{25,17},{10,2},{18,10},{26,18},{... | collective-permute-start | bytes 122888 | tf_op jit(solution)/shard_map/ppermute | solution.py:28
  301.8 33.8 %collective-permute-start.50 = (bf16[4,256,2560]{2,1,0:T(8,128)(2,1)}, bf16[4,256,2560]{2,1,0:T(8,128)(2,1)}, u32[]{:S(2)}, u32[]{:S(2)}) collective-permute-start(bf16[4,256,2560]{2,1,0:T(8,128)(2,1)} %bitcast.26.refs_0_), channel_id=1, source_target_pairs={{0,1},{1,0},{2,3},{3,2},{4,5},{5,4},{6,7},{7,6},{8,9},{9,8},{10,11... | collective-permute-start | bytes 15728648 | tf_op jit(solution)/shard_map/ppermute | solution.py:22
  301.8 21.3 %collective-permute-start.45 = (bf16[128,2560]{1,0:T(8,128)(2,1)}, bf16[128,2560]{1,0:T(8,128)(2,1)S(1)}, u32[]{:S(2)}, u32[]{:S(2)}) collective-permute-start(bf16[128,2560]{1,0:T(8,128)(2,1)} %collective-permute-done.42.refs_1_), channel_id=1, source_target_pairs={{0,1},{1,0},{2,3},{3,2},{4,5},{5,4},{6,7},{7,6},{8,9},{9,8},{10,11... | collective-permute-start | bytes 1966088 | tf_op jit(solution)/shard_map/ppermute | solution.py:22
  302.3 20.8 %collective-permute-start.47 = (bf16[128,2560]{1,0:T(8,128)(2,1)S(1)}, bf16[128,2560]{1,0:T(8,128)(2,1)}, u32[]{:S(2)}, u32[]{:S(2)}) collective-permute-start(bf16[128,2560]{1,0:T(8,128)(2,1)S(1)} %collective-permute-done.43.refs_2_), channel_id=1, source_target_pairs={{0,2},{2,0},{1,3},{3,1},{4,6},{6,4},{5,7},{7,5},{8,10},{10,8},{9,1... | collective-permute-start | bytes 1966088 | tf_op jit(solution)/shard_map/ppermute | solution.py:22
  303.6 19.5 %collective-permute-start.46 = (bf16[128,2560]{1,0:T(8,128)(2,1)S(1)}, bf16[128,2560]{1,0:T(8,128)(2,1)}, u32[]{:S(2)}, u32[]{:S(2)}) collective-permute-start(bf16[128,2560]{1,0:T(8,128)(2,1)S(1)} %collective-permute-done.43.refs_2_), channel_id=1, source_target_pairs={{0,1},{1,0},{2,3},{3,2},{4,5},{5,4},{6,7},{7,6},{8,9},{9,8},{10,11... | collective-permute-start | bytes 1966088 | tf_op jit(solution)/shard_map/ppermute | solution.py:22
  329.8 22.3 %collective-permute-start.49 = (bf16[128,2560]{1,0:T(8,128)(2,1)S(1)}, bf16[128,2560]{1,0:T(8,128)(2,1)}, u32[]{:S(2)}, u32[]{:S(2)}) collective-permute-start(bf16[128,2560]{1,0:T(8,128)(2,1)S(1)} %bitcast.220), channel_id=1, source_target_pairs={{0,4},{4,0},{1,5},{5,1},{2,6},{6,2},{3,7},{7,3},{8,12},{12,8},{9,1... | collective-permute-start | bytes 1966088 | tf_op jit(solution)/shard_map/ppermute | solution.py:22
  332.4 19.7 %collective-permute-start.48 = (bf16[128,2560]{1,0:T(8,128)(2,1)S(1)}, bf16[128,2560]{1,0:T(8,128)(2,1)}, u32[]{:S(2)}, u32[]{:S(2)}) collective-permute-start(bf16[128,2560]{1,0:T(8,128)(2,1)S(1)} %bitcast.221), channel_id=1, source_target_pairs={{0,2},{2,0},{1,3},{3,1},{4,6},{6,4},{5,7},{7,5},{8,10},{10,8},{9,1... | collective-permute-start | bytes 1966088 | tf_op jit(solution)/shard_map/ppermute | solution.py:22
  333.2 202.5 %reduce-scatter.11.cloned.1.call-start = ((), (), s32[]{:S(2)}) async-start(), calls=%async_computation.9 | async-start | bytes 2048000 | tf_op jit(solution)/shard_map/reduce_scatter | solution.py:880
  352.1 17.9 %collective-permute-start.58 = (bf16[128,2560]{1,0:T(8,128)(2,1)}, bf16[128,2560]{1,0:T(8,128)(2,1)S(1)}, u32[]{:S(2)}, u32[]{:S(2)}) collective-permute-start(bf16[128,2560]{1,0:T(8,128)(2,1)} %collective-permute-done.49.refs_2_), channel_id=1, source_target_pairs={{0,2},{2,0},{1,3},{3,1},{4,6},{6,4},{5,7},{7,5},{8,10},{10,8},{9,1... | collective-permute-start | bytes 1966088 | tf_op jit(solution)/shard_map/ppermute | solution.py:22
  353.5 16.6 %collective-permute-start.56 = (bf16[128,2560]{1,0:T(8,128)(2,1)}, bf16[128,2560]{1,0:T(8,128)(2,1)S(1)}, u32[]{:S(2)}, u32[]{:S(2)}) collective-permute-start(bf16[128,2560]{1,0:T(8,128)(2,1)} %collective-permute-done.49.refs_2_), channel_id=1, source_target_pairs={{0,1},{1,0},{2,3},{3,2},{4,5},{5,4},{6,7},{7,6},{8,9},{9,8},{10,11... | collective-permute-start | bytes 1966088 | tf_op jit(solution)/shard_map/ppermute | solution.py:22
  355.6 30.7 %collective-permute-start.54 = (bf16[4,2,80,640]{3,2,1,0:T(8,128)(2,1)S(1)}, bf16[4,2,80,640]{3,2,1,0:T(8,128)(2,1)S(1)}, u32[]{:S(2)}, u32[]{:S(2)}) collective-permute-start(bf16[4,2,80,640]{3,2,1,0:T(8,128)(2,1)S(1)} %fusion.46), channel_id=1, source_target_pairs={{0,2},{2,0},{1,3},{3,1},{4,6},{6,4},{5,7},{7,5},{8,10},{10,8},{9,1... | collective-permute-start | bytes 2457608 | tf_op jit(solution)/shard_map/ppermute | solution.py:22
  405.4 132.3 %reduce-scatter.9.cloned.1.call-start = ((), (), s32[]{:S(2)}) async-start(), calls=%async_computation.8 | async-start | bytes 512000 | tf_op jit(solution)/shard_map/reduce_scatter | solution.py:880
  405.4 12.8 %collective-permute-start.59 = (bf16[4,80,640]{2,1,0:T(8,128)(2,1)}, bf16[4,80,640]{2,1,0:T(8,128)(2,1)}, u32[]{:S(2)}, u32[]{:S(2)}) collective-permute-start(bf16[4,80,640]{2,1,0:T(8,128)(2,1)} %fusion.66), channel_id=1, source_target_pairs={{0,4},{4,0},{1,5},{5,1},{2,6},{6,2},{3,7},{7,3},{8,12},{12,8},{9,1... | collective-permute-start | bytes 1228808 | tf_op jit(solution)/shard_map/ppermute | solution.py:22
  406.8 13.5 %collective-permute-start.60 = (bf16[128,2560]{1,0:T(8,128)(2,1)}, bf16[128,2560]{1,0:T(8,128)(2,1)}, u32[]{:S(2)}, u32[]{:S(2)}) collective-permute-start(bf16[128,2560]{1,0:T(8,128)(2,1)} %copy-done.34), channel_id=1, source_target_pairs={{0,1},{1,0},{2,3},{3,2},{4,5},{5,4},{6,7},{7,6},{8,9},{9,8},{10,11... | collective-permute-start | bytes 1966088 | tf_op jit(solution)/shard_map/ppermute | solution.py:22
  406.8 39.5 %collective-permute-start.62 = (bf16[2,320,1024]{2,1,0:T(8,128)(2,1)}, bf16[2,320,1024]{2,1,0:T(8,128)(2,1)}, u32[]{:S(2)}, u32[]{:S(2)}) collective-permute-start(bf16[2,320,1024]{2,1,0:T(8,128)(2,1)} %get-tuple-element.435), channel_id=1, source_target_pairs={{0,4},{4,0},{1,5},{5,1},{2,6},{6,2},{3,7},{7,3},{8,12},{12,8},{9,1... | collective-permute-start | bytes 3932168 | tf_op jit(solution)/shard_map/ppermute | solution.py:22
  420.2 121.3 %reduce-scatter.7.cloned.1.call-start = ((), (), s32[]{:S(2)}) async-start(), calls=%async_computation.7 | async-start | bytes 2048000 | tf_op jit(solution)/shard_map/reduce_scatter | solution.py:880
  431.9 42.5 %collective-permute-start.61 = (bf16[2,320,1024]{2,1,0:T(8,128)(2,1)}, bf16[2,320,1024]{2,1,0:T(8,128)(2,1)}, u32[]{:S(2)}, u32[]{:S(2)}) collective-permute-start(bf16[2,320,1024]{2,1,0:T(8,128)(2,1)} %get-tuple-element.434), channel_id=1, source_target_pairs={{0,4},{4,0},{1,5},{5,1},{2,6},{6,2},{3,7},{7,3},{8,12},{12,8},{9,1... | collective-permute-start | bytes 3932168 | tf_op jit(solution)/shard_map/ppermute | solution.py:22
  433.9 46.0 %collective-permute-start.21 = (bf16[128,2560]{1,0:T(8,128)(2,1)}, bf16[128,2560]{1,0:T(8,128)(2,1)}, u32[]{:S(2)}, u32[]{:S(2)}) collective-permute-start(bf16[128,2560]{1,0:T(8,128)(2,1)} %get-tuple-element.318), channel_id=1, source_target_pairs={{0,1},{1,0},{2,3},{3,2},{4,5},{5,4},{6,7},{7,6},{8,9},{9,8},{10,11... | collective-permute-start | bytes 1966088 | tf_op jit(solution)/shard_map/ppermute | solution.py:22
  433.9 46.0 %collective-permute-start.22 = (bf16[128,2560]{1,0:T(8,128)(2,1)}, bf16[128,2560]{1,0:T(8,128)(2,1)}, u32[]{:S(2)}, u32[]{:S(2)}) collective-permute-start(bf16[128,2560]{1,0:T(8,128)(2,1)} %get-tuple-element.320), channel_id=1, source_target_pairs={{0,1},{1,0},{2,3},{3,2},{4,5},{5,4},{6,7},{7,6},{8,9},{9,8},{10,11... | collective-permute-start | bytes 1966088 | tf_op jit(solution)/shard_map/ppermute | solution.py:22
  449.8 54.5 %collective-permute-start.67 = (bf16[320,1024]{1,0:T(8,128)(2,1)}, bf16[320,1024]{1,0:T(8,128)(2,1)}, u32[]{:S(2)}, u32[]{:S(2)}) collective-permute-start(bf16[320,1024]{1,0:T(8,128)(2,1)} %get-tuple-element.558), channel_id=1, source_target_pairs={{0,8},{8,0},{16,24},{24,16},{1,9},{9,1},{17,25},{25,17},{2,10},{10... | collective-permute-start | bytes 1966088 | tf_op jit(solution)/shard_map/ppermute | solution.py:38
  463.9 36.5 %collective-permute-start.65 = (bf16[2,320,1024]{2,1,0:T(8,128)(2,1)}, bf16[2,320,1024]{2,1,0:T(8,128)(2,1)}, u32[]{:S(2)}, u32[]{:S(2)}) collective-permute-start(bf16[2,320,1024]{2,1,0:T(8,128)(2,1)} %get-tuple-element.463), channel_id=1, source_target_pairs={{0,4},{4,0},{1,5},{5,1},{2,6},{6,2},{3,7},{7,3},{8,12},{12,8},{9,1... | collective-permute-start | bytes 3932168 | tf_op jit(solution)/shard_map/ppermute | solution.py:22
  477.1 40.2 %collective-permute-start.73 = (bf16[320,1024]{1,0:T(8,128)(2,1)}, bf16[320,1024]{1,0:T(8,128)(2,1)}, u32[]{:S(2)}, u32[]{:S(2)}) collective-permute-start(bf16[320,1024]{1,0:T(8,128)(2,1)} %get-tuple-element.554), channel_id=1, source_target_pairs={{0,8},{8,0},{16,24},{24,16},{1,9},{9,1},{17,25},{25,17},{2,10},{10... | collective-permute-start | bytes 1966088 | tf_op jit(solution)/shard_map/ppermute | solution.py:38
  485.6 17.5 %collective-permute-start.64 = (f32[4,2,2,80]{3,2,1,0:T(2,128)S(1)}, f32[4,2,2,80]{3,2,1,0:T(2,128)S(1)}, u32[]{:S(2)}, u32[]{:S(2)}) collective-permute-start(f32[4,2,2,80]{3,2,1,0:T(2,128)S(1)} %select_bitcast_fusion.7), channel_id=1, source_target_pairs={{0,1},{1,0},{2,3},{3,2},{4,5},{5,4},{6,7},{7,6},{8,9},{9,8},{10,11... | collective-permute-start | bytes 15368 | tf_op jit(solution)/shard_map/ppermute | solution.py:22
  487.1 25.4 %collective-permute-start.63 = (bf16[128,2560]{1,0:T(8,128)(2,1)S(1)}, bf16[128,2560]{1,0:T(8,128)(2,1)S(1)}, u32[]{:S(2)}, u32[]{:S(2)}) collective-permute-start(bf16[128,2560]{1,0:T(8,128)(2,1)S(1)} %add_convert_fusion.6), channel_id=1, source_target_pairs={{0,2},{2,0},{1,3},{3,1},{4,6},{6,4},{5,7},{7,5},{8,10},{10,8},{9,1... | collective-permute-start | bytes 1966088 | tf_op jit(solution)/shard_map/ppermute | solution.py:22
  505.5 25.8 %collective-permute-start.72 = (bf16[320,1024]{1,0:T(8,128)(2,1)S(1)}, bf16[320,1024]{1,0:T(8,128)(2,1)S(1)}, u32[]{:S(2)}, u32[]{:S(2)}) collective-permute-start(bf16[320,1024]{1,0:T(8,128)(2,1)S(1)} %get-tuple-element.556), channel_id=1, source_target_pairs={{0,8},{8,0},{16,24},{24,16},{1,9},{9,1},{17,25},{25,17},{2,10},{10... | collective-permute-start | bytes 1966088 | tf_op jit(solution)/shard_map/ppermute | solution.py:38
  517.3 16.9 %collective-permute-start.71 = (f32[80]{0:T(128)S(1)}, f32[80]{0:T(128)S(1)}, u32[]{:S(2)}, u32[]{:S(2)}) collective-permute-start(f32[80]{0:T(128)S(1)} %get-tuple-element.599), channel_id=1, source_target_pairs={{24,0},{0,8},{8,16},{16,24},{25,1},{1,9},{9,17},{17,25},{26,2},{2,... | collective-permute-start | bytes 968 | tf_op jit(solution)/shard_map/ppermute | solution.py:33
  517.3 16.9 %collective-permute-start.70 = (f32[80]{0:T(128)S(1)}, f32[80]{0:T(128)S(1)}, u32[]{:S(2)}, u32[]{:S(2)}) collective-permute-start(f32[80]{0:T(128)S(1)} %get-tuple-element.600), channel_id=1, source_target_pairs={{16,0},{24,8},{0,16},{8,24},{17,1},{25,9},{1,17},{9,25},{18,2},{26... | collective-permute-start | bytes 968 | tf_op jit(solution)/shard_map/ppermute | solution.py:33
  522.1 12.1 %collective-permute-start.69 = (f32[80]{0:T(128)S(1)}, f32[80]{0:T(128)S(1)}, u32[]{:S(2)}, u32[]{:S(2)}) collective-permute-start(f32[80]{0:T(128)S(1)} %get-tuple-element.601), channel_id=1, source_target_pairs={{8,0},{16,8},{24,16},{0,24},{9,1},{17,9},{25,17},{1,25},{10,2},{18... | collective-permute-start | bytes 968 | tf_op jit(solution)/shard_map/ppermute | solution.py:33
  (70 other events, 561.9 us)
Sparse Core Ops, SparseCore 0:
  11.2 33.9 all-gather.4
Sparse Core Ops, SparseCore 1:
  71.7 54.3 all-gather.6
  144.3 97.5 all-gather.8
  333.3 38.5 reduce-scatter.4
  405.5 38.9 reduce-scatter.10
  446.8 22.6 reduce-scatter.8
  471.8 55.0 reduce-scatter.6

commit v4 on v3

--- a/solution.py
+++ b/solution.py
@@ -595,7 +595,7 @@
 
 def at_distance(places, gathered, steps):
     count = gathered[0].shape[0]
-    return [gathered[0][(places[0] + steps) % count], *[part[steps] for part in gathered[1:]]]
+    return [part[(places[0] + steps) % count] for part in gathered]
 
 
 def others(places, gathered):
@@ -746,8 +746,8 @@
 
 def others_plain(places, gathered):
     features = gathered[0].shape[2]
-    rolled = [jnp.roll(gathered[0], -places[0], axis=0), *gathered[1:]]
-    return jnp.concatenate([v[1:] for v in rolled], axis=1).reshape(-1, features)
+    rolled = [jnp.roll(v, -places[0], axis=0)[1:] for v in gathered]
+    return jnp.concatenate(rolled, axis=1).reshape(-1, features)
 
 
 def share_pull_plain(places, gathered, w_down):
@@ -767,7 +767,7 @@
     count, _, features = here[0].shape
     block = features // (2 * count)
     at = lambda v: lax.dynamic_index_in_dim(v, places[0], 0, keepdims=False)
-    own = [v for part in (here, there) for v in (at(part[0]), *[w[0] for w in part[1:]])]
+    own = [at(v) for v in (*here, *there)]
     tokens = jnp.concatenate(
         own + [others_plain(places, here), others_plain(places, there)], axis=0
     )
@@ -976,12 +976,14 @@
     own_y, received = line(own_y, received)
     recv_y, cot_x = cube(received[:rows]), received[rows:]
     branch_y = line.mark(gelu_pair(own_y + wide(recv_y))[0])
+    line.hold(cot_all)
     carry = carry_finish(*tied_carry(line, other_ends, arrived), sy, 1)
     mixed = flat(low((local_state + running * carry) * branch_y))
     keep, send = split_columns(mixed, wx, wc)
     line.mark(send)
     recv = swap(send, WX)
     cot_core, cot_both = core(cot), core(cot_x)
+    cot_x_all = lax.all_gather(cot_x, SZ)
     both_turned = line.mark(jnp.concatenate([normed_turned, line(mixed)[0].T], axis=1))
     line.hold(cot_core, cot_both)
     sent, own = project(*line(recv, keep, w_out))
@@ -995,9 +997,8 @@
 
     normed_x, normed_core = swap(normed_two, WX), core(normed_two)
     turned = both_turned.reshape(far, 2, 2, 2, features // (8 * far), half)
-    cot_others = line.mark(jnp.roll(*line(cot_all), -sz, axis=0)[1:])
-    normed_x, cot_others = line(normed_x, cot_others)
-    cot_x_far = swap(cot_others, WX)
+    line.hold(cot_x_all)
+    (normed_x,) = line(normed_x)
     normed_both = core(normed_x)
     pair = line.mark(joined_rows(*line(normed_two, normed_x)))
     normed_here = (lax.all_gather(pair, SZ),)
@@ -1016,19 +1017,15 @@
     pulled_there, pulled_both = line(pulled[1], pulled_both)
     for_x = line.mark(low(wide(pulled_there) + wide(pulled_both)))
     from_x = swap(for_x, WX)
-    cot_core_all = core(cot_all)
     made = units_made(*line(hidden), w_down)
     line.mark(made[0])
-    line.hold(cot_core_all)
     mine_y, got_y = line(mine_y, got_y)
     near, send = rows_for(WC, 2, jnp.concatenate([mine_y, got_y], axis=0))
     near, send = (v.reshape(4, features // 8, half) for v in (near, send))
     away = core(line.mark(send))
-    cot_x, cot_x_far = line(cot_x, cot_x_far)
-    cot_x_all = line.mark(jnp.concatenate([cot_x[None], cot_x_far], axis=0))
-    cot_here, cot_there = (cot_all, cot_x_all), (cot_core_all, core(cot_x_all))
-    line.hold(away, cot_there[1])
-    pulled_here, pulled_core, from_x = line(pulled[0], pulled_core, from_x)
+    line.hold(away)
+    pulled_here, pulled_core, from_x, cot_x_all = line(pulled[0], pulled_core, from_x, cot_x_all)
+    cot_here = (cot_all, cot_x_all)
     grad_normed_two = wide(pulled_here) + wide(pulled_core) + wide(from_x)
     weighted_two = grad_normed_two * gain2
     grad_stream = (
@@ -1040,7 +1037,9 @@
     grad_proj = line.mark(low(grad_stream))
     proj_x, proj_y = swap(grad_proj, WX), swap(grad_proj, SY)
     proj_core = core(grad_proj)
-    pull_here = line.mark(pull_of(spots, line(*cot_here), w_down))
+    cot_here = line(*cot_here)
+    cot_there = tuple(core(v) for v in cot_here)
+    pull_here = line.mark(pull_of(spots, cot_here, w_down))
 
     def shared(gathered, pulled):
         *gathered, pulled = line(*gathered, pulled)
@@ -1072,14 +1071,14 @@
         grad = token_grad(*line(near, away), second, line(*pieces))
         return scatter_far(line.mark(grad))
 
-    line.hold(proj_y, proj_core, *normed_here)
+    line.hold(proj_y, proj_core, *cot_there)
     proj_x, grad_proj = line(proj_x, grad_proj)
     sent, own = project_back([(proj_x, grad_proj, w_out)])
     line.mark(sent)
     sent, proj_xy = swap(sent, WX), swap(proj_x, SY)
     proj_x_core, proj_y_core = core(proj_x), core(proj_y)
     pull_there = line.mark(pull_of(spots, line(*cot_there), w_down))
-    line.hold(proj_xy, proj_x_core, proj_y_core)
+    line.hold(proj_xy, proj_x_core, proj_y_core, *normed_here)
     sent, own = line(sent, own)
     grad_mixed = cube(join_columns(own, wide(sent), wx, wc))
     line.mark(grad_mixed)
@@ -1158,8 +1157,8 @@
     line.mark(sent)
     line.hold(grad_x_core, grad_y_core, pre_xy_core, grad_xy)
     sent = swap(sent, WX)
+    (down,) = unit_sums(cot_here, cot_there, [0])
     rest = rest_step(SY, 1, rest_join(*rest))
-    (down,) = unit_sums(cot_here, cot_there, [0])
     y_sums = token_sums(
         0, grad_pre, pre_x, pre_y, pre_xy, pre_core, pre_x_core, pre_y_core, pre_xy_core
     )

time: 558 us -> 548 us (0.982)
  Pallas kernels: 200 us -> 192 us
  waiting for transfers between devices: 135 us -> 128 us
    ppermute x60 -> x59, waiting for transfers between devices: 125 us -> 104 us  [swap(): return lax.ppermute(value, axis, [(0, 1), (1, 0)])]
    all_gather x0 -> x1, waiting for transfers between devices: none -> 10.9 us  [local(): cot_x_all = lax.all_gather(cot_x, SZ)]
    pallas_call x4, Pallas kernels: 61.1 us -> 52.6 us  [share_call(): pl.pallas_call(partial(kernel, len(gathered)), grid_spec=pltpu.PrefetchSc...]
    ppermute x60 -> x59, starting transfers between devices: 44.4 us -> 41.2 us  [swap(): return lax.ppermute(value, axis, [(0, 1), (1, 0)])]
  transfers between devices with their start and end apart: 81 -> 81, of which waited for: 24 -> 27; matrix products, arithmetic and copies ran while one was open for 20% -> 22% of each run, Pallas kernels for 35% -> 36%
where the time goes in v4:
time: 548 us; the launch traced here: 538 us
  Pallas kernels  192 us (35%)
  waiting for transfers between devices  128 us (23%)
  starting transfers between devices  77.3 us (14%)
  other arithmetic  69.2 us (13%)
  local copies, waits for them, and re-layouts  31 us (6%)
  matrix products  25.7 us (5%)
  between operations  15.9 us (3%)
    ppermute x59, waiting for transfers between devices, swap(): return lax.ppermute(value, axis, [(0, 1), (1, 0)])  104 us
    pallas_call x4, Pallas kernels, share_call(): pl.pallas_call(partial(kernel, len(gathered)), grid_spec=pltpu.PrefetchSc...  52.6 us
    ppermute x59, starting transfers between devices, swap(): return lax.ppermute(value, axis, [(0, 1), (1, 0)])  41.2 us
    pallas_call x3, Pallas kernels, unit_grad(): pl.pallas_call(partial(unit_grad_kernel, len(here), kinds), grid_spec=plt...  34.3 us
    convert_element_type x15, other arithmetic, local(): low = lambda v: v.astype(BF16)  22.6 us
    pallas_call x3, Pallas kernels, token_grad(): pl.pallas_call(partial(token_grad_kernel, second * rows), grid=(width //...  19.9 us
    pallas_call x1, Pallas kernels, units(): pl.pallas_call(partial(units_kernel, count), grid=(held // tile,), in_spe...  19.5 us
    pallas_call x1, Pallas kernels, units_back(): pl.pallas_call(units_back_kernel, grid=(width // tile,), in_specs=[whole,...  18.1 us
  transfers between devices with their start and end apart: 81, of which 27 were waited for; matrix products, arithmetic and copies ran while one was open for 22% of the time, Pallas kernels for 36%

profile of v4, /device:TPU:0, one launch (start us, length us, event | category | flops | bytes accessed | tf_op | source)
XLA Modules:
  0.0 538.2 jit_solution(7638904472178062998)
XLA Ops:
  7.3 2.0 pad_maximum_fusion.6
  11.1 2.7 collective-permute-start
  13.8 8.4 %collective-permute-done = bf16[128,1280]{1,0:T(8,128)(2,1)S(1)} collective-permute-done((bf16[128,1280]{1,0:T(8,128)(2,1)S(1)}, bf16[128,1280]{1,0:T(8,128)(2,1)S(1)}, u32[]{:S(2)}, u32[]{:S(2)}) %collective-permute-start) | collective-permute-done | bytes 327712 | tf_op jit(solution)/shard_map/ppermute | solution.py:22
  22.2 2.8 collective-permute-done.2
  25.0 4.0 fusion
  29.3 2.9 collective-permute-start.4
  32.2 3.5 fusion.4
  37.5 2.5 constant_dynamic-update-slice_fusion
  39.9 2.0 constant_dynamic-update-slice_fusion.3
  42.0 4.0 constant_dynamic-update-slice_fusion.2
  46.0 5.0 collective-permute-done.4
  51.9 3.4 collective-permute-start.5
  60.1 9.2 %recur.1 = (bf16[2,64,2560]{2,1,0:T(8,128)(2,1)}, bf16[2,64,2560]{2,1,0:T(8,128)(2,1)}, f32[2,64,2560]{2,1,0:T(8,128)}, f32[2,64,2560]{2,1,0:T(8,128)}, f32[2,64...) custom-call(f32[2,64,2560]{2,1,0:T(8,128)} %bitcast.207, bf16[2,64,2560]{2,1,0:T(8,128)(2,1)} %bitcast.228, ...), custom_call_target="tpu_custom_call" | custom-call | flops 1310720 | bytes 262144 | tf_op jit(solution)/shard_map/recur/pallas_call | solution.py:263
  73.6 7.0 %collective-permute-start.9 = (f32[4,2560]{1,0:T(4,128)S(1)}, f32[4,2560]{1,0:T(4,128)S(1)}, u32[]{:S(2)}, u32[]{:S(2)}) collective-permute-start(f32[4,2560]{1,0:T(4,128)S(1)} %pad_maximum_fusion.11), channel_id=1, source_target_pairs={{0,24},{1,25},{2,26},{3,27},{4,28},{5,29},{6,30},{7,31}} | collective-permute-start | bytes 122888 | tf_op jit(solution)/shard_map/ppermute | solution.py:28
  81.9 2.5 collective-permute-start.7
  84.4 4.5 collective-permute-done.10
  90.1 2.7 multiply_multiply_fusion
  92.8 4.4 all-gather.9.cloned.1.call-done.refs_0_
  102.1 6.8 %collective-permute-done.11 = bf16[128,1280]{1,0:T(8,128)(2,1)S(1)} collective-permute-done((bf16[128,1280]{1,0:T(8,128)(2,1)S(1)}, bf16[128,1280]{1,0:T(8,128)(2,1)S(1)}, u32[]{:S(2)}, u32[]{:S(2)}) %collective-permute-start.11) | collective-permute-done | bytes 327712 | tf_op jit(solution)/shard_map/ppermute | solution.py:22
  108.9 5.1 fusion.59
  115.7 10.5 %pull_units.1.refs_6_ = bf16[512,1920]{1,0:T(8,128)(2,1)} custom-call(bf16[128,2560]{1,0:T(8,128)(2,1)} %bitcast.4.refs_0_, bf16[128,2560]{1,0:T(8,128)(2,1)} %get-tuple-element.286.refs_1_, bf16[128,2560]{1,0:T(8,128)(2,1)} %collective-permute-done.12.refs_2_, bf16[128,2560]{1,0:T(8,128)(2,1)} %collective-permute-done.13.refs_3_, bf16[1920,2560]{1,0:T(8,128)(2,1)} %refs_2_.5), custom_call_target="tpu_custom_call" | custom-call | flops 100663296 | bytes 196608 | tf_op jit(solution)/shard_map/pull_units/pallas_call | solution.py:527
  126.2 3.5 collective-permute-done.14
  134.2 12.0 %collective-permute-done.15.refs_1_ = bf16[128,2560]{1,0:T(8,128)(2,1)} collective-permute-done((bf16[128,2560]{1,0:T(8,128)(2,1)}, bf16[128,2560]{1,0:T(8,128)(2,1)}, u32[]{:S(2)}, u32[]{:S(2)}) %collective-permute-start.15) | collective-permute-done | bytes 655392 | tf_op jit(solution)/shard_map/ppermute | solution.py:22
  146.2 10.9 %all-gather.11.cloned.1.call-done = bf16[512,2560]{1,0:T(8,128)(2,1)} async-done(((bf16[128,2560]{1,0:T(8,128)(2,1)}), bf16[512,2560]{1,0:T(8,128)(2,1)}) %all-gather.11.cloned.1.call-update) | async-done | bytes 2621456 | tf_op jit(solution)/shard_map/all_gather | solution.py:986
  159.1 2.0 constant_dynamic-update-slice_fusion.4
  164.3 19.5 %units.1 = (bf16[512,1920]{1,0:T(8,128)(2,1)}, bf16[512,1920]{1,0:T(8,128)(2,1)}, bf16[512,1920]{1,0:T(8,128)(2,1)}) custom-call(bf16[128,2560]{1,0:T(8,128)(2,1)} %multiply_convert_fusion.refs_0_, bf16[128,2560]{1,0:T(8,128)(2,1)} %collective-permute-done.15.refs_1_, bf16[128,2560]{1,0:T(8,128)(2,1)} %collective-permute-done.16.refs_2_, ...), custom_call_target="tpu_custom_call" | custom-call | flops 201326592 | bytes 393216 | tf_op jit(solution)/shard_map/units/pallas_call | solution.py:498
  185.0 18.1 %units_back.1 = (bf16[128,2560]{1,0:T(8,128)(2,1)}, bf16[128,2560]{1,0:T(8,128)(2,1)}, bf16[128,2560]{1,0:T(8,128)(2,1)}, bf16[128,2560]{1,0:T(8,128)(2,1)}) custom-call(bf16[512,1920]{1,0:T(8,128)(2,1)} %get-tuple-element.424.gate.refs_2_, bf16[512,1920]{1,0:T(8,128)(2,1)} %get-tuple-element.446.up.refs_2_, bf16[2560,1920]{1,0:T(8,128)(2,1)} %refs_1_.3, ...), custom_call_target="tpu_custom_call" | custom-call | flops 201326592 | bytes 393216 | tf_op jit(solution)/shard_map/units_back/pallas_call | solution.py:556
  206.8 9.8 %units_made.1 = (bf16[128,2560]{1,0:T(8,128)(2,1)}, bf16[128,2560]{1,0:T(8,128)(2,1)}, bf16[128,2560]{1,0:T(8,128)(2,1)}, bf16[128,2560]{1,0:T(8,128)(2,1)}) custom-call(bf16[512,1920]{1,0:T(8,128)(2,1)} %get-tuple-element.401.hidden.refs_4_, bf16[1920,2560]{1,0:T(8,128)(2,1)} %refs_2_.5), custom_call_target="tpu_custom_call" | custom-call | flops 100663296 | bytes 196608 | tf_op jit(solution)/shard_map/units_made/pallas_call | solution.py:576
  216.6 3.9 collective-permute-done.24
  224.4 2.8 fusion.77
  230.1 9.8 %share_pull.2.refs_3_ = bf16[768,1024]{1,0:T(8,128)(2,1)} custom-call(s32[3]{0:T(128)} %pad_add_fusion.places, bf16[4,128,2560]{2,1,0:T(8,128)(2,1)} %all-gather.9.cloned.1.call-done.refs_0_, bf16[4,128,2560]{2,1,0:T(8,128)(2,1)} %bitcast.11.refs_1_, bf16[1920,2560]{1,0:T(8,128)(2,1)} %refs_2_.5), custom_call_target="tpu_custom_call" | custom-call | flops 80530640 | bytes 104857 | tf_op jit(solution)/shard_map/share_pull/pallas_call | solution.py:654
  239.9 4.7 collective-permute-done.27.refs_2_
  247.1 5.0 fusion.23
  253.2 9.7 %share_pull.3.refs_3_ = bf16[768,1024]{1,0:T(8,128)(2,1)} custom-call(s32[3]{0:T(128)} %pad_add_fusion.places, bf16[4,128,2560]{2,1,0:T(8,128)(2,1)} %collective-permute-done.29.refs_0_.refs_2_, bf16[4,128,2560]{2,1,0:T(8,128)(2,1)} %collective-permute-done.30.refs_1_.refs_3_, bf16[1920,2560]{1,0:T(8,128)(2,1)} %refs_2_.5), custom_call_target="tpu_custom_call" | custom-call | flops 80530640 | bytes 104857 | tf_op jit(solution)/shard_map/share_pull/pallas_call | solution.py:654
  266.3 7.8 %unroll.1 = (bf16[2,64,2560]{2,1,0:T(8,128)(2,1)}, f32[2,64,2560]{2,1,0:T(8,128)}, f32[2,64,2560]{2,1,0:T(8,128)}, f32[4,2560]{1,0:T(4,128)}) custom-call(f32[2,64,2560]{2,1,0:T(8,128)} %pad_maximum_fusion.1.mixed_grad, f32[2,64,2560]{2,1,0:T(8,128)} %bitcast.193, bf16[2,64,2560]{2,1,0:T(8,128)(2,1)} %bitcast.200, ...), custom_call_target="tpu_custom_call" | custom-call | flops 1310720 | bytes 262144 | tf_op jit(solution)/shard_map/unroll/pallas_call | solution.py:312
  284.2 16.4 %share.2 = (bf16[768,1024]{1,0:T(8,128)(2,1)}, bf16[768,1024]{1,0:T(8,128)(2,1)}, bf16[768,1024]{1,0:T(8,128)(2,1)}) custom-call(s32[3]{0:T(128)} %pad_add_fusion.places, bf16[4,256,2560]{2,1,0:T(8,128)(2,1)} %bitcast.31.refs_0_, bf16[2560,1920]{1,0:T(8,128)(2,1)} %refs_1_.3, bf16[2560,1920]{1,0:T(8,128)(2,1)} %refs_2_.7, bf16[768,1024]{1,0:T(8,128)(2,1)} %share_pull.2.refs_3_), custom_call_target="tpu_custom_call" | custom-call | flops 161061280 | bytes 209715 | tf_op jit(solution)/shard_map/share/pallas_call | solution.py:654
  302.6 9.9 %recur_back.1 = (f32[2,64,2560]{2,1,0:T(8,128)}, f32[2,8,2560]{2,1,0:T(8,128)}, bf16[2560,256]{1,0:T(8,128)(2,1)}, bf16[2560,256]{1,0:T(8,128)(2,1)}, f32[8,2560]{1,0:T(8,128)}) custom-call(f32[2,64,2560]{2,1,0:T(8,128)} %get-tuple-element.352.behind, f32[2,64,2560]{2,1,0:T(8,128)} %get-tuple-element.353.local_grad, f32[2,1,2560]{2,1,0:T(1,128)} %copy.106.carry_back, ...), custom_call_target="tpu_custom_call" | custom-call | flops 1966080 | bytes 327680 | tf_op jit(solution)/shard_map/recur_back/pallas_call | solution.py:422
  314.8 6.7 %token_grad.3 = bf16[320,2560]{1,0:T(8,128)(2,1)} custom-call(bf16[128,2560]{1,0:T(8,128)(2,1)} %copy-done.17, bf16[128,2560]{1,0:T(8,128)(2,1)} %collective-permute-done.26.refs_1_, bf16[128,2560]{1,0:T(8,128)(2,1)} %copy-done.28, bf16[128,2560]{1,0:T(8,128)(2,1)} %collective-permute-done.32.refs_3_, bf16[128,2560]{1,0:T(8,128)(2,1)} %collective-permute-done.28.refs_4_, ...), custom_call_target="tpu_custom_call" | custom-call | flops 33554432 | bytes 131072 | tf_op jit(solution)/shard_map/token_grad/pallas_call | solution.py:845
  328.2 2.6 collective-permute-start.48
  332.2 2.3 fusion.21
  334.6 16.7 %share.3 = (bf16[768,1024]{1,0:T(8,128)(2,1)}, bf16[768,1024]{1,0:T(8,128)(2,1)}, bf16[768,1024]{1,0:T(8,128)(2,1)}) custom-call(s32[3]{0:T(128)} %pad_add_fusion.places, bf16[4,256,2560]{2,1,0:T(8,128)(2,1)} %collective-permute-done.49.refs_0_.refs_1_, bf16[2560,1920]{1,0:T(8,128)(2,1)} %refs_1_.3, bf16[2560,1920]{1,0:T(8,128)(2,1)} %refs_2_.7, ...), custom_call_target="tpu_custom_call" | custom-call | flops 161061280 | bytes 209715 | tf_op jit(solution)/shard_map/share/pallas_call | solution.py:654
  356.0 4.0 fusion.12
  360.1 4.0 fusion.18
  366.1 3.2 collective-permute-done.57.refs_3_
  369.3 11.4 %unit_grad.3 = (f32[2,320,1024]{2,1,0:T(8,128)}, bf16[2,320,1024]{2,1,0:T(8,128)(2,1)}) custom-call(s32[3]{0:T(128)} %pad_add_fusion.places, bf16[4,128,2560]{2,1,0:T(8,128)(2,1)} %all-gather.9.cloned.1.call-done.refs_0_, bf16[4,128,2560]{2,1,0:T(8,128)(2,1)} %bitcast.11.refs_1_, bf16[4,128,2560]{2,1,0:T(8,128)(2,1)} %collective-permute-done.29.refs_0_.refs_2_, ...), custom_call_target="tpu_custom_call" | custom-call | flops 107374184 | bytes 83886 | tf_op jit(solution)/shard_map/unit_grad/pallas_call | solution.py:723
  380.7 4.5 collective-permute-done.53
  386.2 6.7 %token_grad.4 = bf16[320,2560]{1,0:T(8,128)(2,1)} custom-call(bf16[128,2560]{1,0:T(8,128)(2,1)} %bitcast.233, bf16[128,2560]{1,0:T(8,128)(2,1)} %collective-permute-done.41.refs_1_, bf16[128,2560]{1,0:T(8,128)(2,1)} %copy-done.27, bf16[128,2560]{1,0:T(8,128)(2,1)} %collective-permute-done.46.refs_3_, bf16[128,2560]{1,0:T(8,128)(2,1)} %copy-done.26, ...), custom_call_target="tpu_custom_call" | custom-call | flops 33554432 | bytes 131072 | tf_op jit(solution)/shard_map/token_grad/pallas_call | solution.py:845
  395.9 9.9 %collective-permute-done.58 = bf16[4,80,640]{2,1,0:T(8,128)(2,1)} collective-permute-done((bf16[4,80,640]{2,1,0:T(8,128)(2,1)}, bf16[4,80,640]{2,1,0:T(8,128)(2,1)}, u32[]{:S(2)}, u32[]{:S(2)}) %collective-permute-start.58) | collective-permute-done | bytes 409632 | tf_op jit(solution)/shard_map/ppermute | solution.py:22
  405.8 2.0 add_convert_fusion.9
  407.8 11.6 %unit_grad.4 = (f32[2,320,1024]{2,1,0:T(8,128)}, bf16[2,320,1024]{2,1,0:T(8,128)(2,1)}) custom-call(s32[3]{0:T(128)} %pad_add_fusion.places, bf16[4,256,2560]{2,1,0:T(8,128)(2,1)} %bitcast.31.refs_0_, bf16[4,256,2560]{2,1,0:T(8,128)(2,1)} %collective-permute-done.49.refs_0_.refs_1_, bf16[512,1920]{1,0:T(8,128)(2,1)} %get-tuple-element.424.gate.refs_2_, ...), custom_call_target="tpu_custom_call" | custom-call | flops 107374184 | bytes 83886 | tf_op jit(solution)/shard_map/unit_grad/pallas_call | solution.py:723
  422.9 6.6 %token_grad.5 = bf16[320,2560]{1,0:T(8,128)(2,1)} custom-call(bf16[128,2560]{1,0:T(8,128)(2,1)} %bitcast.220, bf16[128,2560]{1,0:T(8,128)(2,1)} %collective-permute-done.47.refs_1_, bf16[128,2560]{1,0:T(8,128)(2,1)} %collective-permute-done.48.refs_2_, bf16[128,2560]{1,0:T(8,128)(2,1)} %collective-permute-done.57.refs_3_, bf16[128,2560]{1,0:T(8,128)(2,1)} %copy-done.24, ...), custom_call_target="tpu_custom_call" | custom-call | flops 33554432 | bytes 131072 | tf_op jit(solution)/shard_map/token_grad/pallas_call | solution.py:845
  429.5 4.3 collective-permute-done.61
  433.8 2.6 add_convert_fusion.3
  437.3 3.0 collective-permute-start.66
  440.3 11.3 %unit_grad.5 = (f32[2,320,1024]{2,1,0:T(8,128)}, bf16[2,320,1024]{2,1,0:T(8,128)(2,1)}) custom-call(s32[3]{0:T(128)} %pad_add_fusion.places, bf16[4,256,2560]{2,1,0:T(8,128)(2,1)} %bitcast.31.refs_0_, bf16[4,256,2560]{2,1,0:T(8,128)(2,1)} %collective-permute-done.49.refs_0_.refs_1_, bf16[512,1920]{1,0:T(8,128)(2,1)} %get-tuple-element.446.up.refs_2_, ...), custom_call_target="tpu_custom_call" | custom-call | flops 107374184 | bytes 83886 | tf_op jit(solution)/shard_map/unit_grad/pallas_call | solution.py:723
  452.1 9.8 %collective-permute-done.60 = bf16[2,320,1024]{2,1,0:T(8,128)(2,1)} collective-permute-done((bf16[2,320,1024]{2,1,0:T(8,128)(2,1)}, bf16[2,320,1024]{2,1,0:T(8,128)(2,1)}, u32[]{:S(2)}, u32[]{:S(2)}) %collective-permute-start.60) | collective-permute-done | bytes 1310752 | tf_op jit(solution)/shard_map/ppermute | solution.py:22
  464.7 3.0 collective-permute-start.72
  470.0 3.1 fusion.35
  475.3 12.3 %collective-permute-done.64 = bf16[2,320,1024]{2,1,0:T(8,128)(2,1)} collective-permute-done((bf16[2,320,1024]{2,1,0:T(8,128)(2,1)}, bf16[2,320,1024]{2,1,0:T(8,128)(2,1)}, u32[]{:S(2)}, u32[]{:S(2)}) %collective-permute-start.64) | collective-permute-done | bytes 1310752 | tf_op jit(solution)/shard_map/ppermute | solution.py:22
  487.6 2.6 add_convert_fusion.1
  492.7 3.9 collective-permute-start.71
  500.1 2.2 add_convert_fusion.5
  504.0 5.6 %collective-permute-start.69 = (f32[80]{0:T(128)S(1)}, f32[80]{0:T(128)S(1)}, u32[]{:S(2)}, u32[]{:S(2)}) collective-permute-start(f32[80]{0:T(128)S(1)} %get-tuple-element.594), channel_id=1, source_target_pairs={{16,0},{24,8},{0,16},{8,24},{17,1},{25,9},{1,17},{9,25},{18,2},{26... | collective-permute-start | bytes 968 | tf_op jit(solution)/shard_map/ppermute | solution.py:33
  512.9 5.8 %collective-permute-done.71 = bf16[320,1024]{1,0:T(8,128)(2,1)S(1)} collective-permute-done((bf16[320,1024]{1,0:T(8,128)(2,1)S(1)}, bf16[320,1024]{1,0:T(8,128)(2,1)S(1)}, u32[]{:S(2)}, u32[]{:S(2)}) %collective-permute-start.71) | collective-permute-done | bytes 655392 | tf_op jit(solution)/shard_map/ppermute | solution.py:38
  (346 shorter events, 119.2 us)
Async XLA Ops:
  7.2 52.1 %all-gather.7.cloned.1.call-start = ((), (), s32[]{:S(2)}) async-start(), calls=%async_computation.4 | async-start | bytes 3276800 | tf_op jit(solution)/shard_map/all_gather | solution.py:932
  9.3 87.9 %all-gather.9.cloned.1.call-start = ((), (), s32[]{:S(2)}) async-start(), calls=%async_computation.5 | async-start | bytes 3276800 | tf_op jit(solution)/shard_map/all_gather | solution.py:934
  9.3 12.9 %collective-permute-start.3 = (bf16[640,2560]{1,0:T(8,128)(2,1)}, bf16[640,2560]{1,0:T(8,128)(2,1)}, u32[]{:S(2)}, u32[]{:S(2)}) collective-permute-start(bf16[640,2560]{1,0:T(8,128)(2,1)} %param.31), channel_id=1, source_target_pairs={{0,1},{1,0},{2,3},{3,2},{4,5},{5,4},{6,7},{7,6},{8,9},{9,8},{10,11... | collective-permute-start | bytes 9830408 | tf_op jit(solution)/shard_map/ppermute | solution.py:22
  9.9 12.3 %collective-permute-start.1 = (bf16[640,2560]{1,0:T(8,128)(2,1)}, bf16[640,2560]{1,0:T(8,128)(2,1)}, u32[]{:S(2)}, u32[]{:S(2)}) collective-permute-start(bf16[640,2560]{1,0:T(8,128)(2,1)} %param.22), channel_id=1, source_target_pairs={{0,1},{1,0},{2,3},{3,2},{4,5},{5,4},{6,7},{7,6},{8,9},{9,8},{10,11... | collective-permute-start | bytes 9830408 | tf_op jit(solution)/shard_map/ppermute | solution.py:22
  9.9 15.1 %collective-permute-start.2 = (bf16[640,2560]{1,0:T(8,128)(2,1)}, bf16[640,2560]{1,0:T(8,128)(2,1)}, u32[]{:S(2)}, u32[]{:S(2)}) collective-permute-start(bf16[640,2560]{1,0:T(8,128)(2,1)} %param.23), channel_id=1, source_target_pairs={{0,1},{1,0},{2,3},{3,2},{4,5},{5,4},{6,7},{7,6},{8,9},{9,8},{10,11... | collective-permute-start | bytes 9830408 | tf_op jit(solution)/shard_map/ppermute | solution.py:22
  11.1 11.1 %collective-permute-start = (bf16[128,1280]{1,0:T(8,128)(2,1)S(1)}, bf16[128,1280]{1,0:T(8,128)(2,1)S(1)}, u32[]{:S(2)}, u32[]{:S(2)}) collective-permute-start(bf16[128,1280]{1,0:T(8,128)(2,1)S(1)} %pad_maximum_fusion.7), channel_id=1, source_target_pairs={{0,2},{2,0},{1,3},{3,1},{4,6},{6,4},{5,7},{7,5},{8,10},{10,8},{9,1... | collective-permute-start | bytes 983048 | tf_op jit(solution)/shard_map/ppermute | solution.py:22
  13.8 143.3 %all-gather.11.cloned.1.call-start = ((), (), s32[]{:S(2)}) async-start(), calls=%async_computation.10 | async-start | bytes 3276800 | tf_op jit(solution)/shard_map/all_gather | solution.py:986
  29.3 21.7 %collective-permute-start.4 = (bf16[128,2560]{1,0:T(8,128)(2,1)S(1)}, bf16[128,2560]{1,0:T(8,128)(2,1)S(1)}, u32[]{:S(2)}, u32[]{:S(2)}) collective-permute-start(bf16[128,2560]{1,0:T(8,128)(2,1)S(1)} %slice.754), channel_id=1, source_target_pairs={{0,2},{2,0},{1,3},{3,1},{4,6},{6,4},{5,7},{7,5},{8,10},{10,8},{9,1... | collective-permute-start | bytes 1966088 | tf_op jit(solution)/shard_map/ppermute | solution.py:22
  58.4 30.5 %collective-permute-start.10 = (bf16[256,2560]{1,0:T(8,128)(2,1)}, bf16[256,2560]{1,0:T(8,128)(2,1)S(1)}, u32[]{:S(2)}, u32[]{:S(2)}) collective-permute-start(bf16[256,2560]{1,0:T(8,128)(2,1)} %constant_dynamic-update-slice_fusion), channel_id=1, source_target_pairs={{0,2},{2,0},{1,3},{3,1},{4,6},{6,4},{5,7},{7,5},{8,10},{10,8},{9,1... | collective-permute-start | bytes 3932168 | tf_op jit(solution)/shard_map/ppermute | solution.py:22
  70.8 31.3 %collective-permute-start.12 = (bf16[128,2560]{1,0:T(8,128)(2,1)}, bf16[128,2560]{1,0:T(8,128)(2,1)}, u32[]{:S(2)}, u32[]{:S(2)}) collective-permute-start(bf16[128,2560]{1,0:T(8,128)(2,1)} %bitcast.4.refs_0_), channel_id=1, source_target_pairs={{0,1},{1,0},{2,3},{3,2},{4,5},{5,4},{6,7},{7,6},{8,9},{9,8},{10,11... | collective-permute-start | bytes 1966088 | tf_op jit(solution)/shard_map/ppermute | solution.py:22
  73.6 23.7 %collective-permute-start.9 = (f32[4,2560]{1,0:T(4,128)S(1)}, f32[4,2560]{1,0:T(4,128)S(1)}, u32[]{:S(2)}, u32[]{:S(2)}) collective-permute-start(f32[4,2560]{1,0:T(4,128)S(1)} %pad_maximum_fusion.11), channel_id=1, source_target_pairs={{0,24},{1,25},{2,26},{3,27},{4,28},{5,29},{6,30},{7,31}} | collective-permute-start | bytes 122888 | tf_op jit(solution)/shard_map/ppermute | solution.py:28
  80.6 16.6 %collective-permute-start.8 = (f32[4,2560]{1,0:T(4,128)S(1)}, f32[4,2560]{1,0:T(4,128)S(1)}, u32[]{:S(2)}, u32[]{:S(2)}) collective-permute-start(f32[4,2560]{1,0:T(4,128)S(1)} %pad_maximum_fusion.11), channel_id=1, source_target_pairs={{0,16},{8,24},{1,17},{9,25},{2,18},{10,26},{3,19},{11,27},{4,20},{... | collective-permute-start | bytes 122888 | tf_op jit(solution)/shard_map/ppermute | solution.py:28
  81.9 15.3 %collective-permute-start.7 = (f32[4,2560]{1,0:T(4,128)S(1)}, f32[4,2560]{1,0:T(4,128)S(1)}, u32[]{:S(2)}, u32[]{:S(2)}) collective-permute-start(f32[4,2560]{1,0:T(4,128)S(1)} %pad_maximum_fusion.11), channel_id=1, source_target_pairs={{0,8},{8,16},{16,24},{1,9},{9,17},{17,25},{2,10},{10,18},{18,26},{... | collective-permute-start | bytes 122888 | tf_op jit(solution)/shard_map/ppermute | solution.py:28
  90.0 18.9 %collective-permute-start.13 = (bf16[128,2560]{1,0:T(8,128)(2,1)}, bf16[128,2560]{1,0:T(8,128)(2,1)}, u32[]{:S(2)}, u32[]{:S(2)}) collective-permute-start(bf16[128,2560]{1,0:T(8,128)(2,1)} %get-tuple-element.286.refs_1_), channel_id=1, source_target_pairs={{0,1},{1,0},{2,3},{3,2},{4,5},{5,4},{6,7},{7,6},{8,9},{9,8},{10,11... | collective-permute-start | bytes 1966088 | tf_op jit(solution)/shard_map/ppermute | solution.py:22
  90.1 173.9 %all-gather.13.cloned.1.call-start = ((), (), s32[]{:S(2)}) async-start(), calls=%async_computation.11 | async-start | bytes 6553600 | tf_op jit(solution)/shard_map/all_gather | solution.py:1004
  114.1 15.6 %collective-permute-start.14 = (bf16[128,2560]{1,0:T(8,128)(2,1)S(1)}, bf16[128,2560]{1,0:T(8,128)(2,1)S(1)}, u32[]{:S(2)}, u32[]{:S(2)}) collective-permute-start(bf16[128,2560]{1,0:T(8,128)(2,1)S(1)} %slice.752), channel_id=1, source_target_pairs={{0,2},{2,0},{1,3},{3,1},{4,6},{6,4},{5,7},{7,5},{8,10},{10,8},{9,1... | collective-permute-start | bytes 1966088 | tf_op jit(solution)/shard_map/ppermute | solution.py:22
  131.1 15.0 %collective-permute-start.15 = (bf16[128,2560]{1,0:T(8,128)(2,1)}, bf16[128,2560]{1,0:T(8,128)(2,1)}, u32[]{:S(2)}, u32[]{:S(2)}) collective-permute-start(bf16[128,2560]{1,0:T(8,128)(2,1)} %multiply_convert_fusion.refs_0_), channel_id=1, source_target_pairs={{0,2},{2,0},{1,3},{3,1},{4,6},{6,4},{5,7},{7,5},{8,10},{10,8},{9,1... | collective-permute-start | bytes 1966088 | tf_op jit(solution)/shard_map/ppermute | solution.py:22
  134.2 30.1 %collective-permute-start.16 = (bf16[128,2560]{1,0:T(8,128)(2,1)}, bf16[128,2560]{1,0:T(8,128)(2,1)}, u32[]{:S(2)}, u32[]{:S(2)}) collective-permute-start(bf16[128,2560]{1,0:T(8,128)(2,1)} %multiply_convert_fusion.refs_0_), channel_id=1, source_target_pairs={{0,1},{1,0},{2,3},{3,2},{4,5},{5,4},{6,7},{7,6},{8,9},{9,8},{10,11... | collective-permute-start | bytes 1966088 | tf_op jit(solution)/shard_map/ppermute | solution.py:22
  162.1 21.7 %collective-permute-start.18 = (bf16[4,2,2,80,256]{4,3,2,1,0:T(8,128)(2,1)}, bf16[4,2,2,80,256]{4,3,2,1,0:T(8,128)(2,1)}, u32[]{:S(2)}, u32[]{:S(2)}) collective-permute-start(bf16[4,2,2,80,256]{4,3,2,1,0:T(8,128)(2,1)} %fusion.64), channel_id=1, source_target_pairs={{0,2},{2,0},{1,3},{3,1},{4,6},{6,4},{5,7},{7,5},{8,10},{10,8},{9,1... | collective-permute-start | bytes 1966088 | tf_op jit(solution)/shard_map/ppermute | solution.py:22
  163.6 232.3 %reduce-scatter.5.cloned.1.call-start = ((), (), s32[]{:S(2)}) async-start(), calls=%async_computation.6 | async-start | bytes 2048000 | tf_op jit(solution)/shard_map/reduce_scatter | solution.py:880
  203.6 16.8 %collective-permute-start.24 = (bf16[2,4,2,80,256]{4,3,2,1,0:T(8,128)(2,1)S(1)}, bf16[2,4,2,80,256]{4,3,2,1,0:T(8,128)(2,1)S(1)}, u32[]{:S(2)}, u32[]{:S(2)}) collective-permute-start(bf16[2,4,2,80,256]{4,3,2,1,0:T(8,128)(2,1)S(1)} %fusion.63), channel_id=1, source_target_pairs={{0,4},{4,0},{1,5},{5,1},{2,6},{6,2},{3,7},{7,3},{8,12},{12,8},{9,1... | collective-permute-start | bytes 1966088 | tf_op jit(solution)/shard_map/ppermute | solution.py:22
  206.5 16.9 %collective-permute-start.23 = (bf16[128,2560]{1,0:T(8,128)(2,1)S(1)}, bf16[128,2560]{1,0:T(8,128)(2,1)S(1)}, u32[]{:S(2)}, u32[]{:S(2)}) collective-permute-start(bf16[128,2560]{1,0:T(8,128)(2,1)S(1)} %add_convert_fusion.8), channel_id=1, source_target_pairs={{0,2},{2,0},{1,3},{3,1},{4,6},{6,4},{5,7},{7,5},{8,10},{10,8},{9,1... | collective-permute-start | bytes 1966088 | tf_op jit(solution)/shard_map/ppermute | solution.py:22
  227.2 19.2 %collective-permute-start.29 = (bf16[4,128,2560]{2,1,0:T(8,128)(2,1)}, bf16[4,128,2560]{2,1,0:T(8,128)(2,1)}, u32[]{:S(2)}, u32[]{:S(2)}) collective-permute-start(bf16[4,128,2560]{2,1,0:T(8,128)(2,1)} %all-gather.9.cloned.1.call-done.refs_0_), channel_id=1, source_target_pairs={{0,1},{1,0},{2,3},{3,2},{4,5},{5,4},{6,7},{7,6},{8,9},{9,8},{10,11... | collective-permute-start | bytes 7864328 | tf_op jit(solution)/shard_map/ppermute | solution.py:22
  227.4 19.0 %collective-permute-start.30 = (bf16[4,128,2560]{2,1,0:T(8,128)(2,1)}, bf16[4,128,2560]{2,1,0:T(8,128)(2,1)}, u32[]{:S(2)}, u32[]{:S(2)}) collective-permute-start(bf16[4,128,2560]{2,1,0:T(8,128)(2,1)} %bitcast.11.refs_1_), channel_id=1, source_target_pairs={{0,1},{1,0},{2,3},{3,2},{4,5},{5,4},{6,7},{7,6},{8,9},{9,8},{10,11... | collective-permute-start | bytes 7864328 | tf_op jit(solution)/shard_map/ppermute | solution.py:22
  227.8 16.8 %collective-permute-start.27 = (bf16[128,2560]{1,0:T(8,128)(2,1)S(1)}, bf16[128,2560]{1,0:T(8,128)(2,1)S(1)}, u32[]{:S(2)}, u32[]{:S(2)}) collective-permute-start(bf16[128,2560]{1,0:T(8,128)(2,1)S(1)} %get-tuple-element.365.refs_0_), channel_id=1, source_target_pairs={{0,4},{4,0},{1,5},{5,1},{2,6},{6,2},{3,7},{7,3},{8,12},{12,8},{9,1... | collective-permute-start | bytes 1966088 | tf_op jit(solution)/shard_map/ppermute | solution.py:22
  229.1 15.4 %collective-permute-start.28 = (bf16[128,2560]{1,0:T(8,128)(2,1)S(1)}, bf16[128,2560]{1,0:T(8,128)(2,1)}, u32[]{:S(2)}, u32[]{:S(2)}) collective-permute-start(bf16[128,2560]{1,0:T(8,128)(2,1)S(1)} %get-tuple-element.365.refs_0_), channel_id=1, source_target_pairs={{0,1},{1,0},{2,3},{3,2},{4,5},{5,4},{6,7},{7,6},{8,9},{9,8},{10,11... | collective-permute-start | bytes 1966088 | tf_op jit(solution)/shard_map/ppermute | solution.py:22
  229.1 17.3 %collective-permute-start.26 = (bf16[128,2560]{1,0:T(8,128)(2,1)S(1)}, bf16[128,2560]{1,0:T(8,128)(2,1)}, u32[]{:S(2)}, u32[]{:S(2)}) collective-permute-start(bf16[128,2560]{1,0:T(8,128)(2,1)S(1)} %get-tuple-element.365.refs_0_), channel_id=1, source_target_pairs={{0,2},{2,0},{1,3},{3,1},{4,6},{6,4},{5,7},{7,5},{8,10},{10,8},{9,1... | collective-permute-start | bytes 1966088 | tf_op jit(solution)/shard_map/ppermute | solution.py:22
  244.5 19.3 %collective-permute-start.34 = (bf16[128,2560]{1,0:T(8,128)(2,1)S(1)}, bf16[128,2560]{1,0:T(8,128)(2,1)}, u32[]{:S(2)}, u32[]{:S(2)}) collective-permute-start(bf16[128,2560]{1,0:T(8,128)(2,1)S(1)} %collective-permute-done.27.refs_2_), channel_id=1, source_target_pairs={{0,1},{1,0},{2,3},{3,2},{4,5},{5,4},{6,7},{7,6},{8,9},{9,8},{10,11... | collective-permute-start | bytes 1966088 | tf_op jit(solution)/shard_map/ppermute | solution.py:22
  246.4 17.5 %collective-permute-start.33 = (bf16[128,2560]{1,0:T(8,128)(2,1)}, bf16[128,2560]{1,0:T(8,128)(2,1)}, u32[]{:S(2)}, u32[]{:S(2)}) collective-permute-start(bf16[128,2560]{1,0:T(8,128)(2,1)} %collective-permute-done.26.refs_1_), channel_id=1, source_target_pairs={{0,1},{1,0},{2,3},{3,2},{4,5},{5,4},{6,7},{7,6},{8,9},{9,8},{10,11... | collective-permute-start | bytes 1966088 | tf_op jit(solution)/shard_map/ppermute | solution.py:22
  246.4 17.5 %collective-permute-start.32 = (bf16[128,2560]{1,0:T(8,128)(2,1)}, bf16[128,2560]{1,0:T(8,128)(2,1)}, u32[]{:S(2)}, u32[]{:S(2)}) collective-permute-start(bf16[128,2560]{1,0:T(8,128)(2,1)} %collective-permute-done.26.refs_1_), channel_id=1, source_target_pairs={{0,4},{4,0},{1,5},{5,1},{2,6},{6,2},{3,7},{7,3},{8,12},{12,8},{9,1... | collective-permute-start | bytes 1966088 | tf_op jit(solution)/shard_map/ppermute | solution.py:22
  252.2 11.6 %collective-permute-start.31 = (bf16[2,128,640]{2,1,0:T(8,128)(2,1)S(1)}, bf16[2,128,640]{2,1,0:T(8,128)(2,1)}, u32[]{:S(2)}, u32[]{:S(2)}) collective-permute-start(bf16[2,128,640]{2,1,0:T(8,128)(2,1)S(1)} %fusion.51), channel_id=1, source_target_pairs={{0,2},{2,0},{1,3},{3,1},{4,6},{6,4},{5,7},{7,5},{8,10},{10,8},{9,1... | collective-permute-start | bytes 983048 | tf_op jit(solution)/shard_map/ppermute | solution.py:22
  263.9 13.8 %collective-permute-start.36 = (bf16[128,2560]{1,0:T(8,128)(2,1)}, bf16[128,2560]{1,0:T(8,128)(2,1)}, u32[]{:S(2)}, u32[]{:S(2)}) collective-permute-start(bf16[128,2560]{1,0:T(8,128)(2,1)} %collective-permute-done.32.refs_3_), channel_id=1, source_target_pairs={{0,1},{1,0},{2,3},{3,2},{4,5},{5,4},{6,7},{7,6},{8,9},{9,8},{10,11... | collective-permute-start | bytes 1966088 | tf_op jit(solution)/shard_map/ppermute | solution.py:22
  275.3 25.3 %collective-permute-start.42 = (bf16[128,2560]{1,0:T(8,128)(2,1)}, bf16[128,2560]{1,0:T(8,128)(2,1)S(1)}, u32[]{:S(2)}, u32[]{:S(2)}) collective-permute-start(bf16[128,2560]{1,0:T(8,128)(2,1)} %bitcast.231), channel_id=1, source_target_pairs={{0,4},{4,0},{1,5},{5,1},{2,6},{6,2},{3,7},{7,3},{8,12},{12,8},{9,1... | collective-permute-start | bytes 1966088 | tf_op jit(solution)/shard_map/ppermute | solution.py:22
  276.7 23.9 %collective-permute-start.41 = (bf16[128,2560]{1,0:T(8,128)(2,1)}, bf16[128,2560]{1,0:T(8,128)(2,1)}, u32[]{:S(2)}, u32[]{:S(2)}) collective-permute-start(bf16[128,2560]{1,0:T(8,128)(2,1)} %bitcast.232), channel_id=1, source_target_pairs={{0,2},{2,0},{1,3},{3,1},{4,6},{6,4},{5,7},{7,5},{8,10},{10,8},{9,1... | collective-permute-start | bytes 1966088 | tf_op jit(solution)/shard_map/ppermute | solution.py:22
  280.3 20.4 %collective-permute-start.40 = (f32[4,2560]{1,0:T(4,128)S(1)}, f32[4,2560]{1,0:T(4,128)S(1)}, u32[]{:S(2)}, u32[]{:S(2)}) collective-permute-start(f32[4,2560]{1,0:T(4,128)S(1)} %pad_maximum_fusion.12), channel_id=1, source_target_pairs={{24,0},{25,1},{26,2},{27,3},{28,4},{29,5},{30,6},{31,7}} | collective-permute-start | bytes 122888 | tf_op jit(solution)/shard_map/ppermute | solution.py:28
  281.6 19.1 %collective-permute-start.39 = (f32[4,2560]{1,0:T(4,128)S(1)}, f32[4,2560]{1,0:T(4,128)S(1)}, u32[]{:S(2)}, u32[]{:S(2)}) collective-permute-start(f32[4,2560]{1,0:T(4,128)S(1)} %pad_maximum_fusion.12), channel_id=1, source_target_pairs={{16,0},{24,8},{17,1},{25,9},{18,2},{26,10},{19,3},{27,11},{20,4},{... | collective-permute-start | bytes 122888 | tf_op jit(solution)/shard_map/ppermute | solution.py:28
  282.9 17.8 %collective-permute-start.38 = (f32[4,2560]{1,0:T(4,128)S(1)}, f32[4,2560]{1,0:T(4,128)S(1)}, u32[]{:S(2)}, u32[]{:S(2)}) collective-permute-start(f32[4,2560]{1,0:T(4,128)S(1)} %pad_maximum_fusion.12), channel_id=1, source_target_pairs={{8,0},{16,8},{24,16},{9,1},{17,9},{25,17},{10,2},{18,10},{26,18},{... | collective-permute-start | bytes 122888 | tf_op jit(solution)/shard_map/ppermute | solution.py:28
  300.7 33.8 %collective-permute-start.49 = (bf16[4,256,2560]{2,1,0:T(8,128)(2,1)}, bf16[4,256,2560]{2,1,0:T(8,128)(2,1)}, u32[]{:S(2)}, u32[]{:S(2)}) collective-permute-start(bf16[4,256,2560]{2,1,0:T(8,128)(2,1)} %bitcast.31.refs_0_), channel_id=1, source_target_pairs={{0,1},{1,0},{2,3},{3,2},{4,5},{5,4},{6,7},{7,6},{8,9},{9,8},{10,11... | collective-permute-start | bytes 15728648 | tf_op jit(solution)/shard_map/ppermute | solution.py:22
  300.8 20.6 %collective-permute-start.44 = (bf16[128,2560]{1,0:T(8,128)(2,1)}, bf16[128,2560]{1,0:T(8,128)(2,1)S(1)}, u32[]{:S(2)}, u32[]{:S(2)}) collective-permute-start(bf16[128,2560]{1,0:T(8,128)(2,1)} %collective-permute-done.41.refs_1_), channel_id=1, source_target_pairs={{0,1},{1,0},{2,3},{3,2},{4,5},{5,4},{6,7},{7,6},{8,9},{9,8},{10,11... | collective-permute-start | bytes 1966088 | tf_op jit(solution)/shard_map/ppermute | solution.py:22
  301.3 20.2 %collective-permute-start.46 = (bf16[128,2560]{1,0:T(8,128)(2,1)S(1)}, bf16[128,2560]{1,0:T(8,128)(2,1)}, u32[]{:S(2)}, u32[]{:S(2)}) collective-permute-start(bf16[128,2560]{1,0:T(8,128)(2,1)S(1)} %collective-permute-done.42.refs_2_), channel_id=1, source_target_pairs={{0,2},{2,0},{1,3},{3,1},{4,6},{6,4},{5,7},{7,5},{8,10},{10,8},{9,1... | collective-permute-start | bytes 1966088 | tf_op jit(solution)/shard_map/ppermute | solution.py:22
  302.0 19.5 %collective-permute-start.45 = (bf16[128,2560]{1,0:T(8,128)(2,1)S(1)}, bf16[128,2560]{1,0:T(8,128)(2,1)}, u32[]{:S(2)}, u32[]{:S(2)}) collective-permute-start(bf16[128,2560]{1,0:T(8,128)(2,1)S(1)} %collective-permute-done.42.refs_2_), channel_id=1, source_target_pairs={{0,1},{1,0},{2,3},{3,2},{4,5},{5,4},{6,7},{7,6},{8,9},{9,8},{10,11... | collective-permute-start | bytes 1966088 | tf_op jit(solution)/shard_map/ppermute | solution.py:22
  328.2 23.1 %collective-permute-start.48 = (bf16[128,2560]{1,0:T(8,128)(2,1)S(1)}, bf16[128,2560]{1,0:T(8,128)(2,1)}, u32[]{:S(2)}, u32[]{:S(2)}) collective-permute-start(bf16[128,2560]{1,0:T(8,128)(2,1)S(1)} %bitcast.217), channel_id=1, source_target_pairs={{0,4},{4,0},{1,5},{5,1},{2,6},{6,2},{3,7},{7,3},{8,12},{12,8},{9,1... | collective-permute-start | bytes 1966088 | tf_op jit(solution)/shard_map/ppermute | solution.py:22
  330.8 20.4 %collective-permute-start.47 = (bf16[128,2560]{1,0:T(8,128)(2,1)S(1)}, bf16[128,2560]{1,0:T(8,128)(2,1)}, u32[]{:S(2)}, u32[]{:S(2)}) collective-permute-start(bf16[128,2560]{1,0:T(8,128)(2,1)S(1)} %bitcast.218), channel_id=1, source_target_pairs={{0,2},{2,0},{1,3},{3,1},{4,6},{6,4},{5,7},{7,5},{8,10},{10,8},{9,1... | collective-permute-start | bytes 1966088 | tf_op jit(solution)/shard_map/ppermute | solution.py:22
  332.2 191.0 %reduce-scatter.11.cloned.1.call-start = ((), (), s32[]{:S(2)}) async-start(), calls=%async_computation.9 | async-start | bytes 2048000 | tf_op jit(solution)/shard_map/reduce_scatter | solution.py:880
  351.3 18.0 %collective-permute-start.57 = (bf16[128,2560]{1,0:T(8,128)(2,1)}, bf16[128,2560]{1,0:T(8,128)(2,1)}, u32[]{:S(2)}, u32[]{:S(2)}) collective-permute-start(bf16[128,2560]{1,0:T(8,128)(2,1)} %collective-permute-done.48.refs_2_), channel_id=1, source_target_pairs={{0,2},{2,0},{1,3},{3,1},{4,6},{6,4},{5,7},{7,5},{8,10},{10,8},{9,1... | collective-permute-start | bytes 1966088 | tf_op jit(solution)/shard_map/ppermute | solution.py:22
  351.9 17.4 %collective-permute-start.55 = (bf16[128,2560]{1,0:T(8,128)(2,1)}, bf16[128,2560]{1,0:T(8,128)(2,1)}, u32[]{:S(2)}, u32[]{:S(2)}) collective-permute-start(bf16[128,2560]{1,0:T(8,128)(2,1)} %collective-permute-done.48.refs_2_), channel_id=1, source_target_pairs={{0,1},{1,0},{2,3},{3,2},{4,5},{5,4},{6,7},{7,6},{8,9},{9,8},{10,11... | collective-permute-start | bytes 1966088 | tf_op jit(solution)/shard_map/ppermute | solution.py:22
  354.0 31.3 %collective-permute-start.53 = (bf16[4,2,80,640]{3,2,1,0:T(8,128)(2,1)S(1)}, bf16[4,2,80,640]{3,2,1,0:T(8,128)(2,1)S(1)}, u32[]{:S(2)}, u32[]{:S(2)}) collective-permute-start(bf16[4,2,80,640]{3,2,1,0:T(8,128)(2,1)S(1)} %fusion.45), channel_id=1, source_target_pairs={{0,2},{2,0},{1,3},{3,1},{4,6},{6,4},{5,7},{7,5},{8,10},{10,8},{9,1... | collective-permute-start | bytes 2457608 | tf_op jit(solution)/shard_map/ppermute | solution.py:22
  392.9 132.2 %reduce-scatter.9.cloned.1.call-start = ((), (), s32[]{:S(2)}) async-start(), calls=%async_computation.8 | async-start | bytes 512000 | tf_op jit(solution)/shard_map/reduce_scatter | solution.py:880
  393.0 12.8 %collective-permute-start.58 = (bf16[4,80,640]{2,1,0:T(8,128)(2,1)}, bf16[4,80,640]{2,1,0:T(8,128)(2,1)}, u32[]{:S(2)}, u32[]{:S(2)}) collective-permute-start(bf16[4,80,640]{2,1,0:T(8,128)(2,1)} %fusion.65), channel_id=1, source_target_pairs={{0,4},{4,0},{1,5},{5,1},{2,6},{6,2},{3,7},{7,3},{8,12},{12,8},{9,1... | collective-permute-start | bytes 1228808 | tf_op jit(solution)/shard_map/ppermute | solution.py:22
  393.8 14.1 %collective-permute-start.59 = (bf16[128,2560]{1,0:T(8,128)(2,1)}, bf16[128,2560]{1,0:T(8,128)(2,1)}, u32[]{:S(2)}, u32[]{:S(2)}) collective-permute-start(bf16[128,2560]{1,0:T(8,128)(2,1)} %collective-permute-done.57.refs_3_), channel_id=1, source_target_pairs={{0,1},{1,0},{2,3},{3,2},{4,5},{5,4},{6,7},{7,6},{8,9},{9,8},{10,11... | collective-permute-start | bytes 1966088 | tf_op jit(solution)/shard_map/ppermute | solution.py:22
  393.8 40.1 %collective-permute-start.61 = (bf16[2,320,1024]{2,1,0:T(8,128)(2,1)}, bf16[2,320,1024]{2,1,0:T(8,128)(2,1)}, u32[]{:S(2)}, u32[]{:S(2)}) collective-permute-start(bf16[2,320,1024]{2,1,0:T(8,128)(2,1)} %get-tuple-element.429), channel_id=1, source_target_pairs={{0,4},{4,0},{1,5},{5,1},{2,6},{6,2},{3,7},{7,3},{8,12},{12,8},{9,1... | collective-permute-start | bytes 3932168 | tf_op jit(solution)/shard_map/ppermute | solution.py:22
  407.8 121.2 %reduce-scatter.7.cloned.1.call-start = ((), (), s32[]{:S(2)}) async-start(), calls=%async_computation.7 | async-start | bytes 2048000 | tf_op jit(solution)/shard_map/reduce_scatter | solution.py:880
  419.4 42.5 %collective-permute-start.60 = (bf16[2,320,1024]{2,1,0:T(8,128)(2,1)}, bf16[2,320,1024]{2,1,0:T(8,128)(2,1)}, u32[]{:S(2)}, u32[]{:S(2)}) collective-permute-start(bf16[2,320,1024]{2,1,0:T(8,128)(2,1)} %get-tuple-element.428), channel_id=1, source_target_pairs={{0,4},{4,0},{1,5},{5,1},{2,6},{6,2},{3,7},{7,3},{8,12},{12,8},{9,1... | collective-permute-start | bytes 3932168 | tf_op jit(solution)/shard_map/ppermute | solution.py:22
  421.5 46.2 %collective-permute-start.21 = (bf16[128,2560]{1,0:T(8,128)(2,1)}, bf16[128,2560]{1,0:T(8,128)(2,1)}, u32[]{:S(2)}, u32[]{:S(2)}) collective-permute-start(bf16[128,2560]{1,0:T(8,128)(2,1)} %get-tuple-element.314), channel_id=1, source_target_pairs={{0,1},{1,0},{2,3},{3,2},{4,5},{5,4},{6,7},{7,6},{8,9},{9,8},{10,11... | collective-permute-start | bytes 1966088 | tf_op jit(solution)/shard_map/ppermute | solution.py:22
  421.5 46.2 %collective-permute-start.22 = (bf16[128,2560]{1,0:T(8,128)(2,1)}, bf16[128,2560]{1,0:T(8,128)(2,1)}, u32[]{:S(2)}, u32[]{:S(2)}) collective-permute-start(bf16[128,2560]{1,0:T(8,128)(2,1)} %get-tuple-element.316), channel_id=1, source_target_pairs={{0,1},{1,0},{2,3},{3,2},{4,5},{5,4},{6,7},{7,6},{8,9},{9,8},{10,11... | collective-permute-start | bytes 1966088 | tf_op jit(solution)/shard_map/ppermute | solution.py:22
  437.3 54.2 %collective-permute-start.66 = (bf16[320,1024]{1,0:T(8,128)(2,1)}, bf16[320,1024]{1,0:T(8,128)(2,1)}, u32[]{:S(2)}, u32[]{:S(2)}) collective-permute-start(bf16[320,1024]{1,0:T(8,128)(2,1)} %get-tuple-element.552), channel_id=1, source_target_pairs={{0,8},{8,0},{16,24},{24,16},{1,9},{9,1},{17,25},{25,17},{2,10},{10... | collective-permute-start | bytes 1966088 | tf_op jit(solution)/shard_map/ppermute | solution.py:38
  451.7 35.9 %collective-permute-start.64 = (bf16[2,320,1024]{2,1,0:T(8,128)(2,1)}, bf16[2,320,1024]{2,1,0:T(8,128)(2,1)}, u32[]{:S(2)}, u32[]{:S(2)}) collective-permute-start(bf16[2,320,1024]{2,1,0:T(8,128)(2,1)} %get-tuple-element.457), channel_id=1, source_target_pairs={{0,4},{4,0},{1,5},{5,1},{2,6},{6,2},{3,7},{7,3},{8,12},{12,8},{9,1... | collective-permute-start | bytes 3932168 | tf_op jit(solution)/shard_map/ppermute | solution.py:22
  464.7 39.3 %collective-permute-start.72 = (bf16[320,1024]{1,0:T(8,128)(2,1)}, bf16[320,1024]{1,0:T(8,128)(2,1)}, u32[]{:S(2)}, u32[]{:S(2)}) collective-permute-start(bf16[320,1024]{1,0:T(8,128)(2,1)} %get-tuple-element.548), channel_id=1, source_target_pairs={{0,8},{8,0},{16,24},{24,16},{1,9},{9,1},{17,25},{25,17},{2,10},{10... | collective-permute-start | bytes 1966088 | tf_op jit(solution)/shard_map/ppermute | solution.py:38
  473.3 17.0 %collective-permute-start.63 = (f32[4,2,2,80]{3,2,1,0:T(2,128)S(1)}, f32[4,2,2,80]{3,2,1,0:T(2,128)S(1)}, u32[]{:S(2)}, u32[]{:S(2)}) collective-permute-start(f32[4,2,2,80]{3,2,1,0:T(2,128)S(1)} %select_bitcast_fusion.7), channel_id=1, source_target_pairs={{0,1},{1,0},{2,3},{3,2},{4,5},{5,4},{6,7},{7,6},{8,9},{9,8},{10,11... | collective-permute-start | bytes 15368 | tf_op jit(solution)/shard_map/ppermute | solution.py:22
  474.8 25.3 %collective-permute-start.62 = (bf16[128,2560]{1,0:T(8,128)(2,1)S(1)}, bf16[128,2560]{1,0:T(8,128)(2,1)S(1)}, u32[]{:S(2)}, u32[]{:S(2)}) collective-permute-start(bf16[128,2560]{1,0:T(8,128)(2,1)S(1)} %add_convert_fusion.6), channel_id=1, source_target_pairs={{0,2},{2,0},{1,3},{3,1},{4,6},{6,4},{5,7},{7,5},{8,10},{10,8},{9,1... | collective-permute-start | bytes 1966088 | tf_op jit(solution)/shard_map/ppermute | solution.py:22
  492.7 25.9 %collective-permute-start.71 = (bf16[320,1024]{1,0:T(8,128)(2,1)S(1)}, bf16[320,1024]{1,0:T(8,128)(2,1)S(1)}, u32[]{:S(2)}, u32[]{:S(2)}) collective-permute-start(bf16[320,1024]{1,0:T(8,128)(2,1)S(1)} %get-tuple-element.550), channel_id=1, source_target_pairs={{0,8},{8,0},{16,24},{24,16},{1,9},{9,1},{17,25},{25,17},{2,10},{10... | collective-permute-start | bytes 1966088 | tf_op jit(solution)/shard_map/ppermute | solution.py:38
  504.0 17.7 %collective-permute-start.70 = (f32[80]{0:T(128)S(1)}, f32[80]{0:T(128)S(1)}, u32[]{:S(2)}, u32[]{:S(2)}) collective-permute-start(f32[80]{0:T(128)S(1)} %get-tuple-element.593), channel_id=1, source_target_pairs={{24,0},{0,8},{8,16},{16,24},{25,1},{1,9},{9,17},{17,25},{26,2},{2,... | collective-permute-start | bytes 968 | tf_op jit(solution)/shard_map/ppermute | solution.py:33
  504.0 17.7 %collective-permute-start.69 = (f32[80]{0:T(128)S(1)}, f32[80]{0:T(128)S(1)}, u32[]{:S(2)}, u32[]{:S(2)}) collective-permute-start(f32[80]{0:T(128)S(1)} %get-tuple-element.594), channel_id=1, source_target_pairs={{16,0},{24,8},{0,16},{8,24},{17,1},{25,9},{1,17},{9,25},{18,2},{26... | collective-permute-start | bytes 968 | tf_op jit(solution)/shard_map/ppermute | solution.py:33
  509.6 12.1 %collective-permute-start.68 = (f32[80]{0:T(128)S(1)}, f32[80]{0:T(128)S(1)}, u32[]{:S(2)}, u32[]{:S(2)}) collective-permute-start(f32[80]{0:T(128)S(1)} %get-tuple-element.595), channel_id=1, source_target_pairs={{8,0},{16,8},{24,16},{0,24},{9,1},{17,9},{25,17},{1,25},{10,2},{18... | collective-permute-start | bytes 968 | tf_op jit(solution)/shard_map/ppermute | solution.py:33
  (61 other events, 437.9 us)
Sparse Core Ops, SparseCore 0:
  10.2 32.0 all-gather.6
  43.9 53.3 all-gather.8
  99.4 57.7 all-gather.10
  163.7 95.9 all-gather.12
  332.3 38.2 reduce-scatter.4
  393.0 38.9 reduce-scatter.10
  434.3 22.7 reduce-scatter.8
  459.6 55.2 reduce-scatter.6
